TPU v7x, 32 devices: a whole 2x2x4 slice. The times are simulated.
32 devices in a mesh: row: 4 (over y, x), col: 8 (over z, core).
Axes of the slice: x: 2, y: 2, z: 4, core: 2. Of those that a mesh axis runs over, the one named last changes fastest.
Arguments:
- record: bfloat16 [45056, 4096], P(('row', 'col')), may hold values from -6 to 6
- fir_taps: float32 [101], replicated, may hold values from -0.625 to 0.625
- bins: int32 [16], replicated, may hold values from 1 to 639
- offsets: int32 [32], P(('row', 'col')), may hold values from 0 to 28, as said below
Outputs:
- cross: bfloat16 [16, 2, 4096, 4096], P(None, None, 'row', 'col')
Inputs may be any that keep to these rules, and one draw needn't show every extreme that they name: `offsets`: a window's start offset within its slot of 1408 samples.
All inputs are finite; a program needn't handle non-finite values.
Results may differ from a plain program's by a relative error of at most 0.0069.
Values may be sent and summed in bfloat16 or wider, within the bound.
No kernel may reach another device: no remote copies, remote signals or barrier semaphores. Data moves between devices by JAX's collectives and lax.ppermute only.
A program may use at most 192 MiB of HBM per device.

v0:
```python
import functools
import math

import jax
import jax.numpy as jnp
from jax import lax
from jax.experimental import pallas as pl
from jax.experimental.pallas import tpu as pltpu
from jax.sharding import PartitionSpec as P

F = 16
WL = 1280
TAPS = 101
SPAN = WL + TAPS - 1
LANES = 128
FLOOR = 0.5
CHUNK = 4
CHUNKS = F // CHUNK
GROUP = 2 * CHUNK
ROWS = 2 * F
CALLS = 2

AXES = ("row", "col")
BF16 = jnp.bfloat16
F32 = jnp.float32


def sine(x):
    square = x * x
    total = jnp.full_like(x, 1.0 / math.factorial(13))
    for order in (11, 9, 7, 5, 3, 1):
        sign = -1.0 if order % 4 == 3 else 1.0
        total = total * square + sign / math.factorial(order)
    return x * total


def analysis_rows(bins, pattern, stacked, taps, offset, kernel):
    depth = kernel.shape[1]
    blocks = depth // LANES
    times = lax.broadcasted_iota(jnp.int32, (1, WL), 1).astype(F32)
    row = lax.broadcasted_iota(jnp.int32, (ROWS, 1), 0)
    chosen = jnp.zeros((ROWS, 1), F32)
    for index in range(F):
        this = (row // GROUP == index // CHUNK) & (row % CHUNK == index % CHUNK)
        chosen = jnp.where(this, bins[index].astype(F32), chosen)
    quarter = jnp.where(row % GROUP < CHUNK, 0.0, WL / 4.0)
    phase = chosen * times + quarter
    phase = phase - WL * jnp.floor((phase + 0.5) * (1.0 / WL))
    half = sine((phase - WL / 2.0) * (math.pi / WL))
    edge = times + 0.5
    taper = sine(jnp.minimum(edge, WL - edge) * (math.pi / WL))
    taper = taper * taper * (1.0 / math.sqrt(WL))
    pattern[:, :LANES] = jnp.zeros((ROWS, LANES), F32)
    pattern[:, LANES + WL :] = jnp.zeros((ROWS, depth - WL), F32)
    pattern[:, LANES : LANES + WL] = (2.0 * half * half - 1.0) * taper

    slack = depth - SPAN
    lane = lax.broadcasted_iota(jnp.int32, (8, 2 * LANES), 1) - (slack - offset)
    filter_row = jnp.zeros((8, 2 * LANES), F32)
    for index in range(TAPS):
        filter_row = jnp.where(lane == index, taps[index], filter_row)
    filter_rows = jnp.concatenate([filter_row] * (LANES // 8), axis=0)
    band = pltpu.roll(filter_rows, 0, 1, stride=1, stride_axis=0)

    for block in range(blocks):
        stacked[block * ROWS : (block + 1) * ROWS, :] = pattern[
            :, block * LANES : (block + 2) * LANES
        ]
    filtered = lax.dot_general(
        stacked[...],
        band,
        (((1,), (1,)), ((), ())),
        precision=lax.Precision.HIGHEST,
        preferred_element_type=F32,
    )
    for block in range(blocks):
        kernel[:, block * LANES : (block + 1) * LANES] = filtered[
            block * ROWS : (block + 1) * ROWS
        ].astype(BF16)


def spectra_body(row_count, col_count, place, offsets, bins, taps, record, *refs):
    to_rows = refs[:row_count]
    to_cols = refs[row_count : row_count + col_count]
    samples, pattern, stacked, kernel, whitened, arrived = refs[row_count + col_count :]
    width = samples.shape[2]
    copies = []
    for block in range(col_count):
        copy = pltpu.make_async_copy(
            record.at[:, pl.ds(block * width, width)], samples.at[block], arrived.at[block]
        )
        copy.start()
        copies.append(copy)
    analysis_rows(bins, pattern, stacked, taps, offsets[0], kernel)
    for block in range(col_count):
        copies[block].wait()
        spectra = jnp.dot(kernel[...], samples[block], preferred_element_type=F32)
        shaped = spectra.reshape(CHUNKS, 2, CHUNK, width)
        real, imag = shaped[:, 0], shaped[:, 1]
        magnitude = jnp.sqrt(real * real + imag * imag)
        inverse = 1.0 / jnp.maximum(magnitude, FLOOR)
        scaled = (shaped * inverse[:, None]).reshape(ROWS, width)
        whitened[block] = scaled.astype(BF16)
    row, col = place[0], place[1]
    share = col_count // row_count
    for step in range(row_count):
        for part in range(share):
            to_rows[step][:, part * width : (part + 1) * width] = whitened[
                (row ^ step) * share + part
            ]
    lines = col_count // 2
    for step in range(lines):
        line = lax.rem(col // 2 + step, lines)
        for flip in range(2):
            to_cols[2 * step + flip][...] = whitened[2 * line + (lax.rem(col, 2) ^ flip)]


def make_spectra(record, fir_taps, bins, offsets, place, row_count, col_count):
    depth, channels = record.shape
    width = channels // col_count
    smem = pl.BlockSpec(memory_space=pltpu.SMEM)
    vmem = pl.BlockSpec(memory_space=pltpu.VMEM)
    outs = [jax.ShapeDtypeStruct((ROWS, channels // row_count), BF16)] * row_count
    outs += [jax.ShapeDtypeStruct((ROWS, width), BF16)] * col_count
    return pl.pallas_call(
        functools.partial(spectra_body, row_count, col_count),
        out_shape=outs,
        in_specs=[smem] * 4 + [pl.BlockSpec(memory_space=pl.ANY)],
        out_specs=[vmem] * len(outs),
        scratch_shapes=[
            pltpu.VMEM((col_count, depth, width), BF16),
            pltpu.VMEM((ROWS, depth + LANES), F32),
            pltpu.VMEM((depth // LANES * ROWS, 2 * LANES), F32),
            pltpu.VMEM((ROWS, depth), BF16),
            pltpu.VMEM((col_count, ROWS, width), BF16),
            pltpu.SemaphoreType.DMA((col_count,)),
        ],
        compiler_params=pltpu.CompilerParams(vmem_limit_bytes=48 * 2**20),
        name="spectra",
    )(place, offsets, bins, fir_taps, record)


def regroup_body(count, *refs):
    pieces = [ref[...].astype(F32) for ref in refs[:count]]
    for chunk in range(CHUNKS):
        rows = slice(chunk * GROUP, (chunk + 1) * GROUP)
        joined = jnp.concatenate([piece[rows] for piece in pieces], axis=0)
        per_call = CHUNKS // CALLS
        refs[count + chunk // per_call][chunk % per_call] = joined.astype(BF16)


def regroup(pieces):
    count, width = len(pieces), pieces[0].shape[1]
    out = jax.ShapeDtypeStruct((CHUNKS // CALLS, count * GROUP, width), BF16)
    vmem = pl.BlockSpec(memory_space=pltpu.VMEM)
    return pl.pallas_call(
        functools.partial(regroup_body, count),
        out_shape=[out] * CALLS,
        in_specs=[vmem] * count,
        out_specs=[vmem] * CALLS,
        name="regroup",
    )(*pieces)


def product_body(left_count, right_count, windows, *refs):
    lefts = refs[:left_count]
    rights = refs[left_count : left_count + right_count]
    out, turned, straight, crossed = refs[-4:]
    depth, width = straight.shape

    @pl.when(pl.program_id(1) == 0)
    def _():
        left = jnp.concatenate([ref[0] for ref in lefts], axis=0)
        turned[...] = left.T
        pieces = [ref[0].astype(F32) for ref in rights]
        right = jnp.concatenate(
            [
                piece[group * GROUP : (group + 1) * GROUP]
                for group in range(left_count)
                for piece in pieces
            ],
            axis=0,
        )
        straight[...] = right
        shaped = right.reshape(depth // GROUP, 2, CHUNK, width)
        swapped = jnp.stack([shaped[:, 1], -shaped[:, 0]], axis=1)
        crossed[...] = swapped.reshape(depth, width)

    row = lax.broadcasted_iota(jnp.int32, (depth, width), 0)
    wanted = row % CHUNK == pl.program_id(1)
    for part, held in enumerate((straight, crossed)):
        right = jnp.where(wanted, held[...], 0.0).astype(BF16)
        product = jnp.dot(turned[...], right, preferred_element_type=F32)
        out[0, part] = (product * (1.0 / windows)).astype(BF16)


def multiply(call, lefts, rights, windows, result):
    per_call, left_rows, height = lefts[0].shape
    right_rows, width = rights[0].shape[1:]
    depth = left_rows * len(lefts)
    in_specs = [pl.BlockSpec((1, left_rows, height), lambda q, f: (q, 0, 0))] * len(lefts)
    in_specs += [pl.BlockSpec((1, right_rows, width), lambda q, f: (q, 0, 0))] * len(rights)
    operands = [*lefts, *rights]
    aliases = {}
    if result is not None:
        aliases = {len(operands): 0}
        in_specs.append(pl.BlockSpec(memory_space=pl.ANY))
        operands.append(result)
    first = call * per_call * CHUNK
    return pl.pallas_call(
        functools.partial(product_body, len(lefts), len(rights), windows),
        out_shape=jax.ShapeDtypeStruct((F, 2, height, width), BF16),
        grid=(per_call, CHUNK),
        in_specs=in_specs,
        out_specs=pl.BlockSpec(
            (1, 2, height, width), lambda q, f: (first + q * CHUNK + f, 0, 0, 0)
        ),
        scratch_shapes=[
            pltpu.VMEM((height, depth), BF16),
            pltpu.VMEM((depth, width), F32),
            pltpu.VMEM((depth, width), F32),
        ],
        input_output_aliases=aliases,
        compiler_params=pltpu.CompilerParams(vmem_limit_bytes=48 * 2**20),
        cost_estimate=pl.CostEstimate(
            flops=2 * per_call * CHUNK * 2 * height * width * depth,
            bytes_accessed=per_call * CHUNK * 2 * height * width * 2,
            transcendentals=0,
        ),
        name="products",
    )(*operands)


def on_device(record, fir_taps, bins, offsets):
    row_count, col_count = lax.axis_size("row"), lax.axis_size("col")
    lines = col_count // 2
    windows = row_count * col_count * offsets.shape[0]
    place = jnp.stack([lax.axis_index("row"), lax.axis_index("col")]).astype(jnp.int32)

    def send(value, row_flip, line_step, core_flip):
        pairs = []
        for row in range(row_count):
            for col in range(col_count):
                line = (col // 2 + line_step) % lines
                target = (row ^ row_flip) * col_count + 2 * line + (col % 2 ^ core_flip)
                pairs.append((row * col_count + col, target))
        return lax.ppermute(value, AXES, pairs)

    spectra = make_spectra(record, fir_taps, bins, offsets, place, row_count, col_count)
    to_rows, to_cols = spectra[:row_count], spectra[row_count:]
    own_row = [to_rows[0]] + [send(to_rows[step], step, 0, 0) for step in range(1, row_count)]
    own_col = [to_cols[0]] + [
        send(to_cols[step], 0, step // 2, step % 2) for step in range(1, col_count)
    ]
    row_pieces = regroup(own_row)
    col_pieces = regroup(own_col)

    result = None
    for call in range(CALLS):
        held = row_pieces[call]
        lefts = []
        for step in range(lines):
            if step:
                held = send(held, 0, 1, 0)
            lefts += [held, send(held, 0, 0, 1)]
        rights = [col_pieces[call]] + [
            send(col_pieces[call], step, 0, 0) for step in range(1, row_count)
        ]
        result = multiply(call, lefts, rights, windows, result)
    return result


def solution(mesh):
    placed = (P(("row", "col"), None), P(), P(), P(("row", "col")))
    return jax.shard_map(
        on_device,
        mesh=mesh,
        in_specs=placed,
        out_specs=P(None, None, "row", "col"),
        check_vma=False,
    )
```

profile of v0, /device:TPU:0, one launch (start us, length us, event | category | flops | bytes accessed | tf_op | source)
XLA Modules:
  0.0 79.7 jit_solution(3365175386001088542)
XLA Ops:
  0.7 0.7 copy-done.6
  1.4 0.7 copy-done.7
  2.0 5.5 %spectra.1 = (bf16[32,1024]{1,0:T(8,128)(2,1)S(1)}, bf16[32,1024]{1,0:T(8,128)(2,1)S(1)}, bf16[32,1024]{1,0:T(8,128)(2,1)S(1)}, bf16[32,1024]{1,0:T(8,128)(2,1)S...) custom-call(s32[2]{0:T(128)S(1)} %pad_add_fusion.place, ...), custom_call_target="tpu_custom_call" | custom-call | tf_op jit(solution)/shard_map/spectra/pallas_call | solution.py:125
  8.8 2.9 %collective-permute-start = (bf16[32,1024]{1,0:T(8,128)(2,1)S(1)}, bf16[32,1024]{1,0:T(8,128)(2,1)S(1)}, u32[]{:S(2)}, u32[]{:S(2)}) collective-permute-start(bf16[32,1024]{1,0:T(8,128)(2,1)S(1)} %get-tuple-element.22), channel_id=1, source_target_pairs={{0,8},{1,9},{2,10},{3,11},{4,12},{5,13},{6,14},{7,15},{8,0},{9,1},... | collective-permute-start | bytes 196616 | tf_op jit(solution)/shard_map/ppermute | solution.py:247
  11.8 1.5 %collective-permute-start.1 = (bf16[32,1024]{1,0:T(8,128)(2,1)S(1)}, bf16[32,1024]{1,0:T(8,128)(2,1)S(1)}, u32[]{:S(2)}, u32[]{:S(2)}) collective-permute-start(bf16[32,1024]{1,0:T(8,128)(2,1)S(1)} %get-tuple-element.23), channel_id=1, source_target_pairs={{0,16},{1,17},{2,18},{3,19},{4,20},{5,21},{6,22},{7,23},{8,24},{9,... | collective-permute-start | bytes 196616 | tf_op jit(solution)/shard_map/ppermute | solution.py:247
  13.3 0.9 %collective-permute-done.refs_1_ = bf16[32,1024]{1,0:T(8,128)(2,1)S(1)} collective-permute-done((bf16[32,1024]{1,0:T(8,128)(2,1)S(1)}, bf16[32,1024]{1,0:T(8,128)(2,1)S(1)}, u32[]{:S(2)}, u32[]{:S(2)}) %collective-permute-start) | collective-permute-done | bytes 65568 | tf_op jit(solution)/shard_map/ppermute | solution.py:247
  14.2 1.9 %collective-permute-done.1.refs_2_ = bf16[32,1024]{1,0:T(8,128)(2,1)S(1)} collective-permute-done((bf16[32,1024]{1,0:T(8,128)(2,1)S(1)}, bf16[32,1024]{1,0:T(8,128)(2,1)S(1)}, u32[]{:S(2)}, u32[]{:S(2)}) %collective-permute-start.1) | collective-permute-done | bytes 65568 | tf_op jit(solution)/shard_map/ppermute | solution.py:247
  16.0 2.4 %collective-permute-done.2.refs_3_ = bf16[32,1024]{1,0:T(8,128)(2,1)S(1)} collective-permute-done((bf16[32,1024]{1,0:T(8,128)(2,1)S(1)}, bf16[32,1024]{1,0:T(8,128)(2,1)S(1)}, u32[]{:S(2)}, u32[]{:S(2)}) %collective-permute-start.2) | collective-permute-done | bytes 65568 | tf_op jit(solution)/shard_map/ppermute | solution.py:247
  19.1 1.6 %regroup.2 = (bf16[2,32,1024]{2,1,0:T(8,128)(2,1)}, bf16[2,32,1024]{2,1,0:T(8,128)(2,1)}) custom-call(bf16[32,1024]{1,0:T(8,128)(2,1)} %copy-done.4, bf16[32,1024]{1,0:T(8,128)(2,1)} %copy-done.8, bf16[32,1024]{1,0:T(8,128)(2,1)} %copy-done.9, bf16[32,1024]{1,0:T(8,128)(2,1)} %copy-done.10), custom_call_target="tpu_custom_call" | custom-call | tf_op jit(solution)/shard_map/regroup/pallas_call | solution.py:156
  20.7 1.6 %collective-permute-start.21 = (bf16[2,32,1024]{2,1,0:T(8,128)(2,1)}, bf16[2,32,1024]{2,1,0:T(8,128)(2,1)S(1)}, u32[]{:S(2)}, u32[]{:S(2)}) collective-permute-start(bf16[2,32,1024]{2,1,0:T(8,128)(2,1)} %get-tuple-element.35.refs_0_), channel_id=1, source_target_pairs={{0,2},{1,3},{2,4},{3,5},{4,6},{5,7},{6,0},{7,1},{8,10},{9,11},{10,... | collective-permute-start | bytes 393224 | tf_op jit(solution)/shard_map/ppermute | solution.py:247
  22.3 1.6 %collective-permute-start.11 = (bf16[32,512]{1,0:T(8,128)(2,1)S(1)}, bf16[32,512]{1,0:T(8,128)(2,1)S(1)}, u32[]{:S(2)}, u32[]{:S(2)}) collective-permute-start(bf16[32,512]{1,0:T(8,128)(2,1)S(1)} %get-tuple-element.28), channel_id=1, source_target_pairs={{0,2},{1,3},{2,4},{3,5},{4,6},{5,7},{6,0},{7,1},{8,10},{9,11},{10,... | collective-permute-start | bytes 98312 | tf_op jit(solution)/shard_map/ppermute | solution.py:247
  23.9 1.4 %collective-permute-start.12 = (bf16[32,512]{1,0:T(8,128)(2,1)S(1)}, bf16[32,512]{1,0:T(8,128)(2,1)S(1)}, u32[]{:S(2)}, u32[]{:S(2)}) collective-permute-start(bf16[32,512]{1,0:T(8,128)(2,1)S(1)} %get-tuple-element.29), channel_id=1, source_target_pairs={{0,3},{1,2},{2,5},{3,4},{4,7},{5,6},{6,1},{7,0},{8,11},{9,10},{10,... | collective-permute-start | bytes 98312 | tf_op jit(solution)/shard_map/ppermute | solution.py:247
  25.3 1.2 %collective-permute-start.13 = (bf16[32,512]{1,0:T(8,128)(2,1)S(1)}, bf16[32,512]{1,0:T(8,128)(2,1)S(1)}, u32[]{:S(2)}, u32[]{:S(2)}) collective-permute-start(bf16[32,512]{1,0:T(8,128)(2,1)S(1)} %get-tuple-element.30), channel_id=1, source_target_pairs={{0,4},{1,5},{2,6},{3,7},{4,0},{5,1},{6,2},{7,3},{8,12},{9,13},{10,... | collective-permute-start | bytes 98312 | tf_op jit(solution)/shard_map/ppermute | solution.py:247
  26.5 1.3 %collective-permute-start.14 = (bf16[32,512]{1,0:T(8,128)(2,1)S(1)}, bf16[32,512]{1,0:T(8,128)(2,1)S(1)}, u32[]{:S(2)}, u32[]{:S(2)}) collective-permute-start(bf16[32,512]{1,0:T(8,128)(2,1)S(1)} %get-tuple-element.31), channel_id=1, source_target_pairs={{0,5},{1,4},{2,7},{3,6},{4,1},{5,0},{6,3},{7,2},{8,13},{9,12},{10,... | collective-permute-start | bytes 98312 | tf_op jit(solution)/shard_map/ppermute | solution.py:247
  28.4 1.8 %collective-permute-start.15 = (bf16[32,512]{1,0:T(8,128)(2,1)S(1)}, bf16[32,512]{1,0:T(8,128)(2,1)S(1)}, u32[]{:S(2)}, u32[]{:S(2)}) collective-permute-start(bf16[32,512]{1,0:T(8,128)(2,1)S(1)} %get-tuple-element.32), channel_id=1, source_target_pairs={{0,6},{1,7},{2,0},{3,1},{4,2},{5,3},{6,4},{7,5},{8,14},{9,15},{10,... | collective-permute-start | bytes 98312 | tf_op jit(solution)/shard_map/ppermute | solution.py:247
  31.5 0.9 %collective-permute-done.15.refs_6_ = bf16[32,512]{1,0:T(8,128)(2,1)S(1)} collective-permute-done((bf16[32,512]{1,0:T(8,128)(2,1)S(1)}, bf16[32,512]{1,0:T(8,128)(2,1)S(1)}, u32[]{:S(2)}, u32[]{:S(2)}) %collective-permute-start.15) | collective-permute-done | bytes 32800 | tf_op jit(solution)/shard_map/ppermute | solution.py:247
  32.3 1.3 %collective-permute-done.16.refs_7_ = bf16[32,512]{1,0:T(8,128)(2,1)S(1)} collective-permute-done((bf16[32,512]{1,0:T(8,128)(2,1)S(1)}, bf16[32,512]{1,0:T(8,128)(2,1)S(1)}, u32[]{:S(2)}, u32[]{:S(2)}) %collective-permute-start.16) | collective-permute-done | bytes 32800 | tf_op jit(solution)/shard_map/ppermute | solution.py:247
  34.2 1.6 %regroup.3 = (bf16[2,64,512]{2,1,0:T(8,128)(2,1)}, bf16[2,64,512]{2,1,0:T(8,128)(2,1)}) custom-call(bf16[32,512]{1,0:T(8,128)(2,1)} %copy-done.5, bf16[32,512]{1,0:T(8,128)(2,1)} %copy-done.11, bf16[32,512]{1,0:T(8,128)(2,1)} %copy-done.12, bf16[32,512]{1,0:T(8,128)(2,1)} %copy-done.13, bf16[32,512]{1,0:T(8,128)(2,1)} %copy-done.14, ...), custom_call_target="tpu_custom_call" | custom-call | tf_op jit(solution)/shard_map/regroup/pallas_call | solution.py:156
  36.8 1.6 %collective-permute-start.18 = (bf16[2,64,512]{2,1,0:T(8,128)(2,1)}, bf16[2,64,512]{2,1,0:T(8,128)(2,1)S(1)}, u32[]{:S(2)}, u32[]{:S(2)}) collective-permute-start(bf16[2,64,512]{2,1,0:T(8,128)(2,1)} %get-tuple-element.34.refs_8_), channel_id=1, source_target_pairs={{0,16},{1,17},{2,18},{3,19},{4,20},{5,21},{6,22},{7,23},{8,24},{9,... | collective-permute-start | bytes 393224 | tf_op jit(solution)/shard_map/ppermute | solution.py:247
  38.5 1.4 %collective-permute-start.29 = (bf16[2,64,512]{2,1,0:T(8,128)(2,1)}, bf16[2,64,512]{2,1,0:T(8,128)(2,1)S(1)}, u32[]{:S(2)}, u32[]{:S(2)}) collective-permute-start(bf16[2,64,512]{2,1,0:T(8,128)(2,1)} %get-tuple-element.36.refs_8_), channel_id=1, source_target_pairs={{0,24},{1,25},{2,26},{3,27},{4,28},{5,29},{6,30},{7,31},{8,16},{9,... | collective-permute-start | bytes 393224 | tf_op jit(solution)/shard_map/ppermute | solution.py:247
  40.0 3.4 %collective-permute-done.19.refs_11_ = bf16[2,64,512]{2,1,0:T(8,128)(2,1)S(1)} collective-permute-done((bf16[2,64,512]{2,1,0:T(8,128)(2,1)}, bf16[2,64,512]{2,1,0:T(8,128)(2,1)S(1)}, u32[]{:S(2)}, u32[]{:S(2)}) %collective-permute-start.19) | collective-permute-done | bytes 131104 | tf_op jit(solution)/shard_map/ppermute | solution.py:247
  43.8 0.8 %collective-permute-done.4.refs_2_ = bf16[2,32,1024]{2,1,0:T(8,128)(2,1)S(1)} collective-permute-done((bf16[2,32,1024]{2,1,0:T(8,128)(2,1)}, bf16[2,32,1024]{2,1,0:T(8,128)(2,1)S(1)}, u32[]{:S(2)}, u32[]{:S(2)}) %collective-permute-start.4) | collective-permute-done | bytes 131104 | tf_op jit(solution)/shard_map/ppermute | solution.py:247
  44.8 3.4 %collective-permute-done.18.refs_10_ = bf16[2,64,512]{2,1,0:T(8,128)(2,1)S(1)} collective-permute-done((bf16[2,64,512]{2,1,0:T(8,128)(2,1)}, bf16[2,64,512]{2,1,0:T(8,128)(2,1)S(1)}, u32[]{:S(2)}, u32[]{:S(2)}) %collective-permute-start.18) | collective-permute-done | bytes 131104 | tf_op jit(solution)/shard_map/ppermute | solution.py:247
  48.8 1.6 %collective-permute-done.28.refs_10_ = bf16[2,64,512]{2,1,0:T(8,128)(2,1)S(1)} collective-permute-done((bf16[2,64,512]{2,1,0:T(8,128)(2,1)}, bf16[2,64,512]{2,1,0:T(8,128)(2,1)S(1)}, u32[]{:S(2)}, u32[]{:S(2)}) %collective-permute-start.28) | collective-permute-done | bytes 131104 | tf_op jit(solution)/shard_map/ppermute | solution.py:247
  50.4 1.1 %collective-permute-done.6.refs_4_ = bf16[2,32,1024]{2,1,0:T(8,128)(2,1)S(1)} collective-permute-done((bf16[2,32,1024]{2,1,0:T(8,128)(2,1)S(1)}, bf16[2,32,1024]{2,1,0:T(8,128)(2,1)S(1)}, u32[]{:S(2)}, u32[]{:S(2)}) %collective-permute-start.6) | collective-permute-done | bytes 131104 | tf_op jit(solution)/shard_map/ppermute | solution.py:247
  51.4 2.0 %collective-permute-done.27.refs_9_ = bf16[2,64,512]{2,1,0:T(8,128)(2,1)S(1)} collective-permute-done((bf16[2,64,512]{2,1,0:T(8,128)(2,1)}, bf16[2,64,512]{2,1,0:T(8,128)(2,1)S(1)}, u32[]{:S(2)}, u32[]{:S(2)}) %collective-permute-start.27) | collective-permute-done | bytes 131104 | tf_op jit(solution)/shard_map/ppermute | solution.py:247
  53.4 2.4 %collective-permute-done.25.refs_6_ = bf16[2,32,1024]{2,1,0:T(8,128)(2,1)S(1)} collective-permute-done((bf16[2,32,1024]{2,1,0:T(8,128)(2,1)S(1)}, bf16[2,32,1024]{2,1,0:T(8,128)(2,1)S(1)}, u32[]{:S(2)}, u32[]{:S(2)}) %collective-permute-start.25) | collective-permute-done | bytes 131104 | tf_op jit(solution)/shard_map/ppermute | solution.py:247
  55.8 2.0 %collective-permute-start.17 = (bf16[2,64,512]{2,1,0:T(8,128)(2,1)}, bf16[2,64,512]{2,1,0:T(8,128)(2,1)S(1)}, u32[]{:S(2)}, u32[]{:S(2)}) collective-permute-start(bf16[2,64,512]{2,1,0:T(8,128)(2,1)} %get-tuple-element.34.refs_8_), channel_id=1, source_target_pairs={{0,8},{1,9},{2,10},{3,11},{4,12},{5,13},{6,14},{7,15},{8,0},{9,1},... | collective-permute-start | bytes 393224 | tf_op jit(solution)/shard_map/ppermute | solution.py:247
  58.9 0.9 %copy-done.1 = bf16[2,32,1024]{2,1,0:T(8,128)(2,1)S(1)} copy-done((bf16[2,32,1024]{2,1,0:T(8,128)(2,1)S(1)}, bf16[2,32,1024]{2,1,0:T(8,128)(2,1)}, u32[]{:S(2)}) %copy-start.1) | copy-done | bytes 131096
  59.8 0.9 %copy-done.3 = bf16[2,64,512]{2,1,0:T(8,128)(2,1)S(1)} copy-done((bf16[2,64,512]{2,1,0:T(8,128)(2,1)S(1)}, bf16[2,64,512]{2,1,0:T(8,128)(2,1)}, u32[]{:S(2)}) %copy-start.3) | copy-done | bytes 131096
  60.7 9.4 %products.2.refs_12_ = bf16[16,2,1024,512]{3,2,1,0:T(8,128)(2,1)} custom-call(bf16[2,32,1024]{2,1,0:T(8,128)(2,1)S(1)} %copy-done.1, bf16[2,32,1024]{2,1,0:T(8,128)(2,1)S(1)} %collective-permute-done.20.refs_1_, bf16[2,32,1024]{2,1,0:T(8,128)(2,1)S(1)} %collective-permute-done.21.refs_2_, bf16[2,32,1024]{2,1,0:T(8,128)(2,1)S(1)} %collective-permute-done.22.refs_3_, ...), custom_call_target="tpu_custom_call" | custom-call | flops 4294967296 | bytes 16777216 | tf_op jit(solution)/shard_map/products/pallas_call | solution.py:210
  70.2 9.5 %products.3 = bf16[16,2,1024,512]{3,2,1,0:T(8,128)(2,1)} custom-call(bf16[2,32,1024]{2,1,0:T(8,128)(2,1)S(1)} %copy-done, bf16[2,32,1024]{2,1,0:T(8,128)(2,1)S(1)} %collective-permute-done.3.refs_1_, bf16[2,32,1024]{2,1,0:T(8,128)(2,1)S(1)} %collective-permute-done.4.refs_2_, ...), custom_call_target="tpu_custom_call", output_to_operand_aliasing={{}: (12, {})} | custom-call | flops 4294967296 | bytes 16777216 | tf_op jit(solution)/shard_map/products/pallas_call | solution.py:210
  (70 shorter events, 8.0 us)
Async XLA Ops:
  8.8 5.3 %collective-permute-start = (bf16[32,1024]{1,0:T(8,128)(2,1)S(1)}, bf16[32,1024]{1,0:T(8,128)(2,1)S(1)}, u32[]{:S(2)}, u32[]{:S(2)}) collective-permute-start(bf16[32,1024]{1,0:T(8,128)(2,1)S(1)} %get-tuple-element.22), channel_id=1, source_target_pairs={{0,8},{1,9},{2,10},{3,11},{4,12},{5,13},{6,14},{7,15},{8,0},{9,1},... | collective-permute-start | bytes 196616 | tf_op jit(solution)/shard_map/ppermute | solution.py:247
  11.8 4.3 %collective-permute-start.1 = (bf16[32,1024]{1,0:T(8,128)(2,1)S(1)}, bf16[32,1024]{1,0:T(8,128)(2,1)S(1)}, u32[]{:S(2)}, u32[]{:S(2)}) collective-permute-start(bf16[32,1024]{1,0:T(8,128)(2,1)S(1)} %get-tuple-element.23), channel_id=1, source_target_pairs={{0,16},{1,17},{2,18},{3,19},{4,20},{5,21},{6,22},{7,23},{8,24},{9,... | collective-permute-start | bytes 196616 | tf_op jit(solution)/shard_map/ppermute | solution.py:247
  13.3 5.2 %collective-permute-start.2 = (bf16[32,1024]{1,0:T(8,128)(2,1)S(1)}, bf16[32,1024]{1,0:T(8,128)(2,1)S(1)}, u32[]{:S(2)}, u32[]{:S(2)}) collective-permute-start(bf16[32,1024]{1,0:T(8,128)(2,1)S(1)} %get-tuple-element.24), channel_id=1, source_target_pairs={{0,24},{1,25},{2,26},{3,27},{4,28},{5,29},{6,30},{7,31},{8,16},{9,... | collective-permute-start | bytes 196616 | tf_op jit(solution)/shard_map/ppermute | solution.py:247
  20.7 49.5 %copy-start = (bf16[2,32,1024]{2,1,0:T(8,128)(2,1)S(1)}, bf16[2,32,1024]{2,1,0:T(8,128)(2,1)}, u32[]{:S(2)}) copy-start(bf16[2,32,1024]{2,1,0:T(8,128)(2,1)} %get-tuple-element.25.refs_0_) | copy-start | bytes 393220
  20.7 17.6 %collective-permute-start.21 = (bf16[2,32,1024]{2,1,0:T(8,128)(2,1)}, bf16[2,32,1024]{2,1,0:T(8,128)(2,1)S(1)}, u32[]{:S(2)}, u32[]{:S(2)}) collective-permute-start(bf16[2,32,1024]{2,1,0:T(8,128)(2,1)} %get-tuple-element.35.refs_0_), channel_id=1, source_target_pairs={{0,2},{1,3},{2,4},{3,5},{4,6},{5,7},{6,0},{7,1},{8,10},{9,11},{10,... | collective-permute-start | bytes 393224 | tf_op jit(solution)/shard_map/ppermute | solution.py:247
  22.3 4.2 %collective-permute-start.10 = (bf16[32,512]{1,0:T(8,128)(2,1)S(1)}, bf16[32,512]{1,0:T(8,128)(2,1)S(1)}, u32[]{:S(2)}, u32[]{:S(2)}) collective-permute-start(bf16[32,512]{1,0:T(8,128)(2,1)S(1)} %get-tuple-element.27), channel_id=1, source_target_pairs={{0,1},{1,0},{2,3},{3,2},{4,5},{5,4},{6,7},{7,6},{8,9},{9,8},{10,11... | collective-permute-start | bytes 98312 | tf_op jit(solution)/shard_map/ppermute | solution.py:247
  22.3 6.1 %collective-permute-start.11 = (bf16[32,512]{1,0:T(8,128)(2,1)S(1)}, bf16[32,512]{1,0:T(8,128)(2,1)S(1)}, u32[]{:S(2)}, u32[]{:S(2)}) collective-permute-start(bf16[32,512]{1,0:T(8,128)(2,1)S(1)} %get-tuple-element.28), channel_id=1, source_target_pairs={{0,2},{1,3},{2,4},{3,5},{4,6},{5,7},{6,0},{7,1},{8,10},{9,11},{10,... | collective-permute-start | bytes 98312 | tf_op jit(solution)/shard_map/ppermute | solution.py:247
  23.9 6.3 %collective-permute-start.12 = (bf16[32,512]{1,0:T(8,128)(2,1)S(1)}, bf16[32,512]{1,0:T(8,128)(2,1)S(1)}, u32[]{:S(2)}, u32[]{:S(2)}) collective-permute-start(bf16[32,512]{1,0:T(8,128)(2,1)S(1)} %get-tuple-element.29), channel_id=1, source_target_pairs={{0,3},{1,2},{2,5},{3,4},{4,7},{5,6},{6,1},{7,0},{8,11},{9,10},{10,... | collective-permute-start | bytes 98312 | tf_op jit(solution)/shard_map/ppermute | solution.py:247
  25.3 5.5 %collective-permute-start.13 = (bf16[32,512]{1,0:T(8,128)(2,1)S(1)}, bf16[32,512]{1,0:T(8,128)(2,1)S(1)}, u32[]{:S(2)}, u32[]{:S(2)}) collective-permute-start(bf16[32,512]{1,0:T(8,128)(2,1)S(1)} %get-tuple-element.30), channel_id=1, source_target_pairs={{0,4},{1,5},{2,6},{3,7},{4,0},{5,1},{6,2},{7,3},{8,12},{9,13},{10,... | collective-permute-start | bytes 98312 | tf_op jit(solution)/shard_map/ppermute | solution.py:247
  26.5 4.9 %collective-permute-start.14 = (bf16[32,512]{1,0:T(8,128)(2,1)S(1)}, bf16[32,512]{1,0:T(8,128)(2,1)S(1)}, u32[]{:S(2)}, u32[]{:S(2)}) collective-permute-start(bf16[32,512]{1,0:T(8,128)(2,1)S(1)} %get-tuple-element.31), channel_id=1, source_target_pairs={{0,5},{1,4},{2,7},{3,6},{4,1},{5,0},{6,3},{7,2},{8,13},{9,12},{10,... | collective-permute-start | bytes 98312 | tf_op jit(solution)/shard_map/ppermute | solution.py:247
  28.4 3.9 %collective-permute-start.15 = (bf16[32,512]{1,0:T(8,128)(2,1)S(1)}, bf16[32,512]{1,0:T(8,128)(2,1)S(1)}, u32[]{:S(2)}, u32[]{:S(2)}) collective-permute-start(bf16[32,512]{1,0:T(8,128)(2,1)S(1)} %get-tuple-element.32), channel_id=1, source_target_pairs={{0,6},{1,7},{2,0},{3,1},{4,2},{5,3},{6,4},{7,5},{8,14},{9,15},{10,... | collective-permute-start | bytes 98312 | tf_op jit(solution)/shard_map/ppermute | solution.py:247
  30.2 3.4 %collective-permute-start.16 = (bf16[32,512]{1,0:T(8,128)(2,1)S(1)}, bf16[32,512]{1,0:T(8,128)(2,1)S(1)}, u32[]{:S(2)}, u32[]{:S(2)}) collective-permute-start(bf16[32,512]{1,0:T(8,128)(2,1)S(1)} %get-tuple-element.33), channel_id=1, source_target_pairs={{0,7},{1,6},{2,1},{3,0},{4,3},{5,2},{6,5},{7,4},{8,15},{9,14},{10,... | collective-permute-start | bytes 98312 | tf_op jit(solution)/shard_map/ppermute | solution.py:247
  35.8 7.6 %collective-permute-start.19 = (bf16[2,64,512]{2,1,0:T(8,128)(2,1)}, bf16[2,64,512]{2,1,0:T(8,128)(2,1)S(1)}, u32[]{:S(2)}, u32[]{:S(2)}) collective-permute-start(bf16[2,64,512]{2,1,0:T(8,128)(2,1)} %get-tuple-element.34.refs_8_), channel_id=1, source_target_pairs={{0,24},{1,25},{2,26},{3,27},{4,28},{5,29},{6,30},{7,31},{8,16},{9,... | collective-permute-start | bytes 393224 | tf_op jit(solution)/shard_map/ppermute | solution.py:247
  36.2 8.4 %collective-permute-start.4 = (bf16[2,32,1024]{2,1,0:T(8,128)(2,1)}, bf16[2,32,1024]{2,1,0:T(8,128)(2,1)S(1)}, u32[]{:S(2)}, u32[]{:S(2)}) collective-permute-start(bf16[2,32,1024]{2,1,0:T(8,128)(2,1)} %get-tuple-element.25.refs_0_), channel_id=1, source_target_pairs={{0,2},{1,3},{2,4},{3,5},{4,6},{5,7},{6,0},{7,1},{8,10},{9,11},{10,... | collective-permute-start | bytes 393224 | tf_op jit(solution)/shard_map/ppermute | solution.py:247
  36.8 11.4 %collective-permute-start.18 = (bf16[2,64,512]{2,1,0:T(8,128)(2,1)}, bf16[2,64,512]{2,1,0:T(8,128)(2,1)S(1)}, u32[]{:S(2)}, u32[]{:S(2)}) collective-permute-start(bf16[2,64,512]{2,1,0:T(8,128)(2,1)} %get-tuple-element.34.refs_8_), channel_id=1, source_target_pairs={{0,16},{1,17},{2,18},{3,19},{4,20},{5,21},{6,22},{7,23},{8,24},{9,... | collective-permute-start | bytes 393224 | tf_op jit(solution)/shard_map/ppermute | solution.py:247
  38.3 10.3 %collective-permute-start.23 = (bf16[2,32,1024]{2,1,0:T(8,128)(2,1)S(1)}, bf16[2,32,1024]{2,1,0:T(8,128)(2,1)S(1)}, u32[]{:S(2)}, u32[]{:S(2)}) collective-permute-start(bf16[2,32,1024]{2,1,0:T(8,128)(2,1)S(1)} %collective-permute-done.21.refs_2_), channel_id=1, source_target_pairs={{0,2},{1,3},{2,4},{3,5},{4,6},{5,7},{6,0},{7,1},{8,10},{9,11},{10,... | collective-permute-start | bytes 393224 | tf_op jit(solution)/shard_map/ppermute | solution.py:247
  38.5 10.1 %collective-permute-start.29 = (bf16[2,64,512]{2,1,0:T(8,128)(2,1)}, bf16[2,64,512]{2,1,0:T(8,128)(2,1)S(1)}, u32[]{:S(2)}, u32[]{:S(2)}) collective-permute-start(bf16[2,64,512]{2,1,0:T(8,128)(2,1)} %get-tuple-element.36.refs_8_), channel_id=1, source_target_pairs={{0,24},{1,25},{2,26},{3,27},{4,28},{5,29},{6,30},{7,31},{8,16},{9,... | collective-permute-start | bytes 393224 | tf_op jit(solution)/shard_map/ppermute | solution.py:247
  43.3 7.0 %collective-permute-start.28 = (bf16[2,64,512]{2,1,0:T(8,128)(2,1)}, bf16[2,64,512]{2,1,0:T(8,128)(2,1)S(1)}, u32[]{:S(2)}, u32[]{:S(2)}) collective-permute-start(bf16[2,64,512]{2,1,0:T(8,128)(2,1)} %get-tuple-element.36.refs_8_), channel_id=1, source_target_pairs={{0,16},{1,17},{2,18},{3,19},{4,20},{5,21},{6,22},{7,23},{8,24},{9,... | collective-permute-start | bytes 393224 | tf_op jit(solution)/shard_map/ppermute | solution.py:247
  44.6 6.8 %collective-permute-start.6 = (bf16[2,32,1024]{2,1,0:T(8,128)(2,1)S(1)}, bf16[2,32,1024]{2,1,0:T(8,128)(2,1)S(1)}, u32[]{:S(2)}, u32[]{:S(2)}) collective-permute-start(bf16[2,32,1024]{2,1,0:T(8,128)(2,1)S(1)} %collective-permute-done.4.refs_2_), channel_id=1, source_target_pairs={{0,2},{1,3},{2,4},{3,5},{4,6},{5,7},{6,0},{7,1},{8,10},{9,11},{10,... | collective-permute-start | bytes 393224 | tf_op jit(solution)/shard_map/ppermute | solution.py:247
  48.2 5.2 %collective-permute-start.27 = (bf16[2,64,512]{2,1,0:T(8,128)(2,1)}, bf16[2,64,512]{2,1,0:T(8,128)(2,1)S(1)}, u32[]{:S(2)}, u32[]{:S(2)}) collective-permute-start(bf16[2,64,512]{2,1,0:T(8,128)(2,1)} %get-tuple-element.36.refs_8_), channel_id=1, source_target_pairs={{0,8},{1,9},{2,10},{3,11},{4,12},{5,13},{6,14},{7,15},{8,0},{9,1},... | collective-permute-start | bytes 393224 | tf_op jit(solution)/shard_map/ppermute | solution.py:247
  48.7 7.1 %collective-permute-start.25 = (bf16[2,32,1024]{2,1,0:T(8,128)(2,1)S(1)}, bf16[2,32,1024]{2,1,0:T(8,128)(2,1)S(1)}, u32[]{:S(2)}, u32[]{:S(2)}) collective-permute-start(bf16[2,32,1024]{2,1,0:T(8,128)(2,1)S(1)} %collective-permute-done.23.refs_4_), channel_id=1, source_target_pairs={{0,2},{1,3},{2,4},{3,5},{4,6},{5,7},{6,0},{7,1},{8,10},{9,11},{10,... | collective-permute-start | bytes 393224 | tf_op jit(solution)/shard_map/ppermute | solution.py:247
  48.7 7.1 %collective-permute-start.20 = (bf16[2,32,1024]{2,1,0:T(8,128)(2,1)}, bf16[2,32,1024]{2,1,0:T(8,128)(2,1)S(1)}, u32[]{:S(2)}, u32[]{:S(2)}) collective-permute-start(bf16[2,32,1024]{2,1,0:T(8,128)(2,1)} %get-tuple-element.35.refs_0_), channel_id=1, source_target_pairs={{0,1},{1,0},{2,3},{3,2},{4,5},{5,4},{6,7},{7,6},{8,9},{9,8},{10,11... | collective-permute-start | bytes 393224 | tf_op jit(solution)/shard_map/ppermute | solution.py:247
  50.3 7.4 %collective-permute-start.22 = (bf16[2,32,1024]{2,1,0:T(8,128)(2,1)S(1)}, bf16[2,32,1024]{2,1,0:T(8,128)(2,1)S(1)}, u32[]{:S(2)}, u32[]{:S(2)}) collective-permute-start(bf16[2,32,1024]{2,1,0:T(8,128)(2,1)S(1)} %collective-permute-done.21.refs_2_), channel_id=1, source_target_pairs={{0,1},{1,0},{2,3},{3,2},{4,5},{5,4},{6,7},{7,6},{8,9},{9,8},{10,11... | collective-permute-start | bytes 393224 | tf_op jit(solution)/shard_map/ppermute | solution.py:247
  51.4 6.9 %collective-permute-start.8 = (bf16[2,32,1024]{2,1,0:T(8,128)(2,1)S(1)}, bf16[2,32,1024]{2,1,0:T(8,128)(2,1)S(1)}, u32[]{:S(2)}, u32[]{:S(2)}) collective-permute-start(bf16[2,32,1024]{2,1,0:T(8,128)(2,1)S(1)} %collective-permute-done.6.refs_4_), channel_id=1, source_target_pairs={{0,2},{1,3},{2,4},{3,5},{4,6},{5,7},{6,0},{7,1},{8,10},{9,11},{10,... | collective-permute-start | bytes 393224 | tf_op jit(solution)/shard_map/ppermute | solution.py:247
  53.4 5.0 %collective-permute-start.24 = (bf16[2,32,1024]{2,1,0:T(8,128)(2,1)S(1)}, bf16[2,32,1024]{2,1,0:T(8,128)(2,1)S(1)}, u32[]{:S(2)}, u32[]{:S(2)}) collective-permute-start(bf16[2,32,1024]{2,1,0:T(8,128)(2,1)S(1)} %collective-permute-done.23.refs_4_), channel_id=1, source_target_pairs={{0,1},{1,0},{2,3},{3,2},{4,5},{5,4},{6,7},{7,6},{8,9},{9,8},{10,11... | collective-permute-start | bytes 393224 | tf_op jit(solution)/shard_map/ppermute | solution.py:247
  55.8 3.1 %collective-permute-start.26 = (bf16[2,32,1024]{2,1,0:T(8,128)(2,1)S(1)}, bf16[2,32,1024]{2,1,0:T(8,128)(2,1)S(1)}, u32[]{:S(2)}, u32[]{:S(2)}) collective-permute-start(bf16[2,32,1024]{2,1,0:T(8,128)(2,1)S(1)} %collective-permute-done.25.refs_6_), channel_id=1, source_target_pairs={{0,1},{1,0},{2,3},{3,2},{4,5},{5,4},{6,7},{7,6},{8,9},{9,8},{10,11... | collective-permute-start | bytes 393224 | tf_op jit(solution)/shard_map/ppermute | solution.py:247
  55.8 14.4 %collective-permute-start.17 = (bf16[2,64,512]{2,1,0:T(8,128)(2,1)}, bf16[2,64,512]{2,1,0:T(8,128)(2,1)S(1)}, u32[]{:S(2)}, u32[]{:S(2)}) collective-permute-start(bf16[2,64,512]{2,1,0:T(8,128)(2,1)} %get-tuple-element.34.refs_8_), channel_id=1, source_target_pairs={{0,8},{1,9},{2,10},{3,11},{4,12},{5,13},{6,14},{7,15},{8,0},{9,1},... | collective-permute-start | bytes 393224 | tf_op jit(solution)/shard_map/ppermute | solution.py:247
  57.8 12.4 %collective-permute-start.3 = (bf16[2,32,1024]{2,1,0:T(8,128)(2,1)}, bf16[2,32,1024]{2,1,0:T(8,128)(2,1)S(1)}, u32[]{:S(2)}, u32[]{:S(2)}) collective-permute-start(bf16[2,32,1024]{2,1,0:T(8,128)(2,1)} %get-tuple-element.25.refs_0_), channel_id=1, source_target_pairs={{0,1},{1,0},{2,3},{3,2},{4,5},{5,4},{6,7},{7,6},{8,9},{9,8},{10,11... | collective-permute-start | bytes 393224 | tf_op jit(solution)/shard_map/ppermute | solution.py:247
  58.3 11.8 %collective-permute-start.5 = (bf16[2,32,1024]{2,1,0:T(8,128)(2,1)S(1)}, bf16[2,32,1024]{2,1,0:T(8,128)(2,1)S(1)}, u32[]{:S(2)}, u32[]{:S(2)}) collective-permute-start(bf16[2,32,1024]{2,1,0:T(8,128)(2,1)S(1)} %collective-permute-done.4.refs_2_), channel_id=1, source_target_pairs={{0,1},{1,0},{2,3},{3,2},{4,5},{5,4},{6,7},{7,6},{8,9},{9,8},{10,11... | collective-permute-start | bytes 393224 | tf_op jit(solution)/shard_map/ppermute | solution.py:247
  58.3 11.8 %collective-permute-start.7 = (bf16[2,32,1024]{2,1,0:T(8,128)(2,1)S(1)}, bf16[2,32,1024]{2,1,0:T(8,128)(2,1)S(1)}, u32[]{:S(2)}, u32[]{:S(2)}) collective-permute-start(bf16[2,32,1024]{2,1,0:T(8,128)(2,1)S(1)} %collective-permute-done.6.refs_4_), channel_id=1, source_target_pairs={{0,1},{1,0},{2,3},{3,2},{4,5},{5,4},{6,7},{7,6},{8,9},{9,8},{10,11... | collective-permute-start | bytes 393224 | tf_op jit(solution)/shard_map/ppermute | solution.py:247
  58.9 11.3 %collective-permute-start.9 = (bf16[2,32,1024]{2,1,0:T(8,128)(2,1)S(1)}, bf16[2,32,1024]{2,1,0:T(8,128)(2,1)S(1)}, u32[]{:S(2)}, u32[]{:S(2)}) collective-permute-start(bf16[2,32,1024]{2,1,0:T(8,128)(2,1)S(1)} %collective-permute-done.8.refs_6_), channel_id=1, source_target_pairs={{0,1},{1,0},{2,3},{3,2},{4,5},{5,4},{6,7},{7,6},{8,9},{9,8},{10,11... | collective-permute-start | bytes 393224 | tf_op jit(solution)/shard_map/ppermute | solution.py:247
  60.7 9.5 %copy-start.2 = (bf16[2,64,512]{2,1,0:T(8,128)(2,1)S(1)}, bf16[2,64,512]{2,1,0:T(8,128)(2,1)}, u32[]{:S(2)}) copy-start(bf16[2,64,512]{2,1,0:T(8,128)(2,1)} %get-tuple-element.34.refs_8_) | copy-start | bytes 393220
  (16 other events, 34.1 us)
where the time goes:
time: 80 us; the launch traced here: 79.7 us
  Pallas kernels  27.7 us (35%)
  waiting for transfers between devices  23.9 us (30%)
  starting transfers between devices  21.7 us (27%)
  local copies, waits for them, and re-layouts  5.58 us (7%)
    ppermute x30, waiting for transfers between devices, send(): return lax.ppermute(value, AXES, pairs)  23.9 us
    ppermute x30, starting transfers between devices, send(): return lax.ppermute(value, AXES, pairs)  21.7 us
    pallas_call x2, Pallas kernels, multiply(): pl.pallas_call(functools.partial(product_body, len(lefts), len(rights), w...  18.9 us
    unnamed x36, local copies, waits for them, and re-layouts  5.58 us
    pallas_call x1, Pallas kernels, make_spectra(): pl.pallas_call(functools.partial(spectra_body, row_count, col_count), out...  5.54 us
    pallas_call x2, Pallas kernels, regroup(): pl.pallas_call(functools.partial(regroup_body, count), out_shape=[out] *...  3.22 us
  transfers between devices with their start and end apart: 30, of which 16 were waited for; matrix products, arithmetic and copies ran while one was open for 0% of the time, Pallas kernels for 14%

commit v1 on v0

v1 whole, which is shorter than its diff:
```python
import functools
import math

import jax
import jax.numpy as jnp
from jax import lax
from jax.experimental import pallas as pl
from jax.experimental.pallas import tpu as pltpu
from jax.sharding import PartitionSpec as P

F = 16
WL = 1280
TAPS = 101
SPAN = WL + TAPS - 1
LANES = 128
FLOOR = 0.5
CHUNK = 4
CHUNKS = F // CHUNK
GROUP = 2 * CHUNK
ROWS = 2 * F
CALLS = 2
WINDOW_GROUP = 2 * GROUP

AXES = ("row", "col")
BF16 = jnp.bfloat16
F32 = jnp.float32


def sine(x):
    square = x * x
    total = jnp.full_like(x, 1.0 / math.factorial(13))
    for order in (11, 9, 7, 5, 3, 1):
        sign = -1.0 if order % 4 == 3 else 1.0
        total = total * square + sign / math.factorial(order)
    return x * total


def analysis_rows(settings, pattern, stacked, kernel):
    depth = kernel.shape[1]
    blocks = depth // LANES
    times = lax.broadcasted_iota(jnp.int32, (1, WL), 1).astype(F32)
    row = lax.broadcasted_iota(jnp.int32, (ROWS, 1), 0)
    chosen = jnp.zeros((ROWS, 1), F32)
    for index in range(F):
        this = (row // GROUP == index // CHUNK) & (row % CHUNK == index % CHUNK)
        chosen = jnp.where(this, settings[TAPS + index], chosen)
    quarter = jnp.where(row % GROUP < CHUNK, 0.0, WL / 4.0)
    phase = chosen * times + quarter
    phase = phase - WL * jnp.floor((phase + 0.5) * (1.0 / WL))
    half = sine((phase - WL / 2.0) * (math.pi / WL))
    edge = times + 0.5
    taper = sine(jnp.minimum(edge, WL - edge) * (math.pi / WL))
    taper = taper * taper * (1.0 / math.sqrt(WL))
    pattern[:, :LANES] = jnp.zeros((ROWS, LANES), F32)
    pattern[:, LANES + WL :] = jnp.zeros((ROWS, depth - WL), F32)
    pattern[:, LANES : LANES + WL] = (2.0 * half * half - 1.0) * taper

    slack = depth - SPAN
    offset = settings[TAPS + F]
    lane = lax.broadcasted_iota(jnp.int32, (8, 2 * LANES), 1).astype(F32) - (slack - offset)
    filter_row = jnp.zeros((8, 2 * LANES), F32)
    for index in range(TAPS):
        filter_row = jnp.where(lane == index, settings[index], filter_row)
    filter_rows = jnp.concatenate([filter_row] * (LANES // 8), axis=0)
    band = pltpu.roll(filter_rows, 0, 1, stride=1, stride_axis=0)

    for block in range(blocks):
        stacked[block * ROWS : (block + 1) * ROWS, :] = pattern[
            :, block * LANES : (block + 2) * LANES
        ]
    filtered = lax.dot_general(
        stacked[...],
        band,
        (((1,), (1,)), ((), ())),
        precision=lax.Precision.HIGHEST,
        preferred_element_type=F32,
    )
    for block in range(blocks):
        kernel[:, block * LANES : (block + 1) * LANES] = filtered[
            block * ROWS : (block + 1) * ROWS
        ].astype(BF16)


def spectra_body(settings, record, whitened, samples, pattern, stacked, kernel, arrived):
    blocks, depth, width = samples.shape
    copies = []
    for block in range(blocks):
        copy = pltpu.make_async_copy(
            record.at[:, pl.ds(block * width, width)], samples.at[block], arrived.at[block]
        )
        copy.start()
        copies.append(copy)
    analysis_rows(settings, pattern, stacked, kernel)
    share = whitened.shape[2] // width
    for block in range(blocks):
        copies[block].wait()
        spectra = jnp.dot(kernel[...], samples[block], preferred_element_type=F32)
        shaped = spectra.reshape(CHUNKS, 2, CHUNK, width)
        real, imag = shaped[:, 0], shaped[:, 1]
        magnitude = jnp.sqrt(real * real + imag * imag)
        inverse = 1.0 / jnp.maximum(magnitude, FLOOR)
        scaled = (shaped * inverse[:, None]).reshape(ROWS, width)
        start = block % share * width
        whitened[block // share, :, start : start + width] = scaled.astype(BF16)


def make_spectra(record, settings, slices):
    depth, channels = record.shape
    blocks = 2 * slices
    width = channels // blocks
    return pl.pallas_call(
        spectra_body,
        out_shape=jax.ShapeDtypeStruct((slices, ROWS, channels // slices), BF16),
        in_specs=[pl.BlockSpec(memory_space=pltpu.SMEM), pl.BlockSpec(memory_space=pl.ANY)],
        out_specs=pl.BlockSpec(memory_space=pltpu.VMEM),
        scratch_shapes=[
            pltpu.VMEM((blocks, depth, width), BF16),
            pltpu.VMEM((ROWS, depth + LANES), F32),
            pltpu.VMEM((depth // LANES * ROWS, 2 * LANES), F32),
            pltpu.VMEM((ROWS, depth), BF16),
            pltpu.SemaphoreType.DMA((blocks,)),
        ],
        compiler_params=pltpu.CompilerParams(vmem_limit_bytes=24 * 2**20),
        name="spectra",
    )(settings, record)


def pair_body(own, other, *outs):
    row, col = lax.axis_index("row"), lax.axis_index("col")
    core = lax.rem(col, 2)
    place = jnp.where(core == 0, row, col // 2)
    for step, out in enumerate(outs):
        mine = own[place ^ step].astype(F32)
        theirs = other[place ^ step].astype(F32)
        first = jnp.where(core == 0, mine, theirs)
        second = jnp.where(core == 0, theirs, mine)
        pieces = []
        for chunk in range(CHUNKS):
            rows = slice(chunk * GROUP, (chunk + 1) * GROUP)
            pieces += [first[rows], second[rows]]
        out[...] = jnp.concatenate(pieces, axis=0).astype(BF16)


def pair_windows(own, other):
    slices, _, width = own.shape
    vmem = pl.BlockSpec(memory_space=pltpu.VMEM)
    return pl.pallas_call(
        pair_body,
        out_shape=[jax.ShapeDtypeStruct((2 * ROWS, width), BF16)] * slices,
        in_specs=[vmem] * 2,
        out_specs=[vmem] * slices,
        compiler_params=pltpu.CompilerParams(vmem_limit_bytes=8 * 2**20),
        name="pair_windows",
    )(own, other)


def regroup_body(count, *refs):
    per_call = CHUNKS // CALLS
    for chunk in range(CHUNKS):
        out = refs[count + chunk // per_call]
        for step in range(count):
            out[chunk % per_call, step * WINDOW_GROUP : (step + 1) * WINDOW_GROUP] = refs[step][
                chunk * WINDOW_GROUP : (chunk + 1) * WINDOW_GROUP
            ]


def regroup(pieces):
    count, width = len(pieces), pieces[0].shape[1]
    out = jax.ShapeDtypeStruct((CHUNKS // CALLS, count * WINDOW_GROUP, width), BF16)
    vmem = pl.BlockSpec(memory_space=pltpu.VMEM)
    return pl.pallas_call(
        functools.partial(regroup_body, count),
        out_shape=[out] * CALLS,
        in_specs=[vmem] * count,
        out_specs=[vmem] * CALLS,
        compiler_params=pltpu.CompilerParams(vmem_limit_bytes=8 * 2**20),
        name="regroup",
    )(*pieces)


def product_body(count, first, windows, *refs):
    held, swapped = refs[:count], refs[count : 2 * count]
    out, turned, straight, crossed, tiles, stored = refs[-6:]
    depth, width = straight.shape
    steps = tiles.shape[0]
    step = pl.program_id(0)
    chunk, index = step // CHUNK, lax.rem(step, CHUNK)
    core = lax.rem(lax.axis_index("col"), 2)

    def prepare(rows_of, cols_of, start):
        turned[...] = jnp.concatenate([ref[chunk] for ref in rows_of], axis=0).T
        pieces = [
            ref[chunk, group * WINDOW_GROUP : (group + 1) * WINDOW_GROUP, start : start + width]
            for group in range(count)
            for ref in cols_of
        ]
        right = jnp.concatenate(pieces, axis=0).astype(F32)
        straight[...] = right
        shaped = right.reshape(depth // GROUP, 2, CHUNK, width)
        crossed[...] = jnp.stack([shaped[:, 1], -shaped[:, 0]], axis=1).reshape(depth, width)

    pl.when((index == 0) & (core == 0))(functools.partial(prepare, held, swapped, 0))
    pl.when((index == 0) & (core == 1))(functools.partial(prepare, swapped, held, width))

    row = lax.broadcasted_iota(jnp.int32, (depth, width), 0)
    wanted = row % CHUNK == index
    for part, operand in enumerate((straight, crossed)):
        right = jnp.where(wanted, operand[...], 0.0).astype(BF16)
        product = jnp.dot(turned[...], right, preferred_element_type=F32)
        tiles[step, part] = (product * (1.0 / windows)).astype(BF16)
        pltpu.make_async_copy(
            tiles.at[step, part], out.at[first + step, part], stored.at[step, part]
        ).start()

    @pl.when(step == steps - 1)
    def _():
        for done in range(steps):
            for part in range(2):
                pltpu.make_async_copy(
                    tiles.at[done, part], out.at[first + done, part], stored.at[done, part]
                ).wait()


def multiply(call, held, swapped, windows, result):
    count = len(held)
    per_call, rows, height = held[0].shape
    depth, width = rows * count, height // 2
    steps = per_call * CHUNK
    vmem = pl.BlockSpec(memory_space=pltpu.VMEM)
    operands = [*held, *swapped]
    in_specs = [vmem] * len(operands)
    aliases = {}
    if result is not None:
        aliases = {len(operands): 0}
        in_specs.append(pl.BlockSpec(memory_space=pl.ANY))
        operands.append(result)
    return pl.pallas_call(
        functools.partial(product_body, count, call * steps, windows),
        out_shape=jax.ShapeDtypeStruct((F, 2, height, width), BF16),
        grid=(steps,),
        in_specs=in_specs,
        out_specs=pl.BlockSpec(memory_space=pl.ANY),
        scratch_shapes=[
            pltpu.VMEM((height, depth), BF16),
            pltpu.VMEM((depth, width), F32),
            pltpu.VMEM((depth, width), F32),
            pltpu.VMEM((steps, 2, height, width), BF16),
            pltpu.SemaphoreType.DMA((steps, 2)),
        ],
        input_output_aliases=aliases,
        compiler_params=pltpu.CompilerParams(vmem_limit_bytes=32 * 2**20),
        cost_estimate=pl.CostEstimate(
            flops=steps * 4 * height * width * depth,
            bytes_accessed=steps * 2 * height * width * 2,
            transcendentals=0,
        ),
        name="products",
    )(*operands)


def on_device(record, fir_taps, bins, offsets):
    row_count, col_count = lax.axis_size("row"), lax.axis_size("col")
    lines = col_count // 2
    windows = row_count * col_count

    def send(value, row_flip, line_flip, core_flip):
        pairs = []
        for row in range(row_count):
            for col in range(col_count):
                core, line = col % 2, col // 2
                target = 2 * (line ^ line_flip[core]) + (core ^ core_flip)
                pairs.append((row * col_count + col, (row ^ row_flip[core]) * col_count + target))
        return lax.ppermute(value, AXES, pairs)

    def swap(value):
        return send(value, (0, 0), (0, 0), 1)

    settings = jnp.concatenate([fir_taps, bins.astype(F32), offsets.astype(F32)])
    own = make_spectra(record, settings, row_count)
    to_send = pair_windows(own, swap(own))
    pieces = [to_send[0]]
    for step in range(1, row_count):
        pieces.append(send(to_send[step], (step, 0), (0, step), 0))
    started = regroup(pieces)

    result = None
    for call in range(CALLS):
        held = {0: started[call]}
        bit = row_count // 2
        while bit:
            for slot in list(held):
                held[slot ^ bit] = send(held[slot], (0, bit), (bit, 0), 0)
            bit //= 2
        ordered = [held[slot] for slot in range(row_count)]
        result = multiply(call, ordered, [swap(value) for value in ordered], windows, result)
    return result


def solution(mesh):
    placed = (P(("row", "col"), None), P(), P(), P(("row", "col")))
    return jax.shard_map(
        on_device,
        mesh=mesh,
        in_specs=placed,
        out_specs=P(None, None, "row", "col"),
        check_vma=False,
    )
```

time: 80 us -> 63.5 us (0.79)
  starting transfers between devices: 21.7 us -> 12.6 us
  Pallas kernels: 27.7 us -> 21.9 us
  waiting for transfers between devices: 23.9 us -> 22.2 us
  other arithmetic: 0.08 us -> 1.39 us
  local copies, waits for them, and re-layouts: 5.58 us -> 4.28 us
    ppermute x30 -> x18, starting transfers between devices: 21.7 us -> 12.6 us  [send(): return lax.ppermute(value, AXES, pairs)]
    pallas_call x2 -> x1, Pallas kernels: 3.22 us -> 0.03 us  [regroup(): pl.pallas_call(functools.partial(regroup_body, count), out_shape=[out] *...]
    pallas_call x3 -> x4, Pallas kernels: 24.4 us -> 21.9 us  [the longest x2 15.6 us: multiply(): pl.pallas_call(functools.partial(product_body, count, call * steps, windo...]
    ppermute x30 -> x18, waiting for transfers between devices: 23.9 us -> 22.2 us  [send(): return lax.ppermute(value, AXES, pairs)]
    unnamed x36 -> x2, local copies, waits for them, and re-layouts: 5.58 us -> 4.28 us
  transfers between devices with their start and end apart: 30 -> 18, of which waited for: 16 -> 9; matrix products, arithmetic and copies ran while one was open for 0% -> 0% of each run, Pallas kernels for 14% -> 12%
where the time goes in v1:
time: 63.5 us; the launch traced here: 63.2 us
  waiting for transfers between devices  22.2 us (35%)
  Pallas kernels  21.9 us (34%)
  starting transfers between devices  12.6 us (20%)
  local copies, waits for them, and re-layouts  4.28 us (7%)
  other arithmetic  1.39 us (2%)
  between operations  0.73 us (1%)
    ppermute x18, waiting for transfers between devices, send(): return lax.ppermute(value, AXES, pairs)  22.2 us
    pallas_call x2, Pallas kernels, multiply(): pl.pallas_call(functools.partial(product_body, count, call * steps, windo...  15.6 us
    ppermute x18, starting transfers between devices, send(): return lax.ppermute(value, AXES, pairs)  12.6 us
    pallas_call x1, Pallas kernels, make_spectra(): pl.pallas_call(spectra_body, out_shape=jax.ShapeDtypeStruct((slices, ROWS...  6.15 us
    unnamed x2, local copies, waits for them, and re-layouts  4.28 us
  transfers between devices with their start and end apart: 18, of which 9 were waited for; matrix products, arithmetic and copies ran while one was open for 0% of the time, Pallas kernels for 12%

profile of v1, /device:TPU:0, one launch (start us, length us, event | category | flops | bytes accessed | tf_op | source)
XLA Modules:
  0.0 63.2 jit_solution(16779999884796336360)
XLA Ops:
  0.7 0.7 %convert_element_type.6 = f32[16]{0:T(128)S(1)} convert(s32[16]{0:T(128)} %param.6) | non-fusion elementwise | flops 16 | bytes 128 | tf_op jit(solution)/shard_map/convert_element_type | solution.py:278
  1.3 0.7 %pad_maximum_fusion.settings = f32[118]{0:T(128)S(1)} fusion(f32[1]{0:T(128)S(6)} %convert_element_type.7, f32[16]{0:T(128)S(1)} %convert_element_type.6, f32[101]{0:T(128)} %param.5), kind=kLoop, calls=%fused_computation | loop fusion | flops 236 | bytes 944 | tf_op jit(solution)/shard_map/concatenate | solution.py:278
  2.0 4.3 %copy-done = bf16[1408,4096]{1,0:T(8,128)(2,1)S(1)} copy-done((bf16[1408,4096]{1,0:T(8,128)(2,1)S(1)}, bf16[1408,4096]{1,0:T(8,128)(2,1)}, u32[]{:S(2)}) %copy-start) | copy-done | bytes 11534360
  6.3 6.2 %spectra.1.own = bf16[4,32,1024]{2,1,0:T(8,128)(2,1)S(1)} custom-call(f32[118]{0:T(128)S(1)} %pad_maximum_fusion.settings, bf16[1408,4096]{1,0:T(8,128)(2,1)S(1)} %copy-done), custom_call_target="tpu_custom_call" | custom-call | tf_op jit(solution)/shard_map/spectra/pallas_call | solution.py:111
  12.5 0.5 collective-permute-start
  13.0 1.2 %collective-permute-done.other = bf16[4,32,1024]{2,1,0:T(8,128)(2,1)S(1)} collective-permute-done((bf16[4,32,1024]{2,1,0:T(8,128)(2,1)S(1)}, bf16[4,32,1024]{2,1,0:T(8,128)(2,1)S(1)}, u32[]{:S(2)}, u32[]{:S(2)}) %collective-permute-start) | collective-permute-done | bytes 262176 | tf_op jit(solution)/shard_map/ppermute | solution.py:273
  14.2 0.1 pair_windows.1
  14.3 2.9 %collective-permute-start.1 = (bf16[64,1024]{1,0:T(8,128)(2,1)S(1)}, bf16[64,1024]{1,0:T(8,128)(2,1)S(1)}, u32[]{:S(2)}, u32[]{:S(2)}) collective-permute-start(bf16[64,1024]{1,0:T(8,128)(2,1)S(1)} %get-tuple-element.12), channel_id=1, source_target_pairs={{0,8},{1,3},{2,10},{3,1},{4,12},{5,7},{6,14},{7,5},{8,0},{9,11},{1... | collective-permute-start | bytes 393224 | tf_op jit(solution)/shard_map/ppermute | solution.py:273
  17.2 1.5 %collective-permute-start.2 = (bf16[64,1024]{1,0:T(8,128)(2,1)S(1)}, bf16[64,1024]{1,0:T(8,128)(2,1)S(1)}, u32[]{:S(2)}, u32[]{:S(2)}) collective-permute-start(bf16[64,1024]{1,0:T(8,128)(2,1)S(1)} %get-tuple-element.13), channel_id=1, source_target_pairs={{0,16},{1,5},{2,18},{3,7},{4,20},{5,1},{6,22},{7,3},{8,24},{9,13},... | collective-permute-start | bytes 393224 | tf_op jit(solution)/shard_map/ppermute | solution.py:273
  18.7 0.0 collective-permute-start.3
  18.7 1.4 %collective-permute-done.1.refs_1_ = bf16[64,1024]{1,0:T(8,128)(2,1)S(1)} collective-permute-done((bf16[64,1024]{1,0:T(8,128)(2,1)S(1)}, bf16[64,1024]{1,0:T(8,128)(2,1)S(1)}, u32[]{:S(2)}, u32[]{:S(2)}) %collective-permute-start.1) | collective-permute-done | bytes 131104 | tf_op jit(solution)/shard_map/ppermute | solution.py:273
  20.1 2.0 %collective-permute-done.2.refs_2_ = bf16[64,1024]{1,0:T(8,128)(2,1)S(1)} collective-permute-done((bf16[64,1024]{1,0:T(8,128)(2,1)S(1)}, bf16[64,1024]{1,0:T(8,128)(2,1)S(1)}, u32[]{:S(2)}, u32[]{:S(2)}) %collective-permute-start.2) | collective-permute-done | bytes 131104 | tf_op jit(solution)/shard_map/ppermute | solution.py:273
  22.1 2.4 %collective-permute-done.3.refs_3_ = bf16[64,1024]{1,0:T(8,128)(2,1)S(1)} collective-permute-done((bf16[64,1024]{1,0:T(8,128)(2,1)S(1)}, bf16[64,1024]{1,0:T(8,128)(2,1)S(1)}, u32[]{:S(2)}, u32[]{:S(2)}) %collective-permute-start.3) | collective-permute-done | bytes 131104 | tf_op jit(solution)/shard_map/ppermute | solution.py:273
  24.6 2.7 %collective-permute-start.12 = (bf16[2,64,1024]{2,1,0:T(8,128)(2,1)S(1)}, bf16[2,64,1024]{2,1,0:T(8,128)(2,1)S(1)}, u32[]{:S(2)}, u32[]{:S(2)}) collective-permute-start(bf16[2,64,1024]{2,1,0:T(8,128)(2,1)S(1)} %get-tuple-element.16.refs_0_), channel_id=1, source_target_pairs={{0,4},{1,17},{2,6},{3,19},{4,0},{5,21},{6,2},{7,23},{8,12},{9,25},... | collective-permute-start | bytes 786440 | tf_op jit(solution)/shard_map/ppermute | solution.py:273
  27.3 0.3 collective-permute-start.5
  27.6 1.6 %collective-permute-start.4 = (bf16[2,64,1024]{2,1,0:T(8,128)(2,1)S(1)}, bf16[2,64,1024]{2,1,0:T(8,128)(2,1)S(1)}, u32[]{:S(2)}, u32[]{:S(2)}) collective-permute-start(bf16[2,64,1024]{2,1,0:T(8,128)(2,1)S(1)} %get-tuple-element.15.refs_0_), channel_id=1, source_target_pairs={{0,2},{1,9},{2,0},{3,11},{4,6},{5,13},{6,4},{7,15},{8,10},{9,1},{1... | collective-permute-start | bytes 786440 | tf_op jit(solution)/shard_map/ppermute | solution.py:273
  29.2 0.4 collective-permute-start.11
  29.6 8.0 %collective-permute-done.12.refs_2_ = bf16[2,64,1024]{2,1,0:T(8,128)(2,1)S(1)} collective-permute-done((bf16[2,64,1024]{2,1,0:T(8,128)(2,1)S(1)}, bf16[2,64,1024]{2,1,0:T(8,128)(2,1)S(1)}, u32[]{:S(2)}, u32[]{:S(2)}) %collective-permute-start.12) | collective-permute-done | bytes 262176 | tf_op jit(solution)/shard_map/ppermute | solution.py:273
  37.7 0.6 collective-permute-start.13
  38.3 0.0 collective-permute-start.14
  38.3 2.2 %collective-permute-done.5.refs_2_ = bf16[2,64,1024]{2,1,0:T(8,128)(2,1)S(1)} collective-permute-done((bf16[2,64,1024]{2,1,0:T(8,128)(2,1)S(1)}, bf16[2,64,1024]{2,1,0:T(8,128)(2,1)S(1)}, u32[]{:S(2)}, u32[]{:S(2)}) %collective-permute-start.5) | collective-permute-done | bytes 262176 | tf_op jit(solution)/shard_map/ppermute | solution.py:273
  40.5 0.6 collective-permute-start.6
  41.1 0.0 collective-permute-start.16
  41.1 0.2 collective-permute-done.11.refs_1_
  41.3 0.3 collective-permute-start.15
  41.6 2.5 %collective-permute-done.13.refs_3_ = bf16[2,64,1024]{2,1,0:T(8,128)(2,1)S(1)} collective-permute-done((bf16[2,64,1024]{2,1,0:T(8,128)(2,1)S(1)}, bf16[2,64,1024]{2,1,0:T(8,128)(2,1)S(1)}, u32[]{:S(2)}, u32[]{:S(2)}) %collective-permute-start.13) | collective-permute-done | bytes 262176 | tf_op jit(solution)/shard_map/ppermute | solution.py:273
  44.1 0.5 collective-permute-start.7
  44.6 2.3 %collective-permute-done.6.refs_3_ = bf16[2,64,1024]{2,1,0:T(8,128)(2,1)S(1)} collective-permute-done((bf16[2,64,1024]{2,1,0:T(8,128)(2,1)S(1)}, bf16[2,64,1024]{2,1,0:T(8,128)(2,1)S(1)}, u32[]{:S(2)}, u32[]{:S(2)}) %collective-permute-start.6) | collective-permute-done | bytes 262176 | tf_op jit(solution)/shard_map/ppermute | solution.py:273
  46.9 0.5 collective-permute-start.8
  47.4 0.1 collective-permute-start.10
  47.5 7.8 %products.2.refs_8_ = bf16[16,2,1024,512]{3,2,1,0:T(8,128)(2,1)} custom-call(bf16[2,64,1024]{2,1,0:T(8,128)(2,1)S(1)} %get-tuple-element.16.refs_0_, bf16[2,64,1024]{2,1,0:T(8,128)(2,1)S(1)} %collective-permute-done.11.refs_1_, bf16[2,64,1024]{2,1,0:T(8,128)(2,1)S(1)} %collective-permute-done.12.refs_2_, ...), custom_call_target="tpu_custom_call" | custom-call | flops 4294967296 | bytes 16777216 | tf_op jit(solution)/shard_map/products/pallas_call | solution.py:237
  55.3 7.8 %products.3 = bf16[16,2,1024,512]{3,2,1,0:T(8,128)(2,1)} custom-call(bf16[2,64,1024]{2,1,0:T(8,128)(2,1)S(1)} %get-tuple-element.15.refs_0_, bf16[2,64,1024]{2,1,0:T(8,128)(2,1)S(1)} %collective-permute-done.4.refs_1_, bf16[2,64,1024]{2,1,0:T(8,128)(2,1)S(1)} %collective-permute-done.5.refs_2_, ...), custom_call_target="tpu_custom_call", output_to_operand_aliasing={{}: (8, {})} | custom-call | flops 4294967296 | bytes 16777216 | tf_op jit(solution)/shard_map/products/pallas_call | solution.py:237
  (13 shorter events, 0.1 us)
Async XLA Ops:
  2.0 4.3 %copy-start = (bf16[1408,4096]{1,0:T(8,128)(2,1)S(1)}, bf16[1408,4096]{1,0:T(8,128)(2,1)}, u32[]{:S(2)}) copy-start(bf16[1408,4096]{1,0:T(8,128)(2,1)} %record.1) | copy-start | bytes 34603012
  12.5 1.7 %collective-permute-start = (bf16[4,32,1024]{2,1,0:T(8,128)(2,1)S(1)}, bf16[4,32,1024]{2,1,0:T(8,128)(2,1)S(1)}, u32[]{:S(2)}, u32[]{:S(2)}) collective-permute-start(bf16[4,32,1024]{2,1,0:T(8,128)(2,1)S(1)} %spectra.1.own), channel_id=1, source_target_pairs={{0,1},{1,0},{2,3},{3,2},{4,5},{5,4},{6,7},{7,6},{8,9},{9,8},{10,11... | collective-permute-start | bytes 786440 | tf_op jit(solution)/shard_map/ppermute | solution.py:273
  14.3 5.9 %collective-permute-start.1 = (bf16[64,1024]{1,0:T(8,128)(2,1)S(1)}, bf16[64,1024]{1,0:T(8,128)(2,1)S(1)}, u32[]{:S(2)}, u32[]{:S(2)}) collective-permute-start(bf16[64,1024]{1,0:T(8,128)(2,1)S(1)} %get-tuple-element.12), channel_id=1, source_target_pairs={{0,8},{1,3},{2,10},{3,1},{4,12},{5,7},{6,14},{7,5},{8,0},{9,11},{1... | collective-permute-start | bytes 393224 | tf_op jit(solution)/shard_map/ppermute | solution.py:273
  17.2 5.0 %collective-permute-start.2 = (bf16[64,1024]{1,0:T(8,128)(2,1)S(1)}, bf16[64,1024]{1,0:T(8,128)(2,1)S(1)}, u32[]{:S(2)}, u32[]{:S(2)}) collective-permute-start(bf16[64,1024]{1,0:T(8,128)(2,1)S(1)} %get-tuple-element.13), channel_id=1, source_target_pairs={{0,16},{1,5},{2,18},{3,7},{4,20},{5,1},{6,22},{7,3},{8,24},{9,13},... | collective-permute-start | bytes 393224 | tf_op jit(solution)/shard_map/ppermute | solution.py:273
  18.7 5.9 %collective-permute-start.3 = (bf16[64,1024]{1,0:T(8,128)(2,1)S(1)}, bf16[64,1024]{1,0:T(8,128)(2,1)S(1)}, u32[]{:S(2)}, u32[]{:S(2)}) collective-permute-start(bf16[64,1024]{1,0:T(8,128)(2,1)S(1)} %get-tuple-element.14), channel_id=1, source_target_pairs={{0,24},{1,7},{2,26},{3,5},{4,28},{5,3},{6,30},{7,1},{8,16},{9,15},... | collective-permute-start | bytes 393224 | tf_op jit(solution)/shard_map/ppermute | solution.py:273
  24.6 13.1 %collective-permute-start.12 = (bf16[2,64,1024]{2,1,0:T(8,128)(2,1)S(1)}, bf16[2,64,1024]{2,1,0:T(8,128)(2,1)S(1)}, u32[]{:S(2)}, u32[]{:S(2)}) collective-permute-start(bf16[2,64,1024]{2,1,0:T(8,128)(2,1)S(1)} %get-tuple-element.16.refs_0_), channel_id=1, source_target_pairs={{0,4},{1,17},{2,6},{3,19},{4,0},{5,21},{6,2},{7,23},{8,12},{9,25},... | collective-permute-start | bytes 786440 | tf_op jit(solution)/shard_map/ppermute | solution.py:273
  27.3 13.2 %collective-permute-start.5 = (bf16[2,64,1024]{2,1,0:T(8,128)(2,1)S(1)}, bf16[2,64,1024]{2,1,0:T(8,128)(2,1)S(1)}, u32[]{:S(2)}, u32[]{:S(2)}) collective-permute-start(bf16[2,64,1024]{2,1,0:T(8,128)(2,1)S(1)} %get-tuple-element.15.refs_0_), channel_id=1, source_target_pairs={{0,4},{1,17},{2,6},{3,19},{4,0},{5,21},{6,2},{7,23},{8,12},{9,25},... | collective-permute-start | bytes 786440 | tf_op jit(solution)/shard_map/ppermute | solution.py:273
  27.6 13.5 %collective-permute-start.4 = (bf16[2,64,1024]{2,1,0:T(8,128)(2,1)S(1)}, bf16[2,64,1024]{2,1,0:T(8,128)(2,1)S(1)}, u32[]{:S(2)}, u32[]{:S(2)}) collective-permute-start(bf16[2,64,1024]{2,1,0:T(8,128)(2,1)S(1)} %get-tuple-element.15.refs_0_), channel_id=1, source_target_pairs={{0,2},{1,9},{2,0},{3,11},{4,6},{5,13},{6,4},{7,15},{8,10},{9,1},{1... | collective-permute-start | bytes 786440 | tf_op jit(solution)/shard_map/ppermute | solution.py:273
  29.2 12.1 %collective-permute-start.11 = (bf16[2,64,1024]{2,1,0:T(8,128)(2,1)S(1)}, bf16[2,64,1024]{2,1,0:T(8,128)(2,1)S(1)}, u32[]{:S(2)}, u32[]{:S(2)}) collective-permute-start(bf16[2,64,1024]{2,1,0:T(8,128)(2,1)S(1)} %get-tuple-element.16.refs_0_), channel_id=1, source_target_pairs={{0,2},{1,9},{2,0},{3,11},{4,6},{5,13},{6,4},{7,15},{8,10},{9,1},{1... | collective-permute-start | bytes 786440 | tf_op jit(solution)/shard_map/ppermute | solution.py:273
  37.7 6.4 %collective-permute-start.13 = (bf16[2,64,1024]{2,1,0:T(8,128)(2,1)S(1)}, bf16[2,64,1024]{2,1,0:T(8,128)(2,1)S(1)}, u32[]{:S(2)}, u32[]{:S(2)}) collective-permute-start(bf16[2,64,1024]{2,1,0:T(8,128)(2,1)S(1)} %collective-permute-done.12.refs_2_), channel_id=1, source_target_pairs={{0,2},{1,9},{2,0},{3,11},{4,6},{5,13},{6,4},{7,15},{8,10},{9,1},{1... | collective-permute-start | bytes 786440 | tf_op jit(solution)/shard_map/ppermute | solution.py:273
  38.3 5.8 %collective-permute-start.14 = (bf16[2,64,1024]{2,1,0:T(8,128)(2,1)S(1)}, bf16[2,64,1024]{2,1,0:T(8,128)(2,1)S(1)}, u32[]{:S(2)}, u32[]{:S(2)}) collective-permute-start(bf16[2,64,1024]{2,1,0:T(8,128)(2,1)S(1)} %get-tuple-element.16.refs_0_), channel_id=1, source_target_pairs={{0,1},{1,0},{2,3},{3,2},{4,5},{5,4},{6,7},{7,6},{8,9},{9,8},{10,11... | collective-permute-start | bytes 786440 | tf_op jit(solution)/shard_map/ppermute | solution.py:273
  40.5 6.4 %collective-permute-start.6 = (bf16[2,64,1024]{2,1,0:T(8,128)(2,1)S(1)}, bf16[2,64,1024]{2,1,0:T(8,128)(2,1)S(1)}, u32[]{:S(2)}, u32[]{:S(2)}) collective-permute-start(bf16[2,64,1024]{2,1,0:T(8,128)(2,1)S(1)} %collective-permute-done.5.refs_2_), channel_id=1, source_target_pairs={{0,2},{1,9},{2,0},{3,11},{4,6},{5,13},{6,4},{7,15},{8,10},{9,1},{1... | collective-permute-start | bytes 786440 | tf_op jit(solution)/shard_map/ppermute | solution.py:273
  41.1 5.8 %collective-permute-start.16 = (bf16[2,64,1024]{2,1,0:T(8,128)(2,1)S(1)}, bf16[2,64,1024]{2,1,0:T(8,128)(2,1)S(1)}, u32[]{:S(2)}, u32[]{:S(2)}) collective-permute-start(bf16[2,64,1024]{2,1,0:T(8,128)(2,1)S(1)} %collective-permute-done.12.refs_2_), channel_id=1, source_target_pairs={{0,1},{1,0},{2,3},{3,2},{4,5},{5,4},{6,7},{7,6},{8,9},{9,8},{10,11... | collective-permute-start | bytes 786440 | tf_op jit(solution)/shard_map/ppermute | solution.py:273
  41.3 6.1 %collective-permute-start.15 = (bf16[2,64,1024]{2,1,0:T(8,128)(2,1)S(1)}, bf16[2,64,1024]{2,1,0:T(8,128)(2,1)S(1)}, u32[]{:S(2)}, u32[]{:S(2)}) collective-permute-start(bf16[2,64,1024]{2,1,0:T(8,128)(2,1)S(1)} %collective-permute-done.11.refs_1_), channel_id=1, source_target_pairs={{0,1},{1,0},{2,3},{3,2},{4,5},{5,4},{6,7},{7,6},{8,9},{9,8},{10,11... | collective-permute-start | bytes 786440 | tf_op jit(solution)/shard_map/ppermute | solution.py:273
  44.1 3.4 %collective-permute-start.17 = (bf16[2,64,1024]{2,1,0:T(8,128)(2,1)S(1)}, bf16[2,64,1024]{2,1,0:T(8,128)(2,1)S(1)}, u32[]{:S(2)}, u32[]{:S(2)}) collective-permute-start(bf16[2,64,1024]{2,1,0:T(8,128)(2,1)S(1)} %collective-permute-done.13.refs_3_), channel_id=1, source_target_pairs={{0,1},{1,0},{2,3},{3,2},{4,5},{5,4},{6,7},{7,6},{8,9},{9,8},{10,11... | collective-permute-start | bytes 786440 | tf_op jit(solution)/shard_map/ppermute | solution.py:273
  44.1 11.2 %collective-permute-start.7 = (bf16[2,64,1024]{2,1,0:T(8,128)(2,1)S(1)}, bf16[2,64,1024]{2,1,0:T(8,128)(2,1)S(1)}, u32[]{:S(2)}, u32[]{:S(2)}) collective-permute-start(bf16[2,64,1024]{2,1,0:T(8,128)(2,1)S(1)} %get-tuple-element.15.refs_0_), channel_id=1, source_target_pairs={{0,1},{1,0},{2,3},{3,2},{4,5},{5,4},{6,7},{7,6},{8,9},{9,8},{10,11... | collective-permute-start | bytes 786440 | tf_op jit(solution)/shard_map/ppermute | solution.py:273
  46.9 8.4 %collective-permute-start.9 = (bf16[2,64,1024]{2,1,0:T(8,128)(2,1)S(1)}, bf16[2,64,1024]{2,1,0:T(8,128)(2,1)S(1)}, u32[]{:S(2)}, u32[]{:S(2)}) collective-permute-start(bf16[2,64,1024]{2,1,0:T(8,128)(2,1)S(1)} %collective-permute-done.5.refs_2_), channel_id=1, source_target_pairs={{0,1},{1,0},{2,3},{3,2},{4,5},{5,4},{6,7},{7,6},{8,9},{9,8},{10,11... | collective-permute-start | bytes 786440 | tf_op jit(solution)/shard_map/ppermute | solution.py:273
  46.9 8.4 %collective-permute-start.8 = (bf16[2,64,1024]{2,1,0:T(8,128)(2,1)S(1)}, bf16[2,64,1024]{2,1,0:T(8,128)(2,1)S(1)}, u32[]{:S(2)}, u32[]{:S(2)}) collective-permute-start(bf16[2,64,1024]{2,1,0:T(8,128)(2,1)S(1)} %collective-permute-done.4.refs_1_), channel_id=1, source_target_pairs={{0,1},{1,0},{2,3},{3,2},{4,5},{5,4},{6,7},{7,6},{8,9},{9,8},{10,11... | collective-permute-start | bytes 786440 | tf_op jit(solution)/shard_map/ppermute | solution.py:273
  47.4 7.9 %collective-permute-start.10 = (bf16[2,64,1024]{2,1,0:T(8,128)(2,1)S(1)}, bf16[2,64,1024]{2,1,0:T(8,128)(2,1)S(1)}, u32[]{:S(2)}, u32[]{:S(2)}) collective-permute-start(bf16[2,64,1024]{2,1,0:T(8,128)(2,1)S(1)} %collective-permute-done.6.refs_3_), channel_id=1, source_target_pairs={{0,1},{1,0},{2,3},{3,2},{4,5},{5,4},{6,7},{7,6},{8,9},{9,8},{10,11... | collective-permute-start | bytes 786440 | tf_op jit(solution)/shard_map/ppermute | solution.py:273

commit v2 on v1

--- a/solution.py
+++ b/solution.py
@@ -35,7 +35,7 @@
     return x * total
 
 
-def analysis_rows(settings, pattern, stacked, kernel):
+def analysis_rows(taps, bins, offsets, pattern, stacked, kernel):
     depth = kernel.shape[1]
     blocks = depth // LANES
     times = lax.broadcasted_iota(jnp.int32, (1, WL), 1).astype(F32)
@@ -43,7 +43,7 @@
     chosen = jnp.zeros((ROWS, 1), F32)
     for index in range(F):
         this = (row // GROUP == index // CHUNK) & (row % CHUNK == index % CHUNK)
-        chosen = jnp.where(this, settings[TAPS + index], chosen)
+        chosen = jnp.where(this, bins[index].astype(F32), chosen)
     quarter = jnp.where(row % GROUP < CHUNK, 0.0, WL / 4.0)
     phase = chosen * times + quarter
     phase = phase - WL * jnp.floor((phase + 0.5) * (1.0 / WL))
@@ -56,11 +56,10 @@
     pattern[:, LANES : LANES + WL] = (2.0 * half * half - 1.0) * taper
 
     slack = depth - SPAN
-    offset = settings[TAPS + F]
-    lane = lax.broadcasted_iota(jnp.int32, (8, 2 * LANES), 1).astype(F32) - (slack - offset)
+    lane = lax.broadcasted_iota(jnp.int32, (8, 2 * LANES), 1) - (slack - offsets[0])
     filter_row = jnp.zeros((8, 2 * LANES), F32)
     for index in range(TAPS):
-        filter_row = jnp.where(lane == index, settings[index], filter_row)
+        filter_row = jnp.where(lane == index, taps[index], filter_row)
     filter_rows = jnp.concatenate([filter_row] * (LANES // 8), axis=0)
     band = pltpu.roll(filter_rows, 0, 1, stride=1, stride_axis=0)
 
@@ -81,8 +80,15 @@
         ].astype(BF16)
 
 
-def spectra_body(settings, record, whitened, samples, pattern, stacked, kernel, arrived):
+def spectra_body(fir_taps, bins, offsets, record, whitened, *scratch):
+    samples, pattern, stacked, kernel, arrived, taps_held, bins_held, offsets_held, read = scratch
     blocks, depth, width = samples.shape
+    small = []
+    for index, pair in enumerate(
+        ((fir_taps, taps_held), (bins, bins_held), (offsets, offsets_held))
+    ):
+        small.append(pltpu.make_async_copy(*pair, read.at[index]))
+        small[-1].start()
     copies = []
     for block in range(blocks):
         copy = pltpu.make_async_copy(
@@ -90,7 +96,9 @@
         )
         copy.start()
         copies.append(copy)
-    analysis_rows(settings, pattern, stacked, kernel)
+    for copy in small:
+        copy.wait()
+    analysis_rows(taps_held, bins_held, offsets_held, pattern, stacked, kernel)
     share = whitened.shape[2] // width
     for block in range(blocks):
         copies[block].wait()
@@ -104,14 +112,14 @@
         whitened[block // share, :, start : start + width] = scaled.astype(BF16)
 
 
-def make_spectra(record, settings, slices):
+def make_spectra(record, fir_taps, bins, offsets, slices):
     depth, channels = record.shape
     blocks = 2 * slices
     width = channels // blocks
     return pl.pallas_call(
         spectra_body,
         out_shape=jax.ShapeDtypeStruct((slices, ROWS, channels // slices), BF16),
-        in_specs=[pl.BlockSpec(memory_space=pltpu.SMEM), pl.BlockSpec(memory_space=pl.ANY)],
+        in_specs=[pl.BlockSpec(memory_space=pltpu.HBM)] * 4,
         out_specs=pl.BlockSpec(memory_space=pltpu.VMEM),
         scratch_shapes=[
             pltpu.VMEM((blocks, depth, width), BF16),
@@ -119,10 +127,14 @@
             pltpu.VMEM((depth // LANES * ROWS, 2 * LANES), F32),
             pltpu.VMEM((ROWS, depth), BF16),
             pltpu.SemaphoreType.DMA((blocks,)),
+            pltpu.SMEM(fir_taps.shape, F32),
+            pltpu.SMEM(bins.shape, jnp.int32),
+            pltpu.SMEM(offsets.shape, jnp.int32),
+            pltpu.SemaphoreType.DMA((3,)),
         ],
-        compiler_params=pltpu.CompilerParams(vmem_limit_bytes=24 * 2**20),
+        compiler_params=pltpu.CompilerParams(vmem_limit_bytes=56 * 2**20),
         name="spectra",
-    )(settings, record)
+    )(fir_taps, bins, offsets, record)
 
 
 def pair_body(own, other, *outs):
@@ -154,37 +166,52 @@
     )(own, other)
 
 
-def regroup_body(count, *refs):
-    per_call = CHUNKS // CALLS
-    for chunk in range(CHUNKS):
-        out = refs[count + chunk // per_call]
+def regroup_body(call, count, *refs):
+    out = refs[-1]
+    for chunk in range(out.shape[0]):
+        start = (call * out.shape[0] + chunk) * WINDOW_GROUP
         for step in range(count):
-            out[chunk % per_call, step * WINDOW_GROUP : (step + 1) * WINDOW_GROUP] = refs[step][
-                chunk * WINDOW_GROUP : (chunk + 1) * WINDOW_GROUP
+            out[chunk, step * WINDOW_GROUP : (step + 1) * WINDOW_GROUP] = refs[step][
+                start : start + WINDOW_GROUP
             ]
 
 
-def regroup(pieces):
+def regroup(call, pieces, after):
     count, width = len(pieces), pieces[0].shape[1]
-    out = jax.ShapeDtypeStruct((CHUNKS // CALLS, count * WINDOW_GROUP, width), BF16)
     vmem = pl.BlockSpec(memory_space=pltpu.VMEM)
     return pl.pallas_call(
-        functools.partial(regroup_body, count),
-        out_shape=[out] * CALLS,
-        in_specs=[vmem] * count,
-        out_specs=[vmem] * CALLS,
+        functools.partial(regroup_body, call, count),
+        out_shape=jax.ShapeDtypeStruct((CHUNKS // CALLS, count * WINDOW_GROUP, width), BF16),
+        in_specs=[vmem] * (count + len(after)),
+        out_specs=vmem,
         compiler_params=pltpu.CompilerParams(vmem_limit_bytes=8 * 2**20),
         name="regroup",
-    )(*pieces)
+    )(*pieces, *after)
+
+
+def hold_body(value, after, out):
+    out[...] = value[...]
+
+
+def hold(value, after):
+    vmem = pl.BlockSpec(memory_space=pltpu.VMEM)
+    return pl.pallas_call(
+        hold_body,
+        out_shape=jax.ShapeDtypeStruct(value.shape, value.dtype),
+        in_specs=[vmem, vmem],
+        out_specs=vmem,
+        compiler_params=pltpu.CompilerParams(vmem_limit_bytes=8 * 2**20),
+        name="hold",
+    )(value, after)
 
 
 def product_body(count, first, windows, *refs):
     held, swapped = refs[:count], refs[count : 2 * count]
-    out, turned, straight, crossed, tiles, stored = refs[-6:]
-    depth, width = straight.shape
-    steps = tiles.shape[0]
-    step = pl.program_id(0)
-    chunk, index = step // CHUNK, lax.rem(step, CHUNK)
+    out, finished, turned, right, tiles, stored = refs[-6:]
+    depth, double = right.shape
+    width = double // 2
+    chunks = pl.num_programs(0)
+    chunk = pl.program_id(0)
     core = lax.rem(lax.axis_index("col"), 2)
 
     def prepare(rows_of, cols_of, start):
@@ -194,40 +221,44 @@
             for group in range(count)
             for ref in cols_of
         ]
-        right = jnp.concatenate(pieces, axis=0).astype(F32)
-        straight[...] = right
-        shaped = right.reshape(depth // GROUP, 2, CHUNK, width)
-        crossed[...] = jnp.stack([shaped[:, 1], -shaped[:, 0]], axis=1).reshape(depth, width)
-
-    pl.when((index == 0) & (core == 0))(functools.partial(prepare, held, swapped, 0))
-    pl.when((index == 0) & (core == 1))(functools.partial(prepare, swapped, held, width))
-
-    row = lax.broadcasted_iota(jnp.int32, (depth, width), 0)
-    wanted = row % CHUNK == index
-    for part, operand in enumerate((straight, crossed)):
-        right = jnp.where(wanted, operand[...], 0.0).astype(BF16)
-        product = jnp.dot(turned[...], right, preferred_element_type=F32)
-        tiles[step, part] = (product * (1.0 / windows)).astype(BF16)
-        pltpu.make_async_copy(
-            tiles.at[step, part], out.at[first + step, part], stored.at[step, part]
-        ).start()
-
-    @pl.when(step == steps - 1)
+        straight = jnp.concatenate(pieces, axis=0).astype(F32)
+        shaped = straight.reshape(depth // GROUP, 2, CHUNK, width)
+        crossed = jnp.stack([shaped[:, 1], -shaped[:, 0]], axis=1).reshape(depth, width)
+        right[:, :width] = straight
+        right[:, width:] = crossed
+
+    pl.when(core == 0)(functools.partial(prepare, held, swapped, 0))
+    pl.when(core == 1)(functools.partial(prepare, swapped, held, width))
+
+    def store(bin_index, part):
+        return pltpu.make_async_copy(
+            tiles.at[bin_index, part], out.at[first + bin_index, part], stored.at[bin_index, part]
+        )
+
+    row = lax.broadcasted_iota(jnp.int32, (depth, double), 0)
+    for index in range(CHUNK):
+        chosen = jnp.where(row % CHUNK == index, right[...], 0.0).astype(BF16)
+        product = jnp.dot(turned[...], chosen, preferred_element_type=F32)
+        for part in range(2):
+            scaled = product[:, part * width : (part + 1) * width] * (1.0 / windows)
+            tiles[chunk * CHUNK + index, part] = scaled.astype(BF16)
+            store(chunk * CHUNK + index, part).start()
+
+    @pl.when(chunk == chunks - 1)
     def _():
-        for done in range(steps):
+        for bin_index in range(tiles.shape[0]):
             for part in range(2):
-                pltpu.make_async_copy(
-                    tiles.at[done, part], out.at[first + done, part], stored.at[done, part]
-                ).wait()
-
-
-def multiply(call, held, swapped, windows, result):
+                store(bin_index, part).wait()
+        finished[...] = jnp.zeros_like(finished)
+
+
+def multiply(call, held, swapped, windows, result, after):
     count = len(held)
     per_call, rows, height = held[0].shape
     depth, width = rows * count, height // 2
     steps = per_call * CHUNK
     vmem = pl.BlockSpec(memory_space=pltpu.VMEM)
-    operands = [*held, *swapped]
+    operands = [*held, *swapped, *after]
     in_specs = [vmem] * len(operands)
     aliases = {}
     if result is not None:
@@ -236,14 +267,16 @@
         operands.append(result)
     return pl.pallas_call(
         functools.partial(product_body, count, call * steps, windows),
-        out_shape=jax.ShapeDtypeStruct((F, 2, height, width), BF16),
-        grid=(steps,),
+        out_shape=[
+            jax.ShapeDtypeStruct((F, 2, height, width), BF16),
+            jax.ShapeDtypeStruct((8, LANES), F32),
+        ],
+        grid=(per_call,),
         in_specs=in_specs,
-        out_specs=pl.BlockSpec(memory_space=pl.ANY),
+        out_specs=[pl.BlockSpec(memory_space=pl.ANY), vmem],
         scratch_shapes=[
             pltpu.VMEM((height, depth), BF16),
-            pltpu.VMEM((depth, width), F32),
-            pltpu.VMEM((depth, width), F32),
+            pltpu.VMEM((depth, 2 * width), F32),
             pltpu.VMEM((steps, 2, height, width), BF16),
             pltpu.SemaphoreType.DMA((steps, 2)),
         ],
@@ -275,24 +308,31 @@
     def swap(value):
         return send(value, (0, 0), (0, 0), 1)
 
-    settings = jnp.concatenate([fir_taps, bins.astype(F32), offsets.astype(F32)])
-    own = make_spectra(record, settings, row_count)
+    own = make_spectra(record, fir_taps, bins, offsets, row_count)
     to_send = pair_windows(own, swap(own))
     pieces = [to_send[0]]
     for step in range(1, row_count):
         pieces.append(send(to_send[step], (step, 0), (0, step), 0))
-    started = regroup(pieces)
-
-    result = None
+
+    bits = [row_count >> shift for shift in range(1, row_count.bit_length())]
+    gathered, after = [], []
     for call in range(CALLS):
-        held = {0: started[call]}
-        bit = row_count // 2
-        while bit:
+        held = {0: regroup(call, pieces, after)}
+        for bit in bits:
             for slot in list(held):
                 held[slot ^ bit] = send(held[slot], (0, bit), (bit, 0), 0)
-            bit //= 2
+        after = [held[bits[0]]]
+        gathered.append(held)
+
+    result, finished = None, None
+    for call, held in enumerate(gathered):
         ordered = [held[slot] for slot in range(row_count)]
-        result = multiply(call, ordered, [swap(value) for value in ordered], windows, result)
+        last = row_count - 1
+        if result is not None:
+            ordered[last] = hold(ordered[last], finished)
+        after = [gathered[call + 1][bits[0]]] if call + 1 < CALLS else []
+        swapped = [swap(value) for value in ordered]
+        result, finished = multiply(call, ordered, swapped, windows, result, after)
     return result
 
 

time: 63.5 us -> 59.2 us (0.932)
  local copies, waits for them, and re-layouts: 4.28 us -> 0.95 us
  starting transfers between devices: 12.6 us -> 15.6 us
  Pallas kernels: 21.9 us -> 20 us
  other arithmetic: 1.39 us -> 0 us
    unnamed x2, local copies, waits for them, and re-layouts: 4.28 us -> 0.95 us
    ppermute x18, starting transfers between devices: 12.6 us -> 15.6 us  [send(): return lax.ppermute(value, AXES, pairs)]
    pallas_call x2, Pallas kernels: 15.6 us -> 14.2 us  [multiply(): pl.pallas_call(functools.partial(product_body, count, call * steps, windo...]
    concatenate x1 -> x0, other arithmetic: 0.73 us -> none  [on_device(): jnp.concatenate([fir_taps, bins.astype(F32), offsets.astype(F32)])]
    convert_element_type x1 -> x0, other arithmetic: 0.66 us -> none  [on_device(): bins.astype(F32)]
where the time goes in v2:
time: 59.2 us; the launch traced here: 59 us
  waiting for transfers between devices  21.8 us (37%)
  Pallas kernels  20 us (34%)
  starting transfers between devices  15.6 us (26%)
  local copies, waits for them, and re-layouts  0.95 us (2%)
  between operations  0.72 us (1%)
    ppermute x18, waiting for transfers between devices, send(): return lax.ppermute(value, AXES, pairs)  21.8 us
    ppermute x18, starting transfers between devices, send(): return lax.ppermute(value, AXES, pairs)  15.6 us
    pallas_call x2, Pallas kernels, multiply(): pl.pallas_call(functools.partial(product_body, count, call * steps, windo...  14.2 us
    pallas_call x1, Pallas kernels, make_spectra(): pl.pallas_call(spectra_body, out_shape=jax.ShapeDtypeStruct((slices, ROWS...  5.66 us
  transfers between devices with their start and end apart: 18, of which 9 were waited for; matrix products, arithmetic and copies ran while one was open for 0% of the time, Pallas kernels for 12%

profile of v2, /device:TPU:0, one launch (start us, length us, event | category | flops | bytes accessed | tf_op | source)
XLA Modules:
  0.0 59.0 jit_solution(11176300040397578442)
XLA Ops:
  0.7 5.7 %spectra.1.own = bf16[4,32,1024]{2,1,0:T(8,128)(2,1)} custom-call(f32[101]{0:T(128)} %fir_taps.1, s32[16]{0:T(128)} %bins.1, s32[1]{0:T(128)S(6)} %copy.7.offsets, bf16[1408,4096]{1,0:T(8,128)(2,1)} %record.1), custom_call_target="tpu_custom_call" | custom-call | tf_op jit(solution)/shard_map/spectra/pallas_call | solution.py:119
  6.3 0.5 collective-permute-start
  6.8 1.4 %collective-permute-done.other = bf16[4,32,1024]{2,1,0:T(8,128)(2,1)S(1)} collective-permute-done((bf16[4,32,1024]{2,1,0:T(8,128)(2,1)}, bf16[4,32,1024]{2,1,0:T(8,128)(2,1)S(1)}, u32[]{:S(2)}, u32[]{:S(2)}) %collective-permute-start) | collective-permute-done | bytes 262176 | tf_op jit(solution)/shard_map/ppermute | solution.py:306
  8.2 0.9 %copy-done = bf16[4,32,1024]{2,1,0:T(8,128)(2,1)S(1)} copy-done((bf16[4,32,1024]{2,1,0:T(8,128)(2,1)S(1)}, bf16[4,32,1024]{2,1,0:T(8,128)(2,1)}, u32[]{:S(2)}) %copy-start) | copy-done | bytes 262168
  9.2 0.1 pair_windows.1
  9.3 2.9 %collective-permute-start.1 = (bf16[64,1024]{1,0:T(8,128)(2,1)S(1)}, bf16[64,1024]{1,0:T(8,128)(2,1)S(1)}, u32[]{:S(2)}, u32[]{:S(2)}) collective-permute-start(bf16[64,1024]{1,0:T(8,128)(2,1)S(1)} %get-tuple-element.13), channel_id=1, source_target_pairs={{0,8},{1,3},{2,10},{3,1},{4,12},{5,7},{6,14},{7,5},{8,0},{9,11},{1... | collective-permute-start | bytes 393224 | tf_op jit(solution)/shard_map/ppermute | solution.py:306
  12.2 1.5 %collective-permute-start.2 = (bf16[64,1024]{1,0:T(8,128)(2,1)S(1)}, bf16[64,1024]{1,0:T(8,128)(2,1)S(1)}, u32[]{:S(2)}, u32[]{:S(2)}) collective-permute-start(bf16[64,1024]{1,0:T(8,128)(2,1)S(1)} %get-tuple-element.14), channel_id=1, source_target_pairs={{0,16},{1,5},{2,18},{3,7},{4,20},{5,1},{6,22},{7,3},{8,24},{9,13},... | collective-permute-start | bytes 393224 | tf_op jit(solution)/shard_map/ppermute | solution.py:306
  13.7 0.0 collective-permute-start.3
  13.7 1.4 %collective-permute-done.1.refs_1_ = bf16[64,1024]{1,0:T(8,128)(2,1)S(1)} collective-permute-done((bf16[64,1024]{1,0:T(8,128)(2,1)S(1)}, bf16[64,1024]{1,0:T(8,128)(2,1)S(1)}, u32[]{:S(2)}, u32[]{:S(2)}) %collective-permute-start.1) | collective-permute-done | bytes 131104 | tf_op jit(solution)/shard_map/ppermute | solution.py:306
  15.1 2.0 %collective-permute-done.2.refs_2_ = bf16[64,1024]{1,0:T(8,128)(2,1)S(1)} collective-permute-done((bf16[64,1024]{1,0:T(8,128)(2,1)S(1)}, bf16[64,1024]{1,0:T(8,128)(2,1)S(1)}, u32[]{:S(2)}, u32[]{:S(2)}) %collective-permute-start.2) | collective-permute-done | bytes 131104 | tf_op jit(solution)/shard_map/ppermute | solution.py:306
  17.1 2.4 %collective-permute-done.3.refs_3_ = bf16[64,1024]{1,0:T(8,128)(2,1)S(1)} collective-permute-done((bf16[64,1024]{1,0:T(8,128)(2,1)S(1)}, bf16[64,1024]{1,0:T(8,128)(2,1)S(1)}, u32[]{:S(2)}, u32[]{:S(2)}) %collective-permute-start.3) | collective-permute-done | bytes 131104 | tf_op jit(solution)/shard_map/ppermute | solution.py:306
  19.6 2.7 %collective-permute-start.4 = (bf16[2,64,1024]{2,1,0:T(8,128)(2,1)S(1)}, bf16[2,64,1024]{2,1,0:T(8,128)(2,1)S(1)}, u32[]{:S(2)}, u32[]{:S(2)}) collective-permute-start(bf16[2,64,1024]{2,1,0:T(8,128)(2,1)S(1)} %regroup.2.refs_0_), channel_id=1, source_target_pairs={{0,4},{1,17},{2,6},{3,19},{4,0},{5,21},{6,2},{7,23},{8,12},{9,25},... | collective-permute-start | bytes 786440 | tf_op jit(solution)/shard_map/ppermute | solution.py:306
  22.2 1.6 %collective-permute-start.8 = (bf16[2,64,1024]{2,1,0:T(8,128)(2,1)S(1)}, bf16[2,64,1024]{2,1,0:T(8,128)(2,1)S(1)}, u32[]{:S(2)}, u32[]{:S(2)}) collective-permute-start(bf16[2,64,1024]{2,1,0:T(8,128)(2,1)S(1)} %regroup.2.refs_0_), channel_id=1, source_target_pairs={{0,2},{1,9},{2,0},{3,11},{4,6},{5,13},{6,4},{7,15},{8,10},{9,1},{1... | collective-permute-start | bytes 786440 | tf_op jit(solution)/shard_map/ppermute | solution.py:306
  23.8 6.0 %collective-permute-done.4.refs_4_.refs_2_ = bf16[2,64,1024]{2,1,0:T(8,128)(2,1)S(1)} collective-permute-done((bf16[2,64,1024]{2,1,0:T(8,128)(2,1)S(1)}, bf16[2,64,1024]{2,1,0:T(8,128)(2,1)S(1)}, u32[]{:S(2)}, u32[]{:S(2)}) %collective-permute-start.4) | collective-permute-done | bytes 262176 | tf_op jit(solution)/shard_map/ppermute | solution.py:306
  29.8 0.6 collective-permute-start.9
  30.4 3.4 %collective-permute-start.6 = (bf16[2,64,1024]{2,1,0:T(8,128)(2,1)S(1)}, bf16[2,64,1024]{2,1,0:T(8,128)(2,1)S(1)}, u32[]{:S(2)}, u32[]{:S(2)}) collective-permute-start(bf16[2,64,1024]{2,1,0:T(8,128)(2,1)S(1)} %regroup.3.refs_0_), channel_id=1, source_target_pairs={{0,4},{1,17},{2,6},{3,19},{4,0},{5,21},{6,2},{7,23},{8,12},{9,25},... | collective-permute-start | bytes 786440 | tf_op jit(solution)/shard_map/ppermute | solution.py:306
  33.9 0.0 collective-permute-start.5
  33.9 0.0 collective-permute-done.10.refs_4_
  33.9 0.0 collective-permute-start.12
  33.9 4.5 %collective-permute-done.9.refs_3_ = bf16[2,64,1024]{2,1,0:T(8,128)(2,1)S(1)} collective-permute-done((bf16[2,64,1024]{2,1,0:T(8,128)(2,1)S(1)}, bf16[2,64,1024]{2,1,0:T(8,128)(2,1)S(1)}, u32[]{:S(2)}, u32[]{:S(2)}) %collective-permute-start.9) | collective-permute-done | bytes 262176 | tf_op jit(solution)/shard_map/ppermute | solution.py:306
  38.4 0.5 collective-permute-start.14
  38.9 2.3 %collective-permute-done.6.refs_8_.refs_2_ = bf16[2,64,1024]{2,1,0:T(8,128)(2,1)S(1)} collective-permute-done((bf16[2,64,1024]{2,1,0:T(8,128)(2,1)S(1)}, bf16[2,64,1024]{2,1,0:T(8,128)(2,1)S(1)}, u32[]{:S(2)}, u32[]{:S(2)}) %collective-permute-start.6) | collective-permute-done | bytes 262176 | tf_op jit(solution)/shard_map/ppermute | solution.py:306
  41.2 0.0 collective-permute-start.16
  41.2 0.6 %collective-permute-done.5.refs_1_ = bf16[2,64,1024]{2,1,0:T(8,128)(2,1)S(1)} collective-permute-done((bf16[2,64,1024]{2,1,0:T(8,128)(2,1)S(1)}, bf16[2,64,1024]{2,1,0:T(8,128)(2,1)S(1)}, u32[]{:S(2)}, u32[]{:S(2)}) %collective-permute-start.5) | collective-permute-done | bytes 262176 | tf_op jit(solution)/shard_map/ppermute | solution.py:306
  41.8 1.3 %collective-permute-start.7 = (bf16[2,64,1024]{2,1,0:T(8,128)(2,1)S(1)}, bf16[2,64,1024]{2,1,0:T(8,128)(2,1)S(1)}, u32[]{:S(2)}, u32[]{:S(2)}) collective-permute-start(bf16[2,64,1024]{2,1,0:T(8,128)(2,1)S(1)} %collective-permute-done.6.refs_8_.refs_2_), channel_id=1, source_target_pairs={{0,2},{1,9},{2,0},{3,11},{4,6},{5,13},{6,4},{7,15},{8,10},{9,1},{1... | collective-permute-start | bytes 786440 | tf_op jit(solution)/shard_map/ppermute | solution.py:306
  43.1 6.8 %products.2 = (bf16[16,2,1024,512]{3,2,1,0:T(8,128)(2,1)}, f32[8,128]{1,0:T(8,128)S(1)}) custom-call(bf16[2,64,1024]{2,1,0:T(8,128)(2,1)S(1)} %regroup.2.refs_0_, bf16[2,64,1024]{2,1,0:T(8,128)(2,1)S(1)} %collective-permute-done.8.refs_1_, bf16[2,64,1024]{2,1,0:T(8,128)(2,1)S(1)} %collective-permute-done.4.refs_4_.refs_2_, ...), custom_call_target="tpu_custom_call" | custom-call | flops 4294967296 | bytes 16777216 | tf_op jit(solution)/shard_map/products/pallas_call | solution.py:268
  49.9 0.0 collective-permute-done.7.value
  50.0 0.5 collective-permute-start.17
  50.5 0.0 collective-permute-done.14.refs_4_
  50.5 0.0 collective-permute-done.16.refs_6_
  50.5 1.1 %collective-permute-done.17.refs_7_ = bf16[2,64,1024]{2,1,0:T(8,128)(2,1)S(1)} collective-permute-done((bf16[2,64,1024]{2,1,0:T(8,128)(2,1)S(1)}, bf16[2,64,1024]{2,1,0:T(8,128)(2,1)S(1)}, u32[]{:S(2)}, u32[]{:S(2)}) %collective-permute-start.17) | collective-permute-done | bytes 262176 | tf_op jit(solution)/shard_map/ppermute | solution.py:306
  51.7 7.4 %products.3 = (bf16[16,2,1024,512]{3,2,1,0:T(8,128)(2,1)}, f32[8,128]{1,0:T(8,128)}) custom-call(bf16[2,64,1024]{2,1,0:T(8,128)(2,1)S(1)} %regroup.3.refs_0_, bf16[2,64,1024]{2,1,0:T(8,128)(2,1)S(1)} %collective-permute-done.5.refs_1_, bf16[2,64,1024]{2,1,0:T(8,128)(2,1)S(1)} %collective-permute-done.6.refs_8_.refs_2_, ...), custom_call_target="tpu_custom_call", output_to_operand_aliasing={{0}: (8, {})} | custom-call | flops 4294967296 | bytes 16777216 | tf_op jit(solution)/shard_map/products/pallas_call | solution.py:268
  (13 shorter events, 0.1 us)
Async XLA Ops:
  6.3 1.9 %collective-permute-start = (bf16[4,32,1024]{2,1,0:T(8,128)(2,1)}, bf16[4,32,1024]{2,1,0:T(8,128)(2,1)S(1)}, u32[]{:S(2)}, u32[]{:S(2)}) collective-permute-start(bf16[4,32,1024]{2,1,0:T(8,128)(2,1)} %spectra.1.own), channel_id=1, source_target_pairs={{0,1},{1,0},{2,3},{3,2},{4,5},{5,4},{6,7},{7,6},{8,9},{9,8},{10,11... | collective-permute-start | bytes 786440 | tf_op jit(solution)/shard_map/ppermute | solution.py:306
  8.2 0.9 %copy-start = (bf16[4,32,1024]{2,1,0:T(8,128)(2,1)S(1)}, bf16[4,32,1024]{2,1,0:T(8,128)(2,1)}, u32[]{:S(2)}) copy-start(bf16[4,32,1024]{2,1,0:T(8,128)(2,1)} %spectra.1.own) | copy-start | bytes 786436
  9.3 5.9 %collective-permute-start.1 = (bf16[64,1024]{1,0:T(8,128)(2,1)S(1)}, bf16[64,1024]{1,0:T(8,128)(2,1)S(1)}, u32[]{:S(2)}, u32[]{:S(2)}) collective-permute-start(bf16[64,1024]{1,0:T(8,128)(2,1)S(1)} %get-tuple-element.13), channel_id=1, source_target_pairs={{0,8},{1,3},{2,10},{3,1},{4,12},{5,7},{6,14},{7,5},{8,0},{9,11},{1... | collective-permute-start | bytes 393224 | tf_op jit(solution)/shard_map/ppermute | solution.py:306
  12.2 5.0 %collective-permute-start.2 = (bf16[64,1024]{1,0:T(8,128)(2,1)S(1)}, bf16[64,1024]{1,0:T(8,128)(2,1)S(1)}, u32[]{:S(2)}, u32[]{:S(2)}) collective-permute-start(bf16[64,1024]{1,0:T(8,128)(2,1)S(1)} %get-tuple-element.14), channel_id=1, source_target_pairs={{0,16},{1,5},{2,18},{3,7},{4,20},{5,1},{6,22},{7,3},{8,24},{9,13},... | collective-permute-start | bytes 393224 | tf_op jit(solution)/shard_map/ppermute | solution.py:306
  13.7 5.9 %collective-permute-start.3 = (bf16[64,1024]{1,0:T(8,128)(2,1)S(1)}, bf16[64,1024]{1,0:T(8,128)(2,1)S(1)}, u32[]{:S(2)}, u32[]{:S(2)}) collective-permute-start(bf16[64,1024]{1,0:T(8,128)(2,1)S(1)} %get-tuple-element.15), channel_id=1, source_target_pairs={{0,24},{1,7},{2,26},{3,5},{4,28},{5,3},{6,30},{7,1},{8,16},{9,15},... | collective-permute-start | bytes 393224 | tf_op jit(solution)/shard_map/ppermute | solution.py:306
  19.6 10.3 %collective-permute-start.4 = (bf16[2,64,1024]{2,1,0:T(8,128)(2,1)S(1)}, bf16[2,64,1024]{2,1,0:T(8,128)(2,1)S(1)}, u32[]{:S(2)}, u32[]{:S(2)}) collective-permute-start(bf16[2,64,1024]{2,1,0:T(8,128)(2,1)S(1)} %regroup.2.refs_0_), channel_id=1, source_target_pairs={{0,4},{1,17},{2,6},{3,19},{4,0},{5,21},{6,2},{7,23},{8,12},{9,25},... | collective-permute-start | bytes 786440 | tf_op jit(solution)/shard_map/ppermute | solution.py:306
  22.2 8.2 %collective-permute-start.8 = (bf16[2,64,1024]{2,1,0:T(8,128)(2,1)S(1)}, bf16[2,64,1024]{2,1,0:T(8,128)(2,1)S(1)}, u32[]{:S(2)}, u32[]{:S(2)}) collective-permute-start(bf16[2,64,1024]{2,1,0:T(8,128)(2,1)S(1)} %regroup.2.refs_0_), channel_id=1, source_target_pairs={{0,2},{1,9},{2,0},{3,11},{4,6},{5,13},{6,4},{7,15},{8,10},{9,1},{1... | collective-permute-start | bytes 786440 | tf_op jit(solution)/shard_map/ppermute | solution.py:306
  23.8 10.1 %collective-permute-start.10 = (bf16[2,64,1024]{2,1,0:T(8,128)(2,1)S(1)}, bf16[2,64,1024]{2,1,0:T(8,128)(2,1)S(1)}, u32[]{:S(2)}, u32[]{:S(2)}) collective-permute-start(bf16[2,64,1024]{2,1,0:T(8,128)(2,1)S(1)} %regroup.2.refs_0_), channel_id=1, source_target_pairs={{0,1},{1,0},{2,3},{3,2},{4,5},{5,4},{6,7},{7,6},{8,9},{9,8},{10,11... | collective-permute-start | bytes 786440 | tf_op jit(solution)/shard_map/ppermute | solution.py:306
  29.8 8.6 %collective-permute-start.9 = (bf16[2,64,1024]{2,1,0:T(8,128)(2,1)S(1)}, bf16[2,64,1024]{2,1,0:T(8,128)(2,1)S(1)}, u32[]{:S(2)}, u32[]{:S(2)}) collective-permute-start(bf16[2,64,1024]{2,1,0:T(8,128)(2,1)S(1)} %collective-permute-done.4.refs_4_.refs_2_), channel_id=1, source_target_pairs={{0,2},{1,9},{2,0},{3,11},{4,6},{5,13},{6,4},{7,15},{8,10},{9,1},{1... | collective-permute-start | bytes 786440 | tf_op jit(solution)/shard_map/ppermute | solution.py:306
  30.4 8.0 %collective-permute-start.11 = (bf16[2,64,1024]{2,1,0:T(8,128)(2,1)S(1)}, bf16[2,64,1024]{2,1,0:T(8,128)(2,1)S(1)}, u32[]{:S(2)}, u32[]{:S(2)}) collective-permute-start(bf16[2,64,1024]{2,1,0:T(8,128)(2,1)S(1)} %collective-permute-done.8.refs_1_), channel_id=1, source_target_pairs={{0,1},{1,0},{2,3},{3,2},{4,5},{5,4},{6,7},{7,6},{8,9},{9,8},{10,11... | collective-permute-start | bytes 786440 | tf_op jit(solution)/shard_map/ppermute | solution.py:306
  30.4 10.8 %collective-permute-start.6 = (bf16[2,64,1024]{2,1,0:T(8,128)(2,1)S(1)}, bf16[2,64,1024]{2,1,0:T(8,128)(2,1)S(1)}, u32[]{:S(2)}, u32[]{:S(2)}) collective-permute-start(bf16[2,64,1024]{2,1,0:T(8,128)(2,1)S(1)} %regroup.3.refs_0_), channel_id=1, source_target_pairs={{0,4},{1,17},{2,6},{3,19},{4,0},{5,21},{6,2},{7,23},{8,12},{9,25},... | collective-permute-start | bytes 786440 | tf_op jit(solution)/shard_map/ppermute | solution.py:306
  33.9 7.9 %collective-permute-start.5 = (bf16[2,64,1024]{2,1,0:T(8,128)(2,1)S(1)}, bf16[2,64,1024]{2,1,0:T(8,128)(2,1)S(1)}, u32[]{:S(2)}, u32[]{:S(2)}) collective-permute-start(bf16[2,64,1024]{2,1,0:T(8,128)(2,1)S(1)} %regroup.3.refs_0_), channel_id=1, source_target_pairs={{0,2},{1,9},{2,0},{3,11},{4,6},{5,13},{6,4},{7,15},{8,10},{9,1},{1... | collective-permute-start | bytes 786440 | tf_op jit(solution)/shard_map/ppermute | solution.py:306
  33.9 9.2 %collective-permute-start.12 = (bf16[2,64,1024]{2,1,0:T(8,128)(2,1)S(1)}, bf16[2,64,1024]{2,1,0:T(8,128)(2,1)S(1)}, u32[]{:S(2)}, u32[]{:S(2)}) collective-permute-start(bf16[2,64,1024]{2,1,0:T(8,128)(2,1)S(1)} %collective-permute-done.4.refs_4_.refs_2_), channel_id=1, source_target_pairs={{0,1},{1,0},{2,3},{3,2},{4,5},{5,4},{6,7},{7,6},{8,9},{9,8},{10,11... | collective-permute-start | bytes 786440 | tf_op jit(solution)/shard_map/ppermute | solution.py:306
  38.4 4.7 %collective-permute-start.13 = (bf16[2,64,1024]{2,1,0:T(8,128)(2,1)S(1)}, bf16[2,64,1024]{2,1,0:T(8,128)(2,1)S(1)}, u32[]{:S(2)}, u32[]{:S(2)}) collective-permute-start(bf16[2,64,1024]{2,1,0:T(8,128)(2,1)S(1)} %collective-permute-done.9.refs_3_), channel_id=1, source_target_pairs={{0,1},{1,0},{2,3},{3,2},{4,5},{5,4},{6,7},{7,6},{8,9},{9,8},{10,11... | collective-permute-start | bytes 786440 | tf_op jit(solution)/shard_map/ppermute | solution.py:306
  38.4 12.1 %collective-permute-start.14 = (bf16[2,64,1024]{2,1,0:T(8,128)(2,1)S(1)}, bf16[2,64,1024]{2,1,0:T(8,128)(2,1)S(1)}, u32[]{:S(2)}, u32[]{:S(2)}) collective-permute-start(bf16[2,64,1024]{2,1,0:T(8,128)(2,1)S(1)} %regroup.3.refs_0_), channel_id=1, source_target_pairs={{0,1},{1,0},{2,3},{3,2},{4,5},{5,4},{6,7},{7,6},{8,9},{9,8},{10,11... | collective-permute-start | bytes 786440 | tf_op jit(solution)/shard_map/ppermute | solution.py:306
  41.2 9.3 %collective-permute-start.16 = (bf16[2,64,1024]{2,1,0:T(8,128)(2,1)S(1)}, bf16[2,64,1024]{2,1,0:T(8,128)(2,1)S(1)}, u32[]{:S(2)}, u32[]{:S(2)}) collective-permute-start(bf16[2,64,1024]{2,1,0:T(8,128)(2,1)S(1)} %collective-permute-done.6.refs_8_.refs_2_), channel_id=1, source_target_pairs={{0,1},{1,0},{2,3},{3,2},{4,5},{5,4},{6,7},{7,6},{8,9},{9,8},{10,11... | collective-permute-start | bytes 786440 | tf_op jit(solution)/shard_map/ppermute | solution.py:306
  41.8 8.1 %collective-permute-start.7 = (bf16[2,64,1024]{2,1,0:T(8,128)(2,1)S(1)}, bf16[2,64,1024]{2,1,0:T(8,128)(2,1)S(1)}, u32[]{:S(2)}, u32[]{:S(2)}) collective-permute-start(bf16[2,64,1024]{2,1,0:T(8,128)(2,1)S(1)} %collective-permute-done.6.refs_8_.refs_2_), channel_id=1, source_target_pairs={{0,2},{1,9},{2,0},{3,11},{4,6},{5,13},{6,4},{7,15},{8,10},{9,1},{1... | collective-permute-start | bytes 786440 | tf_op jit(solution)/shard_map/ppermute | solution.py:306
  43.1 7.4 %collective-permute-start.15 = (bf16[2,64,1024]{2,1,0:T(8,128)(2,1)S(1)}, bf16[2,64,1024]{2,1,0:T(8,128)(2,1)S(1)}, u32[]{:S(2)}, u32[]{:S(2)}) collective-permute-start(bf16[2,64,1024]{2,1,0:T(8,128)(2,1)S(1)} %collective-permute-done.5.refs_1_), channel_id=1, source_target_pairs={{0,1},{1,0},{2,3},{3,2},{4,5},{5,4},{6,7},{7,6},{8,9},{9,8},{10,11... | collective-permute-start | bytes 786440 | tf_op jit(solution)/shard_map/ppermute | solution.py:306
  50.0 1.7 %collective-permute-start.17 = (bf16[2,64,1024]{2,1,0:T(8,128)(2,1)S(1)}, bf16[2,64,1024]{2,1,0:T(8,128)(2,1)S(1)}, u32[]{:S(2)}, u32[]{:S(2)}) collective-permute-start(bf16[2,64,1024]{2,1,0:T(8,128)(2,1)S(1)} %hold.1.refs_3_), channel_id=1, source_target_pairs={{0,1},{1,0},{2,3},{3,2},{4,5},{5,4},{6,7},{7,6},{8,9},{9,8},{10,11... | collective-permute-start | bytes 786440 | tf_op jit(solution)/shard_map/ppermute | solution.py:306

commit v3 on v2

--- a/solution.py
+++ b/solution.py
@@ -18,8 +18,8 @@
 CHUNKS = F // CHUNK
 GROUP = 2 * CHUNK
 ROWS = 2 * F
-CALLS = 2
 WINDOW_GROUP = 2 * GROUP
+GATES = {0: [1], 1: [1]}
 
 AXES = ("row", "col")
 BF16 = jnp.bfloat16
@@ -166,31 +166,25 @@
     )(own, other)
 
 
-def regroup_body(call, count, *refs):
-    out = refs[-1]
-    for chunk in range(out.shape[0]):
-        start = (call * out.shape[0] + chunk) * WINDOW_GROUP
-        for step in range(count):
-            out[chunk, step * WINDOW_GROUP : (step + 1) * WINDOW_GROUP] = refs[step][
-                start : start + WINDOW_GROUP
-            ]
-
-
-def regroup(call, pieces, after):
-    count, width = len(pieces), pieces[0].shape[1]
+def pack_body(*refs):
+    for index, ref in enumerate(refs[:-1]):
+        refs[-1][index] = ref[...]
+
+
+def pack(values):
     vmem = pl.BlockSpec(memory_space=pltpu.VMEM)
     return pl.pallas_call(
-        functools.partial(regroup_body, call, count),
-        out_shape=jax.ShapeDtypeStruct((CHUNKS // CALLS, count * WINDOW_GROUP, width), BF16),
-        in_specs=[vmem] * (count + len(after)),
+        pack_body,
+        out_shape=jax.ShapeDtypeStruct((len(values), *values[0].shape), BF16),
+        in_specs=[vmem] * len(values),
         out_specs=vmem,
         compiler_params=pltpu.CompilerParams(vmem_limit_bytes=8 * 2**20),
-        name="regroup",
-    )(*pieces, *after)
-
-
-def hold_body(value, after, out):
-    out[...] = value[...]
+        name="pack",
+    )(*values)
+
+
+def hold_body(value, *refs):
+    refs[-1][...] = value[...]
 
 
 def hold(value, after):
@@ -198,16 +192,16 @@
     return pl.pallas_call(
         hold_body,
         out_shape=jax.ShapeDtypeStruct(value.shape, value.dtype),
-        in_specs=[vmem, vmem],
+        in_specs=[vmem] * (1 + len(after)),
         out_specs=vmem,
         compiler_params=pltpu.CompilerParams(vmem_limit_bytes=8 * 2**20),
         name="hold",
-    )(value, after)
-
-
-def product_body(count, first, windows, *refs):
+    )(value, *after)
+
+
+def product_body(count, windows, *refs):
     held, swapped = refs[:count], refs[count : 2 * count]
-    out, finished, turned, right, tiles, stored = refs[-6:]
+    out, turned, right, tiles, stored = refs[2 * count :]
     depth, double = right.shape
     width = double // 2
     chunks = pl.num_programs(0)
@@ -215,13 +209,12 @@
     core = lax.rem(lax.axis_index("col"), 2)
 
     def prepare(rows_of, cols_of, start):
-        turned[...] = jnp.concatenate([ref[chunk] for ref in rows_of], axis=0).T
-        pieces = [
-            ref[chunk, group * WINDOW_GROUP : (group + 1) * WINDOW_GROUP, start : start + width]
-            for group in range(count)
-            for ref in cols_of
-        ]
-        straight = jnp.concatenate(pieces, axis=0).astype(F32)
+        unit = pl.ds(pl.multiple_of(chunk * WINDOW_GROUP, WINDOW_GROUP), WINDOW_GROUP)
+        lefts = [ref[line, unit] for line in range(count) for ref in rows_of]
+        turned[...] = jnp.concatenate(lefts, axis=0).T
+        columns = slice(start, start + width)
+        rights = [ref[plane, unit, columns] for ref in cols_of for plane in range(count)]
+        straight = jnp.concatenate(rights, axis=0).astype(F32)
         shaped = straight.reshape(depth // GROUP, 2, CHUNK, width)
         crossed = jnp.stack([shaped[:, 1], -shaped[:, 0]], axis=1).reshape(depth, width)
         right[:, :width] = straight
@@ -232,7 +225,7 @@
 
     def store(bin_index, part):
         return pltpu.make_async_copy(
-            tiles.at[bin_index, part], out.at[first + bin_index, part], stored.at[bin_index, part]
+            tiles.at[bin_index, part], out.at[bin_index, part], stored.at[bin_index, part]
         )
 
     row = lax.broadcasted_iota(jnp.int32, (depth, double), 0)
@@ -249,46 +242,33 @@
         for bin_index in range(tiles.shape[0]):
             for part in range(2):
                 store(bin_index, part).wait()
-        finished[...] = jnp.zeros_like(finished)
-
-
-def multiply(call, held, swapped, windows, result, after):
+
+
+def multiply(held, swapped, windows):
     count = len(held)
-    per_call, rows, height = held[0].shape
-    depth, width = rows * count, height // 2
-    steps = per_call * CHUNK
+    height = held[0].shape[2]
+    depth, width = count * count * WINDOW_GROUP, height // 2
     vmem = pl.BlockSpec(memory_space=pltpu.VMEM)
-    operands = [*held, *swapped, *after]
-    in_specs = [vmem] * len(operands)
-    aliases = {}
-    if result is not None:
-        aliases = {len(operands): 0}
-        in_specs.append(pl.BlockSpec(memory_space=pl.ANY))
-        operands.append(result)
-    return pl.pallas_call(
-        functools.partial(product_body, count, call * steps, windows),
-        out_shape=[
-            jax.ShapeDtypeStruct((F, 2, height, width), BF16),
-            jax.ShapeDtypeStruct((8, LANES), F32),
-        ],
-        grid=(per_call,),
-        in_specs=in_specs,
-        out_specs=[pl.BlockSpec(memory_space=pl.ANY), vmem],
+    return pl.pallas_call(
+        functools.partial(product_body, count, windows),
+        out_shape=jax.ShapeDtypeStruct((F, 2, height, width), BF16),
+        grid=(CHUNKS,),
+        in_specs=[vmem] * (2 * count),
+        out_specs=pl.BlockSpec(memory_space=pl.ANY),
         scratch_shapes=[
             pltpu.VMEM((height, depth), BF16),
             pltpu.VMEM((depth, 2 * width), F32),
-            pltpu.VMEM((steps, 2, height, width), BF16),
-            pltpu.SemaphoreType.DMA((steps, 2)),
+            pltpu.VMEM((F, 2, height, width), BF16),
+            pltpu.SemaphoreType.DMA((F, 2)),
         ],
-        input_output_aliases=aliases,
-        compiler_params=pltpu.CompilerParams(vmem_limit_bytes=32 * 2**20),
+        compiler_params=pltpu.CompilerParams(vmem_limit_bytes=40 * 2**20),
         cost_estimate=pl.CostEstimate(
-            flops=steps * 4 * height * width * depth,
-            bytes_accessed=steps * 2 * height * width * 2,
+            flops=F * 4 * height * width * depth,
+            bytes_accessed=F * 2 * height * width * 2,
             transcendentals=0,
         ),
         name="products",
-    )(*operands)
+    )(*held, *swapped)
 
 
 def on_device(record, fir_taps, bins, offsets):
@@ -309,31 +289,24 @@
         return send(value, (0, 0), (0, 0), 1)
 
     own = make_spectra(record, fir_taps, bins, offsets, row_count)
-    to_send = pair_windows(own, swap(own))
+    to_send = pair_windows(hold(own, []), swap(own))
     pieces = [to_send[0]]
     for step in range(1, row_count):
         pieces.append(send(to_send[step], (step, 0), (0, step), 0))
 
     bits = [row_count >> shift for shift in range(1, row_count.bit_length())]
-    gathered, after = [], []
-    for call in range(CALLS):
-        held = {0: regroup(call, pieces, after)}
+    units, early = [], []
+    for step, piece in enumerate(pieces):
+        if step == row_count - 1:
+            piece = hold(piece, early)
+        held = {0: piece}
         for bit in bits:
             for slot in list(held):
                 held[slot ^ bit] = send(held[slot], (0, bit), (bit, 0), 0)
-        after = [held[bits[0]]]
-        gathered.append(held)
-
-    result, finished = None, None
-    for call, held in enumerate(gathered):
-        ordered = [held[slot] for slot in range(row_count)]
-        last = row_count - 1
-        if result is not None:
-            ordered[last] = hold(ordered[last], finished)
-        after = [gathered[call + 1][bits[0]]] if call + 1 < CALLS else []
-        swapped = [swap(value) for value in ordered]
-        result, finished = multiply(call, ordered, swapped, windows, result, after)
-    return result
+        if step in GATES:
+            early += [held[bit] for bit in GATES[step]]
+        units.append(pack([held[slot] for slot in range(row_count)]))
+    return multiply(units, [swap(unit) for unit in units], windows)
 
 
 def solution(mesh):

time: 59.2 us -> 52.9 us (0.89)
  waiting for transfers between devices: 21.8 us -> 12 us
  starting transfers between devices: 15.6 us -> 20.7 us
  Pallas kernels: 20 us -> 18.3 us
    ppermute x18 -> x20, waiting for transfers between devices: 21.8 us -> 12 us  [send(): return lax.ppermute(value, AXES, pairs)]
    ppermute x18 -> x20, starting transfers between devices: 15.6 us -> 20.7 us  [send(): return lax.ppermute(value, AXES, pairs)]
    pallas_call x4 -> x5, Pallas kernels: 14.2 us -> 12.6 us  [the longest x1 12.4 us: multiply(): pl.pallas_call(functools.partial(product_body, count, windows), out_shape...]
  transfers between devices with their start and end apart: 18 -> 20, of which waited for: 9 -> 13; matrix products, arithmetic and copies ran while one was open for 0% -> 0% of each run, Pallas kernels for 12% -> 0%
where the time goes in v3:
time: 52.9 us; the launch traced here: 52.7 us
  starting transfers between devices  20.7 us (39%)
  Pallas kernels  18.3 us (35%)
  waiting for transfers between devices  12 us (23%)
  local copies, waits for them, and re-layouts  0.95 us (2%)
  between operations  0.75 us (1%)
    ppermute x20, starting transfers between devices, send(): return lax.ppermute(value, AXES, pairs)  20.7 us
    pallas_call x1, Pallas kernels, multiply(): pl.pallas_call(functools.partial(product_body, count, windows), out_shape...  12.4 us
    ppermute x20, waiting for transfers between devices, send(): return lax.ppermute(value, AXES, pairs)  12 us
    pallas_call x1, Pallas kernels, make_spectra(): pl.pallas_call(spectra_body, out_shape=jax.ShapeDtypeStruct((slices, ROWS...  5.66 us
  transfers between devices with their start and end apart: 20, of which 13 were waited for; matrix products, arithmetic and copies ran while one was open for 0% of the time, Pallas kernels for 0%

profile of v3, /device:TPU:0, one launch (start us, length us, event | category | flops | bytes accessed | tf_op | source)
XLA Modules:
  0.0 52.7 jit_solution(17799070216126948626)
XLA Ops:
  0.7 5.7 %spectra.1.value = bf16[4,32,1024]{2,1,0:T(8,128)(2,1)} custom-call(f32[101]{0:T(128)} %fir_taps.1, s32[16]{0:T(128)} %bins.1, s32[1]{0:T(128)S(6)} %copy.5.offsets, bf16[1408,4096]{1,0:T(8,128)(2,1)} %record.1), custom_call_target="tpu_custom_call" | custom-call | tf_op jit(solution)/shard_map/spectra/pallas_call | solution.py:119
  6.3 0.5 collective-permute-start
  6.8 0.9 %copy-done = bf16[4,32,1024]{2,1,0:T(8,128)(2,1)S(1)} copy-done((bf16[4,32,1024]{2,1,0:T(8,128)(2,1)S(1)}, bf16[4,32,1024]{2,1,0:T(8,128)(2,1)}, u32[]{:S(2)}) %copy-start) | copy-done | bytes 262168
  7.8 0.4 collective-permute-done.other
  8.2 0.1 pair_windows.1
  8.3 2.9 %collective-permute-start.4 = (bf16[64,1024]{1,0:T(8,128)(2,1)S(1)}, bf16[64,1024]{1,0:T(8,128)(2,1)S(1)}, u32[]{:S(2)}, u32[]{:S(2)}) collective-permute-start(bf16[64,1024]{1,0:T(8,128)(2,1)S(1)} %get-tuple-element.10), channel_id=1, source_target_pairs={{0,8},{1,3},{2,10},{3,1},{4,12},{5,7},{6,14},{7,5},{8,0},{9,11},{1... | collective-permute-start | bytes 393224 | tf_op jit(solution)/shard_map/ppermute | solution.py:286
  11.2 1.5 %collective-permute-start.8 = (bf16[64,1024]{1,0:T(8,128)(2,1)S(1)}, bf16[64,1024]{1,0:T(8,128)(2,1)S(1)}, u32[]{:S(2)}, u32[]{:S(2)}) collective-permute-start(bf16[64,1024]{1,0:T(8,128)(2,1)S(1)} %get-tuple-element.11), channel_id=1, source_target_pairs={{0,16},{1,5},{2,18},{3,7},{4,20},{5,1},{6,22},{7,3},{8,24},{9,13},... | collective-permute-start | bytes 393224 | tf_op jit(solution)/shard_map/ppermute | solution.py:286
  12.8 3.0 %collective-permute-start.2 = (bf16[64,1024]{1,0:T(8,128)(2,1)S(1)}, bf16[64,1024]{1,0:T(8,128)(2,1)S(1)}, u32[]{:S(2)}, u32[]{:S(2)}) collective-permute-start(bf16[64,1024]{1,0:T(8,128)(2,1)S(1)} %get-tuple-element.9.refs_0_), channel_id=1, source_target_pairs={{0,4},{1,17},{2,6},{3,19},{4,0},{5,21},{6,2},{7,23},{8,12},{9,25},... | collective-permute-start | bytes 393224 | tf_op jit(solution)/shard_map/ppermute | solution.py:286
  15.8 1.6 %collective-permute-start.1 = (bf16[64,1024]{1,0:T(8,128)(2,1)S(1)}, bf16[64,1024]{1,0:T(8,128)(2,1)S(1)}, u32[]{:S(2)}, u32[]{:S(2)}) collective-permute-start(bf16[64,1024]{1,0:T(8,128)(2,1)S(1)} %get-tuple-element.9.refs_0_), channel_id=1, source_target_pairs={{0,2},{1,9},{2,0},{3,11},{4,6},{5,13},{6,4},{7,15},{8,10},{9,1},{1... | collective-permute-start | bytes 393224 | tf_op jit(solution)/shard_map/ppermute | solution.py:286
  17.4 0.5 collective-permute-start.5
  17.8 2.0 %collective-permute-start.10 = (bf16[64,1024]{1,0:T(8,128)(2,1)S(1)}, bf16[64,1024]{1,0:T(8,128)(2,1)S(1)}, u32[]{:S(2)}, u32[]{:S(2)}) collective-permute-start(bf16[64,1024]{1,0:T(8,128)(2,1)S(1)} %collective-permute-done.8.refs_0_), channel_id=1, source_target_pairs={{0,4},{1,17},{2,6},{3,19},{4,0},{5,21},{6,2},{7,23},{8,12},{9,25},... | collective-permute-start | bytes 393224 | tf_op jit(solution)/shard_map/ppermute | solution.py:286
  19.9 0.1 collective-permute-done.12.value
  20.0 2.6 %collective-permute-start.6 = (bf16[64,1024]{1,0:T(8,128)(2,1)S(1)}, bf16[64,1024]{1,0:T(8,128)(2,1)S(1)}, u32[]{:S(2)}, u32[]{:S(2)}) collective-permute-start(bf16[64,1024]{1,0:T(8,128)(2,1)S(1)} %collective-permute-done.4.refs_0_), channel_id=1, source_target_pairs={{0,4},{1,17},{2,6},{3,19},{4,0},{5,21},{6,2},{7,23},{8,12},{9,25},... | collective-permute-start | bytes 393224 | tf_op jit(solution)/shard_map/ppermute | solution.py:286
  22.6 0.5 collective-permute-done.2.refs_2_
  23.1 1.1 %collective-permute-start.3 = (bf16[64,1024]{1,0:T(8,128)(2,1)S(1)}, bf16[64,1024]{1,0:T(8,128)(2,1)S(1)}, u32[]{:S(2)}, u32[]{:S(2)}) collective-permute-start(bf16[64,1024]{1,0:T(8,128)(2,1)S(1)} %collective-permute-done.2.refs_2_), channel_id=1, source_target_pairs={{0,2},{1,9},{2,0},{3,11},{4,6},{5,13},{6,4},{7,15},{8,10},{9,1},{1... | collective-permute-start | bytes 393224 | tf_op jit(solution)/shard_map/ppermute | solution.py:286
  24.2 1.9 %collective-permute-start.14 = (bf16[64,1024]{1,0:T(8,128)(2,1)S(1)}, bf16[64,1024]{1,0:T(8,128)(2,1)S(1)}, u32[]{:S(2)}, u32[]{:S(2)}) collective-permute-start(bf16[64,1024]{1,0:T(8,128)(2,1)S(1)} %hold.3.refs_0_), channel_id=1, source_target_pairs={{0,4},{1,17},{2,6},{3,19},{4,0},{5,21},{6,2},{7,23},{8,12},{9,25},... | collective-permute-start | bytes 393224 | tf_op jit(solution)/shard_map/ppermute | solution.py:286
  26.1 0.2 collective-permute-start.9
  26.4 1.0 %collective-permute-done.10.refs_2_ = bf16[64,1024]{1,0:T(8,128)(2,1)S(1)} collective-permute-done((bf16[64,1024]{1,0:T(8,128)(2,1)S(1)}, bf16[64,1024]{1,0:T(8,128)(2,1)S(1)}, u32[]{:S(2)}, u32[]{:S(2)}) %collective-permute-start.10) | collective-permute-done | bytes 131104 | tf_op jit(solution)/shard_map/ppermute | solution.py:286
  27.4 0.7 %collective-permute-start.11 = (bf16[64,1024]{1,0:T(8,128)(2,1)S(1)}, bf16[64,1024]{1,0:T(8,128)(2,1)S(1)}, u32[]{:S(2)}, u32[]{:S(2)}) collective-permute-start(bf16[64,1024]{1,0:T(8,128)(2,1)S(1)} %collective-permute-done.10.refs_2_), channel_id=1, source_target_pairs={{0,2},{1,9},{2,0},{3,11},{4,6},{5,13},{6,4},{7,15},{8,10},{9,1},{1... | collective-permute-start | bytes 393224 | tf_op jit(solution)/shard_map/ppermute | solution.py:286
  28.1 0.7 %collective-permute-done.6.refs_2_ = bf16[64,1024]{1,0:T(8,128)(2,1)S(1)} collective-permute-done((bf16[64,1024]{1,0:T(8,128)(2,1)S(1)}, bf16[64,1024]{1,0:T(8,128)(2,1)S(1)}, u32[]{:S(2)}, u32[]{:S(2)}) %collective-permute-start.6) | collective-permute-done | bytes 131104 | tf_op jit(solution)/shard_map/ppermute | solution.py:286
  28.8 0.6 %collective-permute-start.7 = (bf16[64,1024]{1,0:T(8,128)(2,1)S(1)}, bf16[64,1024]{1,0:T(8,128)(2,1)S(1)}, u32[]{:S(2)}, u32[]{:S(2)}) collective-permute-start(bf16[64,1024]{1,0:T(8,128)(2,1)S(1)} %collective-permute-done.6.refs_2_), channel_id=1, source_target_pairs={{0,2},{1,9},{2,0},{3,11},{4,6},{5,13},{6,4},{7,15},{8,10},{9,1},{1... | collective-permute-start | bytes 393224 | tf_op jit(solution)/shard_map/ppermute | solution.py:286
  29.4 0.9 %collective-permute-done.3.refs_3_ = bf16[64,1024]{1,0:T(8,128)(2,1)S(1)} collective-permute-done((bf16[64,1024]{1,0:T(8,128)(2,1)S(1)}, bf16[64,1024]{1,0:T(8,128)(2,1)S(1)}, u32[]{:S(2)}, u32[]{:S(2)}) %collective-permute-start.3) | collective-permute-done | bytes 131104 | tf_op jit(solution)/shard_map/ppermute | solution.py:286
  30.3 0.5 collective-permute-start.13
  30.8 0.8 %collective-permute-done.14.refs_2_ = bf16[64,1024]{1,0:T(8,128)(2,1)S(1)} collective-permute-done((bf16[64,1024]{1,0:T(8,128)(2,1)S(1)}, bf16[64,1024]{1,0:T(8,128)(2,1)S(1)}, u32[]{:S(2)}, u32[]{:S(2)}) %collective-permute-start.14) | collective-permute-done | bytes 131104 | tf_op jit(solution)/shard_map/ppermute | solution.py:286
  31.7 0.7 %collective-permute-start.15 = (bf16[64,1024]{1,0:T(8,128)(2,1)S(1)}, bf16[64,1024]{1,0:T(8,128)(2,1)S(1)}, u32[]{:S(2)}, u32[]{:S(2)}) collective-permute-start(bf16[64,1024]{1,0:T(8,128)(2,1)S(1)} %collective-permute-done.14.refs_2_), channel_id=1, source_target_pairs={{0,2},{1,9},{2,0},{3,11},{4,6},{5,13},{6,4},{7,15},{8,10},{9,1},{1... | collective-permute-start | bytes 393224 | tf_op jit(solution)/shard_map/ppermute | solution.py:286
  32.4 0.3 collective-permute-done.9.refs_1_
  32.7 1.4 %collective-permute-done.11.refs_3_ = bf16[64,1024]{1,0:T(8,128)(2,1)S(1)} collective-permute-done((bf16[64,1024]{1,0:T(8,128)(2,1)S(1)}, bf16[64,1024]{1,0:T(8,128)(2,1)S(1)}, u32[]{:S(2)}, u32[]{:S(2)}) %collective-permute-start.11) | collective-permute-done | bytes 131104 | tf_op jit(solution)/shard_map/ppermute | solution.py:286
  34.2 1.3 %collective-permute-done.7.refs_3_ = bf16[64,1024]{1,0:T(8,128)(2,1)S(1)} collective-permute-done((bf16[64,1024]{1,0:T(8,128)(2,1)S(1)}, bf16[64,1024]{1,0:T(8,128)(2,1)S(1)}, u32[]{:S(2)}, u32[]{:S(2)}) %collective-permute-start.7) | collective-permute-done | bytes 131104 | tf_op jit(solution)/shard_map/ppermute | solution.py:286
  35.6 1.3 %collective-permute-done.13.refs_1_ = bf16[64,1024]{1,0:T(8,128)(2,1)S(1)} collective-permute-done((bf16[64,1024]{1,0:T(8,128)(2,1)S(1)}, bf16[64,1024]{1,0:T(8,128)(2,1)S(1)}, u32[]{:S(2)}, u32[]{:S(2)}) %collective-permute-start.13) | collective-permute-done | bytes 131104 | tf_op jit(solution)/shard_map/ppermute | solution.py:286
  36.9 1.4 %collective-permute-done.15.refs_3_ = bf16[64,1024]{1,0:T(8,128)(2,1)S(1)} collective-permute-done((bf16[64,1024]{1,0:T(8,128)(2,1)S(1)}, bf16[64,1024]{1,0:T(8,128)(2,1)S(1)}, u32[]{:S(2)}, u32[]{:S(2)}) %collective-permute-start.15) | collective-permute-done | bytes 131104 | tf_op jit(solution)/shard_map/ppermute | solution.py:286
  38.4 1.9 %collective-permute-done.19.refs_7_ = bf16[4,64,1024]{2,1,0:T(8,128)(2,1)S(1)} collective-permute-done((bf16[4,64,1024]{2,1,0:T(8,128)(2,1)S(1)}, bf16[4,64,1024]{2,1,0:T(8,128)(2,1)S(1)}, u32[]{:S(2)}, u32[]{:S(2)}) %collective-permute-start.19) | collective-permute-done | bytes 524320 | tf_op jit(solution)/shard_map/ppermute | solution.py:286
  40.3 12.4 %products.1 = bf16[16,2,1024,512]{3,2,1,0:T(8,128)(2,1)} custom-call(bf16[4,64,1024]{2,1,0:T(8,128)(2,1)S(1)} %pack.4.refs_0_, bf16[4,64,1024]{2,1,0:T(8,128)(2,1)S(1)} %pack.5.refs_1_, bf16[4,64,1024]{2,1,0:T(8,128)(2,1)S(1)} %pack.6.refs_2_, bf16[4,64,1024]{2,1,0:T(8,128)(2,1)S(1)} %pack.7.refs_3_, ...), custom_call_target="tpu_custom_call" | custom-call | flops 8589934592 | bytes 33554432 | tf_op jit(solution)/shard_map/products/pallas_call | solution.py:252
  (19 shorter events, 0.4 us)
Async XLA Ops:
  6.3 1.9 %collective-permute-start = (bf16[4,32,1024]{2,1,0:T(8,128)(2,1)}, bf16[4,32,1024]{2,1,0:T(8,128)(2,1)S(1)}, u32[]{:S(2)}, u32[]{:S(2)}) collective-permute-start(bf16[4,32,1024]{2,1,0:T(8,128)(2,1)} %spectra.1.value), channel_id=1, source_target_pairs={{0,1},{1,0},{2,3},{3,2},{4,5},{5,4},{6,7},{7,6},{8,9},{9,8},{10,11... | collective-permute-start | bytes 786440 | tf_op jit(solution)/shard_map/ppermute | solution.py:286
  6.8 0.9 %copy-start = (bf16[4,32,1024]{2,1,0:T(8,128)(2,1)S(1)}, bf16[4,32,1024]{2,1,0:T(8,128)(2,1)}, u32[]{:S(2)}) copy-start(bf16[4,32,1024]{2,1,0:T(8,128)(2,1)} %spectra.1.value) | copy-start | bytes 786436
  8.3 9.1 %collective-permute-start.4 = (bf16[64,1024]{1,0:T(8,128)(2,1)S(1)}, bf16[64,1024]{1,0:T(8,128)(2,1)S(1)}, u32[]{:S(2)}, u32[]{:S(2)}) collective-permute-start(bf16[64,1024]{1,0:T(8,128)(2,1)S(1)} %get-tuple-element.10), channel_id=1, source_target_pairs={{0,8},{1,3},{2,10},{3,1},{4,12},{5,7},{6,14},{7,5},{8,0},{9,11},{1... | collective-permute-start | bytes 393224 | tf_op jit(solution)/shard_map/ppermute | solution.py:286
  11.2 6.6 %collective-permute-start.8 = (bf16[64,1024]{1,0:T(8,128)(2,1)S(1)}, bf16[64,1024]{1,0:T(8,128)(2,1)S(1)}, u32[]{:S(2)}, u32[]{:S(2)}) collective-permute-start(bf16[64,1024]{1,0:T(8,128)(2,1)S(1)} %get-tuple-element.11), channel_id=1, source_target_pairs={{0,16},{1,5},{2,18},{3,7},{4,20},{5,1},{6,22},{7,3},{8,24},{9,13},... | collective-permute-start | bytes 393224 | tf_op jit(solution)/shard_map/ppermute | solution.py:286
  12.7 7.2 %collective-permute-start.12 = (bf16[64,1024]{1,0:T(8,128)(2,1)S(1)}, bf16[64,1024]{1,0:T(8,128)(2,1)S(1)}, u32[]{:S(2)}, u32[]{:S(2)}) collective-permute-start(bf16[64,1024]{1,0:T(8,128)(2,1)S(1)} %get-tuple-element.12), channel_id=1, source_target_pairs={{0,24},{1,7},{2,26},{3,5},{4,28},{5,3},{6,30},{7,1},{8,16},{9,15},... | collective-permute-start | bytes 393224 | tf_op jit(solution)/shard_map/ppermute | solution.py:286
  12.8 10.3 %collective-permute-start.2 = (bf16[64,1024]{1,0:T(8,128)(2,1)S(1)}, bf16[64,1024]{1,0:T(8,128)(2,1)S(1)}, u32[]{:S(2)}, u32[]{:S(2)}) collective-permute-start(bf16[64,1024]{1,0:T(8,128)(2,1)S(1)} %get-tuple-element.9.refs_0_), channel_id=1, source_target_pairs={{0,4},{1,17},{2,6},{3,19},{4,0},{5,21},{6,2},{7,23},{8,12},{9,25},... | collective-permute-start | bytes 393224 | tf_op jit(solution)/shard_map/ppermute | solution.py:286
  15.8 8.4 %collective-permute-start.1 = (bf16[64,1024]{1,0:T(8,128)(2,1)S(1)}, bf16[64,1024]{1,0:T(8,128)(2,1)S(1)}, u32[]{:S(2)}, u32[]{:S(2)}) collective-permute-start(bf16[64,1024]{1,0:T(8,128)(2,1)S(1)} %get-tuple-element.9.refs_0_), channel_id=1, source_target_pairs={{0,2},{1,9},{2,0},{3,11},{4,6},{5,13},{6,4},{7,15},{8,10},{9,1},{1... | collective-permute-start | bytes 393224 | tf_op jit(solution)/shard_map/ppermute | solution.py:286
  17.4 6.8 %collective-permute-start.5 = (bf16[64,1024]{1,0:T(8,128)(2,1)S(1)}, bf16[64,1024]{1,0:T(8,128)(2,1)S(1)}, u32[]{:S(2)}, u32[]{:S(2)}) collective-permute-start(bf16[64,1024]{1,0:T(8,128)(2,1)S(1)} %collective-permute-done.4.refs_0_), channel_id=1, source_target_pairs={{0,2},{1,9},{2,0},{3,11},{4,6},{5,13},{6,4},{7,15},{8,10},{9,1},{1... | collective-permute-start | bytes 393224 | tf_op jit(solution)/shard_map/ppermute | solution.py:286
  17.8 9.6 %collective-permute-start.10 = (bf16[64,1024]{1,0:T(8,128)(2,1)S(1)}, bf16[64,1024]{1,0:T(8,128)(2,1)S(1)}, u32[]{:S(2)}, u32[]{:S(2)}) collective-permute-start(bf16[64,1024]{1,0:T(8,128)(2,1)S(1)} %collective-permute-done.8.refs_0_), channel_id=1, source_target_pairs={{0,4},{1,17},{2,6},{3,19},{4,0},{5,21},{6,2},{7,23},{8,12},{9,25},... | collective-permute-start | bytes 393224 | tf_op jit(solution)/shard_map/ppermute | solution.py:286
  20.0 8.8 %collective-permute-start.6 = (bf16[64,1024]{1,0:T(8,128)(2,1)S(1)}, bf16[64,1024]{1,0:T(8,128)(2,1)S(1)}, u32[]{:S(2)}, u32[]{:S(2)}) collective-permute-start(bf16[64,1024]{1,0:T(8,128)(2,1)S(1)} %collective-permute-done.4.refs_0_), channel_id=1, source_target_pairs={{0,4},{1,17},{2,6},{3,19},{4,0},{5,21},{6,2},{7,23},{8,12},{9,25},... | collective-permute-start | bytes 393224 | tf_op jit(solution)/shard_map/ppermute | solution.py:286
  23.1 7.2 %collective-permute-start.3 = (bf16[64,1024]{1,0:T(8,128)(2,1)S(1)}, bf16[64,1024]{1,0:T(8,128)(2,1)S(1)}, u32[]{:S(2)}, u32[]{:S(2)}) collective-permute-start(bf16[64,1024]{1,0:T(8,128)(2,1)S(1)} %collective-permute-done.2.refs_2_), channel_id=1, source_target_pairs={{0,2},{1,9},{2,0},{3,11},{4,6},{5,13},{6,4},{7,15},{8,10},{9,1},{1... | collective-permute-start | bytes 393224 | tf_op jit(solution)/shard_map/ppermute | solution.py:286
  24.2 7.5 %collective-permute-start.14 = (bf16[64,1024]{1,0:T(8,128)(2,1)S(1)}, bf16[64,1024]{1,0:T(8,128)(2,1)S(1)}, u32[]{:S(2)}, u32[]{:S(2)}) collective-permute-start(bf16[64,1024]{1,0:T(8,128)(2,1)S(1)} %hold.3.refs_0_), channel_id=1, source_target_pairs={{0,4},{1,17},{2,6},{3,19},{4,0},{5,21},{6,2},{7,23},{8,12},{9,25},... | collective-permute-start | bytes 393224 | tf_op jit(solution)/shard_map/ppermute | solution.py:286
  26.1 6.6 %collective-permute-start.9 = (bf16[64,1024]{1,0:T(8,128)(2,1)S(1)}, bf16[64,1024]{1,0:T(8,128)(2,1)S(1)}, u32[]{:S(2)}, u32[]{:S(2)}) collective-permute-start(bf16[64,1024]{1,0:T(8,128)(2,1)S(1)} %collective-permute-done.8.refs_0_), channel_id=1, source_target_pairs={{0,2},{1,9},{2,0},{3,11},{4,6},{5,13},{6,4},{7,15},{8,10},{9,1},{1... | collective-permute-start | bytes 393224 | tf_op jit(solution)/shard_map/ppermute | solution.py:286
  27.4 6.7 %collective-permute-start.11 = (bf16[64,1024]{1,0:T(8,128)(2,1)S(1)}, bf16[64,1024]{1,0:T(8,128)(2,1)S(1)}, u32[]{:S(2)}, u32[]{:S(2)}) collective-permute-start(bf16[64,1024]{1,0:T(8,128)(2,1)S(1)} %collective-permute-done.10.refs_2_), channel_id=1, source_target_pairs={{0,2},{1,9},{2,0},{3,11},{4,6},{5,13},{6,4},{7,15},{8,10},{9,1},{1... | collective-permute-start | bytes 393224 | tf_op jit(solution)/shard_map/ppermute | solution.py:286
  28.8 6.7 %collective-permute-start.7 = (bf16[64,1024]{1,0:T(8,128)(2,1)S(1)}, bf16[64,1024]{1,0:T(8,128)(2,1)S(1)}, u32[]{:S(2)}, u32[]{:S(2)}) collective-permute-start(bf16[64,1024]{1,0:T(8,128)(2,1)S(1)} %collective-permute-done.6.refs_2_), channel_id=1, source_target_pairs={{0,2},{1,9},{2,0},{3,11},{4,6},{5,13},{6,4},{7,15},{8,10},{9,1},{1... | collective-permute-start | bytes 393224 | tf_op jit(solution)/shard_map/ppermute | solution.py:286
  30.3 6.6 %collective-permute-start.13 = (bf16[64,1024]{1,0:T(8,128)(2,1)S(1)}, bf16[64,1024]{1,0:T(8,128)(2,1)S(1)}, u32[]{:S(2)}, u32[]{:S(2)}) collective-permute-start(bf16[64,1024]{1,0:T(8,128)(2,1)S(1)} %hold.3.refs_0_), channel_id=1, source_target_pairs={{0,2},{1,9},{2,0},{3,11},{4,6},{5,13},{6,4},{7,15},{8,10},{9,1},{1... | collective-permute-start | bytes 393224 | tf_op jit(solution)/shard_map/ppermute | solution.py:286
  31.7 6.6 %collective-permute-start.15 = (bf16[64,1024]{1,0:T(8,128)(2,1)S(1)}, bf16[64,1024]{1,0:T(8,128)(2,1)S(1)}, u32[]{:S(2)}, u32[]{:S(2)}) collective-permute-start(bf16[64,1024]{1,0:T(8,128)(2,1)S(1)} %collective-permute-done.14.refs_2_), channel_id=1, source_target_pairs={{0,2},{1,9},{2,0},{3,11},{4,6},{5,13},{6,4},{7,15},{8,10},{9,1},{1... | collective-permute-start | bytes 393224 | tf_op jit(solution)/shard_map/ppermute | solution.py:286
  32.7 5.7 %collective-permute-start.16 = (bf16[4,64,1024]{2,1,0:T(8,128)(2,1)S(1)}, bf16[4,64,1024]{2,1,0:T(8,128)(2,1)S(1)}, u32[]{:S(2)}, u32[]{:S(2)}) collective-permute-start(bf16[4,64,1024]{2,1,0:T(8,128)(2,1)S(1)} %pack.4.refs_0_), channel_id=1, source_target_pairs={{0,1},{1,0},{2,3},{3,2},{4,5},{5,4},{6,7},{7,6},{8,9},{9,8},{10,11... | collective-permute-start | bytes 1572872 | tf_op jit(solution)/shard_map/ppermute | solution.py:286
  34.1 4.3 %collective-permute-start.18 = (bf16[4,64,1024]{2,1,0:T(8,128)(2,1)S(1)}, bf16[4,64,1024]{2,1,0:T(8,128)(2,1)S(1)}, u32[]{:S(2)}, u32[]{:S(2)}) collective-permute-start(bf16[4,64,1024]{2,1,0:T(8,128)(2,1)S(1)} %pack.6.refs_2_), channel_id=1, source_target_pairs={{0,1},{1,0},{2,3},{3,2},{4,5},{5,4},{6,7},{7,6},{8,9},{9,8},{10,11... | collective-permute-start | bytes 1572872 | tf_op jit(solution)/shard_map/ppermute | solution.py:286
  35.5 2.9 %collective-permute-start.17 = (bf16[4,64,1024]{2,1,0:T(8,128)(2,1)S(1)}, bf16[4,64,1024]{2,1,0:T(8,128)(2,1)S(1)}, u32[]{:S(2)}, u32[]{:S(2)}) collective-permute-start(bf16[4,64,1024]{2,1,0:T(8,128)(2,1)S(1)} %pack.5.refs_1_), channel_id=1, source_target_pairs={{0,1},{1,0},{2,3},{3,2},{4,5},{5,4},{6,7},{7,6},{8,9},{9,8},{10,11... | collective-permute-start | bytes 1572872 | tf_op jit(solution)/shard_map/ppermute | solution.py:286
  38.3 2.0 %collective-permute-start.19 = (bf16[4,64,1024]{2,1,0:T(8,128)(2,1)S(1)}, bf16[4,64,1024]{2,1,0:T(8,128)(2,1)S(1)}, u32[]{:S(2)}, u32[]{:S(2)}) collective-permute-start(bf16[4,64,1024]{2,1,0:T(8,128)(2,1)S(1)} %pack.7.refs_3_), channel_id=1, source_target_pairs={{0,1},{1,0},{2,3},{3,2},{4,5},{5,4},{6,7},{7,6},{8,9},{9,8},{10,11... | collective-permute-start | bytes 1572872 | tf_op jit(solution)/shard_map/ppermute | solution.py:286

commit v4 on v3

--- a/solution.py
+++ b/solution.py
@@ -19,7 +19,6 @@
 GROUP = 2 * CHUNK
 ROWS = 2 * F
 WINDOW_GROUP = 2 * GROUP
-GATES = {0: [1], 1: [1]}
 
 AXES = ("row", "col")
 BF16 = jnp.bfloat16
@@ -162,23 +161,28 @@
         in_specs=[vmem] * 2,
         out_specs=[vmem] * slices,
         compiler_params=pltpu.CompilerParams(vmem_limit_bytes=8 * 2**20),
+        cost_estimate=pl.CostEstimate(flops=1, bytes_accessed=1, transcendentals=0),
         name="pair_windows",
     )(own, other)
 
 
 def pack_body(*refs):
-    for index, ref in enumerate(refs[:-1]):
-        refs[-1][index] = ref[...]
+    out, start = refs[-1], 0
+    for ref in refs[:-1]:
+        out[start : start + ref.shape[0]] = ref[...]
+        start += ref.shape[0]
 
 
 def pack(values):
+    rows = sum(value.shape[0] for value in values)
     vmem = pl.BlockSpec(memory_space=pltpu.VMEM)
     return pl.pallas_call(
         pack_body,
-        out_shape=jax.ShapeDtypeStruct((len(values), *values[0].shape), BF16),
+        out_shape=jax.ShapeDtypeStruct((rows, *values[0].shape[1:]), BF16),
         in_specs=[vmem] * len(values),
         out_specs=vmem,
         compiler_params=pltpu.CompilerParams(vmem_limit_bytes=8 * 2**20),
+        cost_estimate=pl.CostEstimate(flops=1, bytes_accessed=1, transcendentals=0),
         name="pack",
     )(*values)
 
@@ -195,13 +199,15 @@
         in_specs=[vmem] * (1 + len(after)),
         out_specs=vmem,
         compiler_params=pltpu.CompilerParams(vmem_limit_bytes=8 * 2**20),
+        cost_estimate=pl.CostEstimate(flops=1, bytes_accessed=1, transcendentals=0),
         name="hold",
     )(value, *after)
 
 
-def product_body(count, windows, *refs):
-    held, swapped = refs[:count], refs[count : 2 * count]
-    out, turned, right, tiles, stored = refs[2 * count :]
+def product_body(count, windows, places, *refs):
+    arrays = len(refs) // 2 - 2
+    held, swapped = refs[:arrays], refs[arrays : 2 * arrays]
+    out, turned, right, tiles, stored = refs[2 * arrays :]
     depth, double = right.shape
     width = double // 2
     chunks = pl.num_programs(0)
@@ -209,12 +215,16 @@
     core = lax.rem(lax.axis_index("col"), 2)
 
     def prepare(rows_of, cols_of, start):
-        unit = pl.ds(pl.multiple_of(chunk * WINDOW_GROUP, WINDOW_GROUP), WINDOW_GROUP)
-        lefts = [ref[line, unit] for line in range(count) for ref in rows_of]
+        def take(arrays, first, second):
+            array, start = places[first, second]
+            base = pl.multiple_of(start + chunk * WINDOW_GROUP, WINDOW_GROUP)
+            return arrays[array][pl.ds(base, WINDOW_GROUP), :]
+
+        lefts = [take(rows_of, plane, line) for line in range(count) for plane in range(count)]
         turned[...] = jnp.concatenate(lefts, axis=0).T
         columns = slice(start, start + width)
-        rights = [ref[plane, unit, columns] for ref in cols_of for plane in range(count)]
-        straight = jnp.concatenate(rights, axis=0).astype(F32)
+        rights = [take(cols_of, line, plane) for line in range(count) for plane in range(count)]
+        straight = jnp.concatenate(rights, axis=0)[:, columns].astype(F32)
         shaped = straight.reshape(depth // GROUP, 2, CHUNK, width)
         crossed = jnp.stack([shaped[:, 1], -shaped[:, 0]], axis=1).reshape(depth, width)
         right[:, :width] = straight
@@ -244,16 +254,15 @@
                 store(bin_index, part).wait()
 
 
-def multiply(held, swapped, windows):
-    count = len(held)
-    height = held[0].shape[2]
+def multiply(count, places, held, swapped, windows):
+    height = held[0].shape[1]
     depth, width = count * count * WINDOW_GROUP, height // 2
     vmem = pl.BlockSpec(memory_space=pltpu.VMEM)
     return pl.pallas_call(
-        functools.partial(product_body, count, windows),
+        functools.partial(product_body, count, windows, places),
         out_shape=jax.ShapeDtypeStruct((F, 2, height, width), BF16),
         grid=(CHUNKS,),
-        in_specs=[vmem] * (2 * count),
+        in_specs=[vmem] * (2 * len(held)),
         out_specs=pl.BlockSpec(memory_space=pl.ANY),
         scratch_shapes=[
             pltpu.VMEM((height, depth), BF16),
@@ -295,18 +304,19 @@
         pieces.append(send(to_send[step], (step, 0), (0, step), 0))
 
     bits = [row_count >> shift for shift in range(1, row_count.bit_length())]
-    units, early = [], []
+    packs, places, early = [], {}, []
     for step, piece in enumerate(pieces):
         if step == row_count - 1:
-            piece = hold(piece, early)
+            piece = hold(piece, early[:2])
         held = {0: piece}
         for bit in bits:
             for slot in list(held):
                 held[slot ^ bit] = send(held[slot], (0, bit), (bit, 0), 0)
-        if step in GATES:
-            early += [held[bit] for bit in GATES[step]]
-        units.append(pack([held[slot] for slot in range(row_count)]))
-    return multiply(units, [swap(unit) for unit in units], windows)
+        early.append(held[1])
+        for order, slot in enumerate(held):
+            places[step, slot] = (step, order * 2 * ROWS)
+        packs.append(pack(list(held.values())))
+    return multiply(row_count, places, packs, [swap(value) for value in packs], windows)
 
 
 def solution(mesh):

time: 52.9 us -> 52.5 us (level)
  no operation moved by 1% of the time
where the time goes in v4:
time: 52.5 us; the launch traced here: 52.3 us
  starting transfers between devices  20.7 us (39%)
  Pallas kernels  17.9 us (34%)
  waiting for transfers between devices  12 us (23%)
  local copies, waits for them, and re-layouts  0.95 us (2%)
  between operations  0.75 us (1%)
    ppermute x20, starting transfers between devices, send(): return lax.ppermute(value, AXES, pairs)  20.7 us
    pallas_call x1, Pallas kernels, multiply(): pl.pallas_call(functools.partial(product_body, count, windows, places), o...  12 us
    ppermute x20, waiting for transfers between devices, send(): return lax.ppermute(value, AXES, pairs)  12 us
    pallas_call x1, Pallas kernels, make_spectra(): pl.pallas_call(spectra_body, out_shape=jax.ShapeDtypeStruct((slices, ROWS...  5.66 us
  transfers between devices with their start and end apart: 20, of which 13 were waited for; matrix products, arithmetic and copies ran while one was open for 0% of the time, Pallas kernels for 0%

profile of v4, /device:TPU:0, one launch (start us, length us, event | category | flops | bytes accessed | tf_op | source)
XLA Modules:
  0.0 52.3 jit_solution(8906749635136921507)
XLA Ops:
  0.7 5.7 %spectra.1.value = bf16[4,32,1024]{2,1,0:T(8,128)(2,1)} custom-call(f32[101]{0:T(128)} %fir_taps.1, s32[16]{0:T(128)} %bins.1, s32[1]{0:T(128)S(6)} %copy.5.offsets, bf16[1408,4096]{1,0:T(8,128)(2,1)} %record.1), custom_call_target="tpu_custom_call" | custom-call | tf_op jit(solution)/shard_map/spectra/pallas_call | solution.py:118
  6.3 0.5 collective-permute-start
  6.8 0.9 %copy-done = bf16[4,32,1024]{2,1,0:T(8,128)(2,1)S(1)} copy-done((bf16[4,32,1024]{2,1,0:T(8,128)(2,1)S(1)}, bf16[4,32,1024]{2,1,0:T(8,128)(2,1)}, u32[]{:S(2)}) %copy-start) | copy-done | bytes 262168
  7.8 0.4 collective-permute-done.other
  8.2 0.1 pair_windows.1
  8.3 2.9 %collective-permute-start.4 = (bf16[64,1024]{1,0:T(8,128)(2,1)S(1)}, bf16[64,1024]{1,0:T(8,128)(2,1)S(1)}, u32[]{:S(2)}, u32[]{:S(2)}) collective-permute-start(bf16[64,1024]{1,0:T(8,128)(2,1)S(1)} %get-tuple-element.10), channel_id=1, source_target_pairs={{0,8},{1,3},{2,10},{3,1},{4,12},{5,7},{6,14},{7,5},{8,0},{9,11},{1... | collective-permute-start | bytes 393224 | tf_op jit(solution)/shard_map/ppermute | solution.py:295
  11.2 1.5 %collective-permute-start.8 = (bf16[64,1024]{1,0:T(8,128)(2,1)S(1)}, bf16[64,1024]{1,0:T(8,128)(2,1)S(1)}, u32[]{:S(2)}, u32[]{:S(2)}) collective-permute-start(bf16[64,1024]{1,0:T(8,128)(2,1)S(1)} %get-tuple-element.11), channel_id=1, source_target_pairs={{0,16},{1,5},{2,18},{3,7},{4,20},{5,1},{6,22},{7,3},{8,24},{9,13},... | collective-permute-start | bytes 393224 | tf_op jit(solution)/shard_map/ppermute | solution.py:295
  12.8 3.0 %collective-permute-start.1 = (bf16[64,1024]{1,0:T(8,128)(2,1)S(1)}, bf16[64,1024]{1,0:T(8,128)(2,1)S(1)}, u32[]{:S(2)}, u32[]{:S(2)}) collective-permute-start(bf16[64,1024]{1,0:T(8,128)(2,1)S(1)} %get-tuple-element.9.refs_0_), channel_id=1, source_target_pairs={{0,4},{1,17},{2,6},{3,19},{4,0},{5,21},{6,2},{7,23},{8,12},{9,25},... | collective-permute-start | bytes 393224 | tf_op jit(solution)/shard_map/ppermute | solution.py:295
  15.8 1.6 %collective-permute-start.2 = (bf16[64,1024]{1,0:T(8,128)(2,1)S(1)}, bf16[64,1024]{1,0:T(8,128)(2,1)S(1)}, u32[]{:S(2)}, u32[]{:S(2)}) collective-permute-start(bf16[64,1024]{1,0:T(8,128)(2,1)S(1)} %get-tuple-element.9.refs_0_), channel_id=1, source_target_pairs={{0,2},{1,9},{2,0},{3,11},{4,6},{5,13},{6,4},{7,15},{8,10},{9,1},{1... | collective-permute-start | bytes 393224 | tf_op jit(solution)/shard_map/ppermute | solution.py:295
  17.4 0.5 collective-permute-start.6
  17.8 2.0 %collective-permute-start.9 = (bf16[64,1024]{1,0:T(8,128)(2,1)S(1)}, bf16[64,1024]{1,0:T(8,128)(2,1)S(1)}, u32[]{:S(2)}, u32[]{:S(2)}) collective-permute-start(bf16[64,1024]{1,0:T(8,128)(2,1)S(1)} %collective-permute-done.8.refs_0_), channel_id=1, source_target_pairs={{0,4},{1,17},{2,6},{3,19},{4,0},{5,21},{6,2},{7,23},{8,12},{9,25},... | collective-permute-start | bytes 393224 | tf_op jit(solution)/shard_map/ppermute | solution.py:295
  19.9 0.1 collective-permute-done.12.value
  20.0 2.6 %collective-permute-start.5 = (bf16[64,1024]{1,0:T(8,128)(2,1)S(1)}, bf16[64,1024]{1,0:T(8,128)(2,1)S(1)}, u32[]{:S(2)}, u32[]{:S(2)}) collective-permute-start(bf16[64,1024]{1,0:T(8,128)(2,1)S(1)} %collective-permute-done.4.refs_0_), channel_id=1, source_target_pairs={{0,4},{1,17},{2,6},{3,19},{4,0},{5,21},{6,2},{7,23},{8,12},{9,25},... | collective-permute-start | bytes 393224 | tf_op jit(solution)/shard_map/ppermute | solution.py:295
  22.6 0.5 collective-permute-done.1.refs_1_
  23.1 1.1 %collective-permute-start.3 = (bf16[64,1024]{1,0:T(8,128)(2,1)S(1)}, bf16[64,1024]{1,0:T(8,128)(2,1)S(1)}, u32[]{:S(2)}, u32[]{:S(2)}) collective-permute-start(bf16[64,1024]{1,0:T(8,128)(2,1)S(1)} %collective-permute-done.1.refs_1_), channel_id=1, source_target_pairs={{0,2},{1,9},{2,0},{3,11},{4,6},{5,13},{6,4},{7,15},{8,10},{9,1},{1... | collective-permute-start | bytes 393224 | tf_op jit(solution)/shard_map/ppermute | solution.py:295
  24.2 1.9 %collective-permute-start.13 = (bf16[64,1024]{1,0:T(8,128)(2,1)S(1)}, bf16[64,1024]{1,0:T(8,128)(2,1)S(1)}, u32[]{:S(2)}, u32[]{:S(2)}) collective-permute-start(bf16[64,1024]{1,0:T(8,128)(2,1)S(1)} %hold.3.refs_0_), channel_id=1, source_target_pairs={{0,4},{1,17},{2,6},{3,19},{4,0},{5,21},{6,2},{7,23},{8,12},{9,25},... | collective-permute-start | bytes 393224 | tf_op jit(solution)/shard_map/ppermute | solution.py:295
  26.1 0.2 collective-permute-start.10
  26.4 1.0 %collective-permute-done.9.refs_1_ = bf16[64,1024]{1,0:T(8,128)(2,1)S(1)} collective-permute-done((bf16[64,1024]{1,0:T(8,128)(2,1)S(1)}, bf16[64,1024]{1,0:T(8,128)(2,1)S(1)}, u32[]{:S(2)}, u32[]{:S(2)}) %collective-permute-start.9) | collective-permute-done | bytes 131104 | tf_op jit(solution)/shard_map/ppermute | solution.py:295
  27.4 0.7 %collective-permute-start.11 = (bf16[64,1024]{1,0:T(8,128)(2,1)S(1)}, bf16[64,1024]{1,0:T(8,128)(2,1)S(1)}, u32[]{:S(2)}, u32[]{:S(2)}) collective-permute-start(bf16[64,1024]{1,0:T(8,128)(2,1)S(1)} %collective-permute-done.9.refs_1_), channel_id=1, source_target_pairs={{0,2},{1,9},{2,0},{3,11},{4,6},{5,13},{6,4},{7,15},{8,10},{9,1},{1... | collective-permute-start | bytes 393224 | tf_op jit(solution)/shard_map/ppermute | solution.py:295
  28.1 0.7 %collective-permute-done.5.refs_1_ = bf16[64,1024]{1,0:T(8,128)(2,1)S(1)} collective-permute-done((bf16[64,1024]{1,0:T(8,128)(2,1)S(1)}, bf16[64,1024]{1,0:T(8,128)(2,1)S(1)}, u32[]{:S(2)}, u32[]{:S(2)}) %collective-permute-start.5) | collective-permute-done | bytes 131104 | tf_op jit(solution)/shard_map/ppermute | solution.py:295
  28.8 0.6 %collective-permute-start.7 = (bf16[64,1024]{1,0:T(8,128)(2,1)S(1)}, bf16[64,1024]{1,0:T(8,128)(2,1)S(1)}, u32[]{:S(2)}, u32[]{:S(2)}) collective-permute-start(bf16[64,1024]{1,0:T(8,128)(2,1)S(1)} %collective-permute-done.5.refs_1_), channel_id=1, source_target_pairs={{0,2},{1,9},{2,0},{3,11},{4,6},{5,13},{6,4},{7,15},{8,10},{9,1},{1... | collective-permute-start | bytes 393224 | tf_op jit(solution)/shard_map/ppermute | solution.py:295
  29.4 0.9 %collective-permute-done.3.refs_3_ = bf16[64,1024]{1,0:T(8,128)(2,1)S(1)} collective-permute-done((bf16[64,1024]{1,0:T(8,128)(2,1)S(1)}, bf16[64,1024]{1,0:T(8,128)(2,1)S(1)}, u32[]{:S(2)}, u32[]{:S(2)}) %collective-permute-start.3) | collective-permute-done | bytes 131104 | tf_op jit(solution)/shard_map/ppermute | solution.py:295
  30.3 0.5 collective-permute-start.14
  30.8 0.8 %collective-permute-done.13.refs_1_ = bf16[64,1024]{1,0:T(8,128)(2,1)S(1)} collective-permute-done((bf16[64,1024]{1,0:T(8,128)(2,1)S(1)}, bf16[64,1024]{1,0:T(8,128)(2,1)S(1)}, u32[]{:S(2)}, u32[]{:S(2)}) %collective-permute-start.13) | collective-permute-done | bytes 131104 | tf_op jit(solution)/shard_map/ppermute | solution.py:295
  31.7 0.7 %collective-permute-start.15 = (bf16[64,1024]{1,0:T(8,128)(2,1)S(1)}, bf16[64,1024]{1,0:T(8,128)(2,1)S(1)}, u32[]{:S(2)}, u32[]{:S(2)}) collective-permute-start(bf16[64,1024]{1,0:T(8,128)(2,1)S(1)} %collective-permute-done.13.refs_1_), channel_id=1, source_target_pairs={{0,2},{1,9},{2,0},{3,11},{4,6},{5,13},{6,4},{7,15},{8,10},{9,1},{1... | collective-permute-start | bytes 393224 | tf_op jit(solution)/shard_map/ppermute | solution.py:295
  32.4 0.3 collective-permute-done.10.refs_2_
  32.7 1.4 %collective-permute-done.11.refs_3_ = bf16[64,1024]{1,0:T(8,128)(2,1)S(1)} collective-permute-done((bf16[64,1024]{1,0:T(8,128)(2,1)S(1)}, bf16[64,1024]{1,0:T(8,128)(2,1)S(1)}, u32[]{:S(2)}, u32[]{:S(2)}) %collective-permute-start.11) | collective-permute-done | bytes 131104 | tf_op jit(solution)/shard_map/ppermute | solution.py:295
  34.2 1.3 %collective-permute-done.7.refs_3_ = bf16[64,1024]{1,0:T(8,128)(2,1)S(1)} collective-permute-done((bf16[64,1024]{1,0:T(8,128)(2,1)S(1)}, bf16[64,1024]{1,0:T(8,128)(2,1)S(1)}, u32[]{:S(2)}, u32[]{:S(2)}) %collective-permute-start.7) | collective-permute-done | bytes 131104 | tf_op jit(solution)/shard_map/ppermute | solution.py:295
  35.6 1.3 %collective-permute-done.14.refs_2_ = bf16[64,1024]{1,0:T(8,128)(2,1)S(1)} collective-permute-done((bf16[64,1024]{1,0:T(8,128)(2,1)S(1)}, bf16[64,1024]{1,0:T(8,128)(2,1)S(1)}, u32[]{:S(2)}, u32[]{:S(2)}) %collective-permute-start.14) | collective-permute-done | bytes 131104 | tf_op jit(solution)/shard_map/ppermute | solution.py:295
  36.9 1.4 %collective-permute-done.15.refs_3_ = bf16[64,1024]{1,0:T(8,128)(2,1)S(1)} collective-permute-done((bf16[64,1024]{1,0:T(8,128)(2,1)S(1)}, bf16[64,1024]{1,0:T(8,128)(2,1)S(1)}, u32[]{:S(2)}, u32[]{:S(2)}) %collective-permute-start.15) | collective-permute-done | bytes 131104 | tf_op jit(solution)/shard_map/ppermute | solution.py:295
  38.4 1.9 %collective-permute-done.19.refs_7_ = bf16[256,1024]{1,0:T(8,128)(2,1)S(1)} collective-permute-done((bf16[256,1024]{1,0:T(8,128)(2,1)S(1)}, bf16[256,1024]{1,0:T(8,128)(2,1)S(1)}, u32[]{:S(2)}, u32[]{:S(2)}) %collective-permute-start.19) | collective-permute-done | bytes 524320 | tf_op jit(solution)/shard_map/ppermute | solution.py:295
  40.3 12.0 %products.1 = bf16[16,2,1024,512]{3,2,1,0:T(8,128)(2,1)} custom-call(bf16[256,1024]{1,0:T(8,128)(2,1)S(1)} %pack.4.refs_0_, bf16[256,1024]{1,0:T(8,128)(2,1)S(1)} %pack.5.refs_1_, bf16[256,1024]{1,0:T(8,128)(2,1)S(1)} %pack.6.refs_2_, bf16[256,1024]{1,0:T(8,128)(2,1)S(1)} %pack.7.refs_3_, bf16[256,1024]{1,0:T(8,128)(2,1)S(1)} %collective-permute-done.16.refs_4_, ...), custom_call_target="tpu_custom_call" | custom-call | flops 8589934592 | bytes 33554432 | tf_op jit(solution)/shard_map/products/pallas_call | solution.py:261
  (19 shorter events, 0.4 us)
Async XLA Ops:
  6.3 1.9 %collective-permute-start = (bf16[4,32,1024]{2,1,0:T(8,128)(2,1)}, bf16[4,32,1024]{2,1,0:T(8,128)(2,1)S(1)}, u32[]{:S(2)}, u32[]{:S(2)}) collective-permute-start(bf16[4,32,1024]{2,1,0:T(8,128)(2,1)} %spectra.1.value), channel_id=1, source_target_pairs={{0,1},{1,0},{2,3},{3,2},{4,5},{5,4},{6,7},{7,6},{8,9},{9,8},{10,11... | collective-permute-start | bytes 786440 | tf_op jit(solution)/shard_map/ppermute | solution.py:295
  6.8 0.9 %copy-start = (bf16[4,32,1024]{2,1,0:T(8,128)(2,1)S(1)}, bf16[4,32,1024]{2,1,0:T(8,128)(2,1)}, u32[]{:S(2)}) copy-start(bf16[4,32,1024]{2,1,0:T(8,128)(2,1)} %spectra.1.value) | copy-start | bytes 786436
  8.3 9.1 %collective-permute-start.4 = (bf16[64,1024]{1,0:T(8,128)(2,1)S(1)}, bf16[64,1024]{1,0:T(8,128)(2,1)S(1)}, u32[]{:S(2)}, u32[]{:S(2)}) collective-permute-start(bf16[64,1024]{1,0:T(8,128)(2,1)S(1)} %get-tuple-element.10), channel_id=1, source_target_pairs={{0,8},{1,3},{2,10},{3,1},{4,12},{5,7},{6,14},{7,5},{8,0},{9,11},{1... | collective-permute-start | bytes 393224 | tf_op jit(solution)/shard_map/ppermute | solution.py:295
  11.2 6.6 %collective-permute-start.8 = (bf16[64,1024]{1,0:T(8,128)(2,1)S(1)}, bf16[64,1024]{1,0:T(8,128)(2,1)S(1)}, u32[]{:S(2)}, u32[]{:S(2)}) collective-permute-start(bf16[64,1024]{1,0:T(8,128)(2,1)S(1)} %get-tuple-element.11), channel_id=1, source_target_pairs={{0,16},{1,5},{2,18},{3,7},{4,20},{5,1},{6,22},{7,3},{8,24},{9,13},... | collective-permute-start | bytes 393224 | tf_op jit(solution)/shard_map/ppermute | solution.py:295
  12.7 7.2 %collective-permute-start.12 = (bf16[64,1024]{1,0:T(8,128)(2,1)S(1)}, bf16[64,1024]{1,0:T(8,128)(2,1)S(1)}, u32[]{:S(2)}, u32[]{:S(2)}) collective-permute-start(bf16[64,1024]{1,0:T(8,128)(2,1)S(1)} %get-tuple-element.12), channel_id=1, source_target_pairs={{0,24},{1,7},{2,26},{3,5},{4,28},{5,3},{6,30},{7,1},{8,16},{9,15},... | collective-permute-start | bytes 393224 | tf_op jit(solution)/shard_map/ppermute | solution.py:295
  12.8 10.3 %collective-permute-start.1 = (bf16[64,1024]{1,0:T(8,128)(2,1)S(1)}, bf16[64,1024]{1,0:T(8,128)(2,1)S(1)}, u32[]{:S(2)}, u32[]{:S(2)}) collective-permute-start(bf16[64,1024]{1,0:T(8,128)(2,1)S(1)} %get-tuple-element.9.refs_0_), channel_id=1, source_target_pairs={{0,4},{1,17},{2,6},{3,19},{4,0},{5,21},{6,2},{7,23},{8,12},{9,25},... | collective-permute-start | bytes 393224 | tf_op jit(solution)/shard_map/ppermute | solution.py:295
  15.8 8.4 %collective-permute-start.2 = (bf16[64,1024]{1,0:T(8,128)(2,1)S(1)}, bf16[64,1024]{1,0:T(8,128)(2,1)S(1)}, u32[]{:S(2)}, u32[]{:S(2)}) collective-permute-start(bf16[64,1024]{1,0:T(8,128)(2,1)S(1)} %get-tuple-element.9.refs_0_), channel_id=1, source_target_pairs={{0,2},{1,9},{2,0},{3,11},{4,6},{5,13},{6,4},{7,15},{8,10},{9,1},{1... | collective-permute-start | bytes 393224 | tf_op jit(solution)/shard_map/ppermute | solution.py:295
  17.4 6.8 %collective-permute-start.6 = (bf16[64,1024]{1,0:T(8,128)(2,1)S(1)}, bf16[64,1024]{1,0:T(8,128)(2,1)S(1)}, u32[]{:S(2)}, u32[]{:S(2)}) collective-permute-start(bf16[64,1024]{1,0:T(8,128)(2,1)S(1)} %collective-permute-done.4.refs_0_), channel_id=1, source_target_pairs={{0,2},{1,9},{2,0},{3,11},{4,6},{5,13},{6,4},{7,15},{8,10},{9,1},{1... | collective-permute-start | bytes 393224 | tf_op jit(solution)/shard_map/ppermute | solution.py:295
  17.8 9.6 %collective-permute-start.9 = (bf16[64,1024]{1,0:T(8,128)(2,1)S(1)}, bf16[64,1024]{1,0:T(8,128)(2,1)S(1)}, u32[]{:S(2)}, u32[]{:S(2)}) collective-permute-start(bf16[64,1024]{1,0:T(8,128)(2,1)S(1)} %collective-permute-done.8.refs_0_), channel_id=1, source_target_pairs={{0,4},{1,17},{2,6},{3,19},{4,0},{5,21},{6,2},{7,23},{8,12},{9,25},... | collective-permute-start | bytes 393224 | tf_op jit(solution)/shard_map/ppermute | solution.py:295
  20.0 8.8 %collective-permute-start.5 = (bf16[64,1024]{1,0:T(8,128)(2,1)S(1)}, bf16[64,1024]{1,0:T(8,128)(2,1)S(1)}, u32[]{:S(2)}, u32[]{:S(2)}) collective-permute-start(bf16[64,1024]{1,0:T(8,128)(2,1)S(1)} %collective-permute-done.4.refs_0_), channel_id=1, source_target_pairs={{0,4},{1,17},{2,6},{3,19},{4,0},{5,21},{6,2},{7,23},{8,12},{9,25},... | collective-permute-start | bytes 393224 | tf_op jit(solution)/shard_map/ppermute | solution.py:295
  23.1 7.2 %collective-permute-start.3 = (bf16[64,1024]{1,0:T(8,128)(2,1)S(1)}, bf16[64,1024]{1,0:T(8,128)(2,1)S(1)}, u32[]{:S(2)}, u32[]{:S(2)}) collective-permute-start(bf16[64,1024]{1,0:T(8,128)(2,1)S(1)} %collective-permute-done.1.refs_1_), channel_id=1, source_target_pairs={{0,2},{1,9},{2,0},{3,11},{4,6},{5,13},{6,4},{7,15},{8,10},{9,1},{1... | collective-permute-start | bytes 393224 | tf_op jit(solution)/shard_map/ppermute | solution.py:295
  24.2 7.5 %collective-permute-start.13 = (bf16[64,1024]{1,0:T(8,128)(2,1)S(1)}, bf16[64,1024]{1,0:T(8,128)(2,1)S(1)}, u32[]{:S(2)}, u32[]{:S(2)}) collective-permute-start(bf16[64,1024]{1,0:T(8,128)(2,1)S(1)} %hold.3.refs_0_), channel_id=1, source_target_pairs={{0,4},{1,17},{2,6},{3,19},{4,0},{5,21},{6,2},{7,23},{8,12},{9,25},... | collective-permute-start | bytes 393224 | tf_op jit(solution)/shard_map/ppermute | solution.py:295
  26.1 6.6 %collective-permute-start.10 = (bf16[64,1024]{1,0:T(8,128)(2,1)S(1)}, bf16[64,1024]{1,0:T(8,128)(2,1)S(1)}, u32[]{:S(2)}, u32[]{:S(2)}) collective-permute-start(bf16[64,1024]{1,0:T(8,128)(2,1)S(1)} %collective-permute-done.8.refs_0_), channel_id=1, source_target_pairs={{0,2},{1,9},{2,0},{3,11},{4,6},{5,13},{6,4},{7,15},{8,10},{9,1},{1... | collective-permute-start | bytes 393224 | tf_op jit(solution)/shard_map/ppermute | solution.py:295
  27.4 6.7 %collective-permute-start.11 = (bf16[64,1024]{1,0:T(8,128)(2,1)S(1)}, bf16[64,1024]{1,0:T(8,128)(2,1)S(1)}, u32[]{:S(2)}, u32[]{:S(2)}) collective-permute-start(bf16[64,1024]{1,0:T(8,128)(2,1)S(1)} %collective-permute-done.9.refs_1_), channel_id=1, source_target_pairs={{0,2},{1,9},{2,0},{3,11},{4,6},{5,13},{6,4},{7,15},{8,10},{9,1},{1... | collective-permute-start | bytes 393224 | tf_op jit(solution)/shard_map/ppermute | solution.py:295
  28.8 6.7 %collective-permute-start.7 = (bf16[64,1024]{1,0:T(8,128)(2,1)S(1)}, bf16[64,1024]{1,0:T(8,128)(2,1)S(1)}, u32[]{:S(2)}, u32[]{:S(2)}) collective-permute-start(bf16[64,1024]{1,0:T(8,128)(2,1)S(1)} %collective-permute-done.5.refs_1_), channel_id=1, source_target_pairs={{0,2},{1,9},{2,0},{3,11},{4,6},{5,13},{6,4},{7,15},{8,10},{9,1},{1... | collective-permute-start | bytes 393224 | tf_op jit(solution)/shard_map/ppermute | solution.py:295
  30.3 6.6 %collective-permute-start.14 = (bf16[64,1024]{1,0:T(8,128)(2,1)S(1)}, bf16[64,1024]{1,0:T(8,128)(2,1)S(1)}, u32[]{:S(2)}, u32[]{:S(2)}) collective-permute-start(bf16[64,1024]{1,0:T(8,128)(2,1)S(1)} %hold.3.refs_0_), channel_id=1, source_target_pairs={{0,2},{1,9},{2,0},{3,11},{4,6},{5,13},{6,4},{7,15},{8,10},{9,1},{1... | collective-permute-start | bytes 393224 | tf_op jit(solution)/shard_map/ppermute | solution.py:295
  31.7 6.6 %collective-permute-start.15 = (bf16[64,1024]{1,0:T(8,128)(2,1)S(1)}, bf16[64,1024]{1,0:T(8,128)(2,1)S(1)}, u32[]{:S(2)}, u32[]{:S(2)}) collective-permute-start(bf16[64,1024]{1,0:T(8,128)(2,1)S(1)} %collective-permute-done.13.refs_1_), channel_id=1, source_target_pairs={{0,2},{1,9},{2,0},{3,11},{4,6},{5,13},{6,4},{7,15},{8,10},{9,1},{1... | collective-permute-start | bytes 393224 | tf_op jit(solution)/shard_map/ppermute | solution.py:295
  32.7 5.7 %collective-permute-start.16 = (bf16[256,1024]{1,0:T(8,128)(2,1)S(1)}, bf16[256,1024]{1,0:T(8,128)(2,1)S(1)}, u32[]{:S(2)}, u32[]{:S(2)}) collective-permute-start(bf16[256,1024]{1,0:T(8,128)(2,1)S(1)} %pack.4.refs_0_), channel_id=1, source_target_pairs={{0,1},{1,0},{2,3},{3,2},{4,5},{5,4},{6,7},{7,6},{8,9},{9,8},{10,11... | collective-permute-start | bytes 1572872 | tf_op jit(solution)/shard_map/ppermute | solution.py:295
  34.1 4.3 %collective-permute-start.18 = (bf16[256,1024]{1,0:T(8,128)(2,1)S(1)}, bf16[256,1024]{1,0:T(8,128)(2,1)S(1)}, u32[]{:S(2)}, u32[]{:S(2)}) collective-permute-start(bf16[256,1024]{1,0:T(8,128)(2,1)S(1)} %pack.6.refs_2_), channel_id=1, source_target_pairs={{0,1},{1,0},{2,3},{3,2},{4,5},{5,4},{6,7},{7,6},{8,9},{9,8},{10,11... | collective-permute-start | bytes 1572872 | tf_op jit(solution)/shard_map/ppermute | solution.py:295
  35.5 2.9 %collective-permute-start.17 = (bf16[256,1024]{1,0:T(8,128)(2,1)S(1)}, bf16[256,1024]{1,0:T(8,128)(2,1)S(1)}, u32[]{:S(2)}, u32[]{:S(2)}) collective-permute-start(bf16[256,1024]{1,0:T(8,128)(2,1)S(1)} %pack.5.refs_1_), channel_id=1, source_target_pairs={{0,1},{1,0},{2,3},{3,2},{4,5},{5,4},{6,7},{7,6},{8,9},{9,8},{10,11... | collective-permute-start | bytes 1572872 | tf_op jit(solution)/shard_map/ppermute | solution.py:295
  38.3 2.0 %collective-permute-start.19 = (bf16[256,1024]{1,0:T(8,128)(2,1)S(1)}, bf16[256,1024]{1,0:T(8,128)(2,1)S(1)}, u32[]{:S(2)}, u32[]{:S(2)}) collective-permute-start(bf16[256,1024]{1,0:T(8,128)(2,1)S(1)} %pack.7.refs_3_), channel_id=1, source_target_pairs={{0,1},{1,0},{2,3},{3,2},{4,5},{5,4},{6,7},{7,6},{8,9},{9,8},{10,11... | collective-permute-start | bytes 1572872 | tf_op jit(solution)/shard_map/ppermute | solution.py:295

commit v5 on v4

--- a/solution.py
+++ b/solution.py
@@ -299,14 +299,15 @@
 
     own = make_spectra(record, fir_taps, bins, offsets, row_count)
     to_send = pair_windows(hold(own, []), swap(own))
-    pieces = [to_send[0]]
-    for step in range(1, row_count):
-        pieces.append(send(to_send[step], (step, 0), (0, step), 0))
+    turns = [0, *reversed(range(1, row_count))]
+    pieces = {0: to_send[0]}
+    for step in turns[1:]:
+        pieces[step] = send(to_send[step], (step, 0), (0, step), 0)
 
     bits = [row_count >> shift for shift in range(1, row_count.bit_length())]
     packs, places, early = [], {}, []
-    for step, piece in enumerate(pieces):
-        if step == row_count - 1:
+    for step, piece in pieces.items():
+        if step == turns[-1]:
             piece = hold(piece, early[:2])
         held = {0: piece}
         for bit in bits:
@@ -314,7 +315,7 @@
                 held[slot ^ bit] = send(held[slot], (0, bit), (bit, 0), 0)
         early.append(held[1])
         for order, slot in enumerate(held):
-            places[step, slot] = (step, order * 2 * ROWS)
+            places[step, slot] = (len(packs), order * 2 * ROWS)
         packs.append(pack(list(held.values())))
     return multiply(row_count, places, packs, [swap(value) for value in packs], windows)
 

time: 52.5 us -> 51.6 us (0.983)
  transfers between devices with their start and end apart: 20 -> 20, of which waited for: 13 -> 11; matrix products, arithmetic and copies ran while one was open for 0% -> 0% of each run, Pallas kernels for 0% -> 0%
where the time goes in v5:
time: 51.6 us; the launch traced here: 51.5 us
  starting transfers between devices  20.2 us (39%)
  Pallas kernels  17.9 us (35%)
  waiting for transfers between devices  11.6 us (22%)
  local copies, waits for them, and re-layouts  0.95 us (2%)
  between operations  0.76 us (1%)
    ppermute x20, starting transfers between devices, send(): return lax.ppermute(value, AXES, pairs)  20.2 us
    pallas_call x1, Pallas kernels, multiply(): pl.pallas_call(functools.partial(product_body, count, windows, places), o...  12 us
    ppermute x20, waiting for transfers between devices, send(): return lax.ppermute(value, AXES, pairs)  11.6 us
    pallas_call x1, Pallas kernels, make_spectra(): pl.pallas_call(spectra_body, out_shape=jax.ShapeDtypeStruct((slices, ROWS...  5.66 us
  transfers between devices with their start and end apart: 20, of which 11 were waited for; matrix products, arithmetic and copies ran while one was open for 0% of the time, Pallas kernels for 0%

profile of v5, /device:TPU:0, one launch (start us, length us, event | category | flops | bytes accessed | tf_op | source)
XLA Modules:
  0.0 51.5 jit_solution(14579897092475366934)
XLA Ops:
  0.7 5.7 %spectra.1.value = bf16[4,32,1024]{2,1,0:T(8,128)(2,1)} custom-call(f32[101]{0:T(128)} %fir_taps.1, s32[16]{0:T(128)} %bins.1, s32[1]{0:T(128)S(6)} %copy.5.offsets, bf16[1408,4096]{1,0:T(8,128)(2,1)} %record.1), custom_call_target="tpu_custom_call" | custom-call | tf_op jit(solution)/shard_map/spectra/pallas_call | solution.py:118
  6.3 0.5 %collective-permute-start = (bf16[4,32,1024]{2,1,0:T(8,128)(2,1)}, bf16[4,32,1024]{2,1,0:T(8,128)(2,1)S(1)}, u32[]{:S(2)}, u32[]{:S(2)}) collective-permute-start(bf16[4,32,1024]{2,1,0:T(8,128)(2,1)} %spectra.1.value), channel_id=1, source_target_pairs={{0,1},{1,0},{2,3},{3,2},{4,5},{5,4},{6,7},{7,6},{8,9},{9,8},{10,11... | collective-permute-start | bytes 786440 | tf_op jit(solution)/shard_map/ppermute | solution.py:295
  6.8 0.9 %copy-done = bf16[4,32,1024]{2,1,0:T(8,128)(2,1)S(1)} copy-done((bf16[4,32,1024]{2,1,0:T(8,128)(2,1)S(1)}, bf16[4,32,1024]{2,1,0:T(8,128)(2,1)}, u32[]{:S(2)}) %copy-start) | copy-done | bytes 262168
  7.8 0.4 collective-permute-done.other
  8.2 0.1 pair_windows.1
  8.3 3.9 %collective-permute-start.4 = (bf16[64,1024]{1,0:T(8,128)(2,1)S(1)}, bf16[64,1024]{1,0:T(8,128)(2,1)S(1)}, u32[]{:S(2)}, u32[]{:S(2)}) collective-permute-start(bf16[64,1024]{1,0:T(8,128)(2,1)S(1)} %get-tuple-element.10), channel_id=1, source_target_pairs={{0,24},{1,7},{2,26},{3,5},{4,28},{5,3},{6,30},{7,1},{8,16},{9,15},... | collective-permute-start | bytes 393224 | tf_op jit(solution)/shard_map/ppermute | solution.py:295
  12.2 0.5 collective-permute-start.8
  12.7 0.1 collective-permute-start.12
  12.8 3.0 %collective-permute-start.1 = (bf16[64,1024]{1,0:T(8,128)(2,1)S(1)}, bf16[64,1024]{1,0:T(8,128)(2,1)S(1)}, u32[]{:S(2)}, u32[]{:S(2)}) collective-permute-start(bf16[64,1024]{1,0:T(8,128)(2,1)S(1)} %get-tuple-element.9.refs_0_), channel_id=1, source_target_pairs={{0,4},{1,17},{2,6},{3,19},{4,0},{5,21},{6,2},{7,23},{8,12},{9,25},... | collective-permute-start | bytes 393224 | tf_op jit(solution)/shard_map/ppermute | solution.py:295
  15.8 1.6 %collective-permute-start.2 = (bf16[64,1024]{1,0:T(8,128)(2,1)S(1)}, bf16[64,1024]{1,0:T(8,128)(2,1)S(1)}, u32[]{:S(2)}, u32[]{:S(2)}) collective-permute-start(bf16[64,1024]{1,0:T(8,128)(2,1)S(1)} %get-tuple-element.9.refs_0_), channel_id=1, source_target_pairs={{0,2},{1,9},{2,0},{3,11},{4,6},{5,13},{6,4},{7,15},{8,10},{9,1},{1... | collective-permute-start | bytes 393224 | tf_op jit(solution)/shard_map/ppermute | solution.py:295
  17.4 0.5 collective-permute-start.6
  17.8 0.4 collective-permute-done.8.refs_0_
  18.2 2.8 %collective-permute-start.9 = (bf16[64,1024]{1,0:T(8,128)(2,1)S(1)}, bf16[64,1024]{1,0:T(8,128)(2,1)S(1)}, u32[]{:S(2)}, u32[]{:S(2)}) collective-permute-start(bf16[64,1024]{1,0:T(8,128)(2,1)S(1)} %collective-permute-done.8.refs_0_), channel_id=1, source_target_pairs={{0,4},{1,17},{2,6},{3,19},{4,0},{5,21},{6,2},{7,23},{8,12},{9,25},... | collective-permute-start | bytes 393224 | tf_op jit(solution)/shard_map/ppermute | solution.py:295
  21.0 0.1 collective-permute-start.5
  21.2 0.6 %collective-permute-done.1.refs_1_ = bf16[64,1024]{1,0:T(8,128)(2,1)S(1)} collective-permute-done((bf16[64,1024]{1,0:T(8,128)(2,1)S(1)}, bf16[64,1024]{1,0:T(8,128)(2,1)S(1)}, u32[]{:S(2)}, u32[]{:S(2)}) %collective-permute-start.1) | collective-permute-done | bytes 131104 | tf_op jit(solution)/shard_map/ppermute | solution.py:295
  21.7 1.1 %collective-permute-start.3 = (bf16[64,1024]{1,0:T(8,128)(2,1)S(1)}, bf16[64,1024]{1,0:T(8,128)(2,1)S(1)}, u32[]{:S(2)}, u32[]{:S(2)}) collective-permute-start(bf16[64,1024]{1,0:T(8,128)(2,1)S(1)} %collective-permute-done.1.refs_1_), channel_id=1, source_target_pairs={{0,2},{1,9},{2,0},{3,11},{4,6},{5,13},{6,4},{7,15},{8,10},{9,1},{1... | collective-permute-start | bytes 393224 | tf_op jit(solution)/shard_map/ppermute | solution.py:295
  22.9 2.0 %collective-permute-done.6.refs_2_.refs_1_ = bf16[64,1024]{1,0:T(8,128)(2,1)S(1)} collective-permute-done((bf16[64,1024]{1,0:T(8,128)(2,1)S(1)}, bf16[64,1024]{1,0:T(8,128)(2,1)S(1)}, u32[]{:S(2)}, u32[]{:S(2)}) %collective-permute-start.6) | collective-permute-done | bytes 131104 | tf_op jit(solution)/shard_map/ppermute | solution.py:295
  24.8 0.6 %collective-permute-start.13 = (bf16[64,1024]{1,0:T(8,128)(2,1)S(1)}, bf16[64,1024]{1,0:T(8,128)(2,1)S(1)}, u32[]{:S(2)}, u32[]{:S(2)}) collective-permute-start(bf16[64,1024]{1,0:T(8,128)(2,1)S(1)} %hold.3.refs_0_), channel_id=1, source_target_pairs={{0,4},{1,17},{2,6},{3,19},{4,0},{5,21},{6,2},{7,23},{8,12},{9,25},... | collective-permute-start | bytes 393224 | tf_op jit(solution)/shard_map/ppermute | solution.py:295
  25.5 1.0 %collective-permute-start.10 = (bf16[64,1024]{1,0:T(8,128)(2,1)S(1)}, bf16[64,1024]{1,0:T(8,128)(2,1)S(1)}, u32[]{:S(2)}, u32[]{:S(2)}) collective-permute-start(bf16[64,1024]{1,0:T(8,128)(2,1)S(1)} %collective-permute-done.8.refs_0_), channel_id=1, source_target_pairs={{0,2},{1,9},{2,0},{3,11},{4,6},{5,13},{6,4},{7,15},{8,10},{9,1},{1... | collective-permute-start | bytes 393224 | tf_op jit(solution)/shard_map/ppermute | solution.py:295
  26.4 1.4 %collective-permute-start.11 = (bf16[64,1024]{1,0:T(8,128)(2,1)S(1)}, bf16[64,1024]{1,0:T(8,128)(2,1)S(1)}, u32[]{:S(2)}, u32[]{:S(2)}) collective-permute-start(bf16[64,1024]{1,0:T(8,128)(2,1)S(1)} %collective-permute-done.9.refs_1_), channel_id=1, source_target_pairs={{0,2},{1,9},{2,0},{3,11},{4,6},{5,13},{6,4},{7,15},{8,10},{9,1},{1... | collective-permute-start | bytes 393224 | tf_op jit(solution)/shard_map/ppermute | solution.py:295
  27.8 0.6 %collective-permute-done.5.refs_1_ = bf16[64,1024]{1,0:T(8,128)(2,1)S(1)} collective-permute-done((bf16[64,1024]{1,0:T(8,128)(2,1)S(1)}, bf16[64,1024]{1,0:T(8,128)(2,1)S(1)}, u32[]{:S(2)}, u32[]{:S(2)}) %collective-permute-start.5) | collective-permute-done | bytes 131104 | tf_op jit(solution)/shard_map/ppermute | solution.py:295
  28.4 2.2 %collective-permute-start.7 = (bf16[64,1024]{1,0:T(8,128)(2,1)S(1)}, bf16[64,1024]{1,0:T(8,128)(2,1)S(1)}, u32[]{:S(2)}, u32[]{:S(2)}) collective-permute-start(bf16[64,1024]{1,0:T(8,128)(2,1)S(1)} %collective-permute-done.5.refs_1_), channel_id=1, source_target_pairs={{0,2},{1,9},{2,0},{3,11},{4,6},{5,13},{6,4},{7,15},{8,10},{9,1},{1... | collective-permute-start | bytes 393224 | tf_op jit(solution)/shard_map/ppermute | solution.py:295
  30.7 1.4 %collective-permute-done.13.refs_1_ = bf16[64,1024]{1,0:T(8,128)(2,1)S(1)} collective-permute-done((bf16[64,1024]{1,0:T(8,128)(2,1)S(1)}, bf16[64,1024]{1,0:T(8,128)(2,1)S(1)}, u32[]{:S(2)}, u32[]{:S(2)}) %collective-permute-start.13) | collective-permute-done | bytes 131104 | tf_op jit(solution)/shard_map/ppermute | solution.py:295
  32.1 0.6 %collective-permute-start.15 = (bf16[64,1024]{1,0:T(8,128)(2,1)S(1)}, bf16[64,1024]{1,0:T(8,128)(2,1)S(1)}, u32[]{:S(2)}, u32[]{:S(2)}) collective-permute-start(bf16[64,1024]{1,0:T(8,128)(2,1)S(1)} %collective-permute-done.13.refs_1_), channel_id=1, source_target_pairs={{0,2},{1,9},{2,0},{3,11},{4,6},{5,13},{6,4},{7,15},{8,10},{9,1},{1... | collective-permute-start | bytes 393224 | tf_op jit(solution)/shard_map/ppermute | solution.py:295
  32.7 0.1 collective-permute-start.16
  32.8 0.4 collective-permute-done.11.refs_3_
  33.3 0.1 collective-permute-start.18
  33.4 1.2 %collective-permute-done.7.refs_3_ = bf16[64,1024]{1,0:T(8,128)(2,1)S(1)} collective-permute-done((bf16[64,1024]{1,0:T(8,128)(2,1)S(1)}, bf16[64,1024]{1,0:T(8,128)(2,1)S(1)}, u32[]{:S(2)}, u32[]{:S(2)}) %collective-permute-start.7) | collective-permute-done | bytes 131104 | tf_op jit(solution)/shard_map/ppermute | solution.py:295
  34.8 1.3 %collective-permute-done.14.refs_2_ = bf16[64,1024]{1,0:T(8,128)(2,1)S(1)} collective-permute-done((bf16[64,1024]{1,0:T(8,128)(2,1)S(1)}, bf16[64,1024]{1,0:T(8,128)(2,1)S(1)}, u32[]{:S(2)}, u32[]{:S(2)}) %collective-permute-start.14) | collective-permute-done | bytes 131104 | tf_op jit(solution)/shard_map/ppermute | solution.py:295
  36.1 1.4 %collective-permute-done.15.refs_3_ = bf16[64,1024]{1,0:T(8,128)(2,1)S(1)} collective-permute-done((bf16[64,1024]{1,0:T(8,128)(2,1)S(1)}, bf16[64,1024]{1,0:T(8,128)(2,1)S(1)}, u32[]{:S(2)}, u32[]{:S(2)}) %collective-permute-start.15) | collective-permute-done | bytes 131104 | tf_op jit(solution)/shard_map/ppermute | solution.py:295
  37.6 1.9 %collective-permute-done.19.refs_7_ = bf16[256,1024]{1,0:T(8,128)(2,1)S(1)} collective-permute-done((bf16[256,1024]{1,0:T(8,128)(2,1)S(1)}, bf16[256,1024]{1,0:T(8,128)(2,1)S(1)}, u32[]{:S(2)}, u32[]{:S(2)}) %collective-permute-start.19) | collective-permute-done | bytes 524320 | tf_op jit(solution)/shard_map/ppermute | solution.py:295
  39.5 12.0 %products.1 = bf16[16,2,1024,512]{3,2,1,0:T(8,128)(2,1)} custom-call(bf16[256,1024]{1,0:T(8,128)(2,1)S(1)} %pack.4.refs_0_, bf16[256,1024]{1,0:T(8,128)(2,1)S(1)} %pack.5.refs_1_, bf16[256,1024]{1,0:T(8,128)(2,1)S(1)} %pack.6.refs_2_, bf16[256,1024]{1,0:T(8,128)(2,1)S(1)} %pack.7.refs_3_, bf16[256,1024]{1,0:T(8,128)(2,1)S(1)} %collective-permute-done.16.refs_4_, ...), custom_call_target="tpu_custom_call" | custom-call | flops 8589934592 | bytes 33554432 | tf_op jit(solution)/shard_map/products/pallas_call | solution.py:261
  (19 shorter events, 0.4 us)
Async XLA Ops:
  6.3 1.9 %collective-permute-start = (bf16[4,32,1024]{2,1,0:T(8,128)(2,1)}, bf16[4,32,1024]{2,1,0:T(8,128)(2,1)S(1)}, u32[]{:S(2)}, u32[]{:S(2)}) collective-permute-start(bf16[4,32,1024]{2,1,0:T(8,128)(2,1)} %spectra.1.value), channel_id=1, source_target_pairs={{0,1},{1,0},{2,3},{3,2},{4,5},{5,4},{6,7},{7,6},{8,9},{9,8},{10,11... | collective-permute-start | bytes 786440 | tf_op jit(solution)/shard_map/ppermute | solution.py:295
  6.8 0.9 %copy-start = (bf16[4,32,1024]{2,1,0:T(8,128)(2,1)S(1)}, bf16[4,32,1024]{2,1,0:T(8,128)(2,1)}, u32[]{:S(2)}) copy-start(bf16[4,32,1024]{2,1,0:T(8,128)(2,1)} %spectra.1.value) | copy-start | bytes 786436
  8.3 9.1 %collective-permute-start.4 = (bf16[64,1024]{1,0:T(8,128)(2,1)S(1)}, bf16[64,1024]{1,0:T(8,128)(2,1)S(1)}, u32[]{:S(2)}, u32[]{:S(2)}) collective-permute-start(bf16[64,1024]{1,0:T(8,128)(2,1)S(1)} %get-tuple-element.10), channel_id=1, source_target_pairs={{0,24},{1,7},{2,26},{3,5},{4,28},{5,3},{6,30},{7,1},{8,16},{9,15},... | collective-permute-start | bytes 393224 | tf_op jit(solution)/shard_map/ppermute | solution.py:295
  12.2 6.1 %collective-permute-start.8 = (bf16[64,1024]{1,0:T(8,128)(2,1)S(1)}, bf16[64,1024]{1,0:T(8,128)(2,1)S(1)}, u32[]{:S(2)}, u32[]{:S(2)}) collective-permute-start(bf16[64,1024]{1,0:T(8,128)(2,1)S(1)} %get-tuple-element.11), channel_id=1, source_target_pairs={{0,16},{1,5},{2,18},{3,7},{4,20},{5,1},{6,22},{7,3},{8,24},{9,13},... | collective-permute-start | bytes 393224 | tf_op jit(solution)/shard_map/ppermute | solution.py:295
  12.7 8.4 %collective-permute-start.12 = (bf16[64,1024]{1,0:T(8,128)(2,1)S(1)}, bf16[64,1024]{1,0:T(8,128)(2,1)S(1)}, u32[]{:S(2)}, u32[]{:S(2)}) collective-permute-start(bf16[64,1024]{1,0:T(8,128)(2,1)S(1)} %get-tuple-element.12), channel_id=1, source_target_pairs={{0,8},{1,3},{2,10},{3,1},{4,12},{5,7},{6,14},{7,5},{8,0},{9,11},{1... | collective-permute-start | bytes 393224 | tf_op jit(solution)/shard_map/ppermute | solution.py:295
  12.8 8.9 %collective-permute-start.1 = (bf16[64,1024]{1,0:T(8,128)(2,1)S(1)}, bf16[64,1024]{1,0:T(8,128)(2,1)S(1)}, u32[]{:S(2)}, u32[]{:S(2)}) collective-permute-start(bf16[64,1024]{1,0:T(8,128)(2,1)S(1)} %get-tuple-element.9.refs_0_), channel_id=1, source_target_pairs={{0,4},{1,17},{2,6},{3,19},{4,0},{5,21},{6,2},{7,23},{8,12},{9,25},... | collective-permute-start | bytes 393224 | tf_op jit(solution)/shard_map/ppermute | solution.py:295
  15.8 7.0 %collective-permute-start.2 = (bf16[64,1024]{1,0:T(8,128)(2,1)S(1)}, bf16[64,1024]{1,0:T(8,128)(2,1)S(1)}, u32[]{:S(2)}, u32[]{:S(2)}) collective-permute-start(bf16[64,1024]{1,0:T(8,128)(2,1)S(1)} %get-tuple-element.9.refs_0_), channel_id=1, source_target_pairs={{0,2},{1,9},{2,0},{3,11},{4,6},{5,13},{6,4},{7,15},{8,10},{9,1},{1... | collective-permute-start | bytes 393224 | tf_op jit(solution)/shard_map/ppermute | solution.py:295
  17.4 7.4 %collective-permute-start.6 = (bf16[64,1024]{1,0:T(8,128)(2,1)S(1)}, bf16[64,1024]{1,0:T(8,128)(2,1)S(1)}, u32[]{:S(2)}, u32[]{:S(2)}) collective-permute-start(bf16[64,1024]{1,0:T(8,128)(2,1)S(1)} %collective-permute-done.4.refs_0_), channel_id=1, source_target_pairs={{0,2},{1,9},{2,0},{3,11},{4,6},{5,13},{6,4},{7,15},{8,10},{9,1},{1... | collective-permute-start | bytes 393224 | tf_op jit(solution)/shard_map/ppermute | solution.py:295
  18.2 8.2 %collective-permute-start.9 = (bf16[64,1024]{1,0:T(8,128)(2,1)S(1)}, bf16[64,1024]{1,0:T(8,128)(2,1)S(1)}, u32[]{:S(2)}, u32[]{:S(2)}) collective-permute-start(bf16[64,1024]{1,0:T(8,128)(2,1)S(1)} %collective-permute-done.8.refs_0_), channel_id=1, source_target_pairs={{0,4},{1,17},{2,6},{3,19},{4,0},{5,21},{6,2},{7,23},{8,12},{9,25},... | collective-permute-start | bytes 393224 | tf_op jit(solution)/shard_map/ppermute | solution.py:295
  21.0 7.4 %collective-permute-start.5 = (bf16[64,1024]{1,0:T(8,128)(2,1)S(1)}, bf16[64,1024]{1,0:T(8,128)(2,1)S(1)}, u32[]{:S(2)}, u32[]{:S(2)}) collective-permute-start(bf16[64,1024]{1,0:T(8,128)(2,1)S(1)} %collective-permute-done.4.refs_0_), channel_id=1, source_target_pairs={{0,4},{1,17},{2,6},{3,19},{4,0},{5,21},{6,2},{7,23},{8,12},{9,25},... | collective-permute-start | bytes 393224 | tf_op jit(solution)/shard_map/ppermute | solution.py:295
  21.7 8.9 %collective-permute-start.3 = (bf16[64,1024]{1,0:T(8,128)(2,1)S(1)}, bf16[64,1024]{1,0:T(8,128)(2,1)S(1)}, u32[]{:S(2)}, u32[]{:S(2)}) collective-permute-start(bf16[64,1024]{1,0:T(8,128)(2,1)S(1)} %collective-permute-done.1.refs_1_), channel_id=1, source_target_pairs={{0,2},{1,9},{2,0},{3,11},{4,6},{5,13},{6,4},{7,15},{8,10},{9,1},{1... | collective-permute-start | bytes 393224 | tf_op jit(solution)/shard_map/ppermute | solution.py:295
  24.8 7.3 %collective-permute-start.13 = (bf16[64,1024]{1,0:T(8,128)(2,1)S(1)}, bf16[64,1024]{1,0:T(8,128)(2,1)S(1)}, u32[]{:S(2)}, u32[]{:S(2)}) collective-permute-start(bf16[64,1024]{1,0:T(8,128)(2,1)S(1)} %hold.3.refs_0_), channel_id=1, source_target_pairs={{0,4},{1,17},{2,6},{3,19},{4,0},{5,21},{6,2},{7,23},{8,12},{9,25},... | collective-permute-start | bytes 393224 | tf_op jit(solution)/shard_map/ppermute | solution.py:295
  25.5 7.3 %collective-permute-start.10 = (bf16[64,1024]{1,0:T(8,128)(2,1)S(1)}, bf16[64,1024]{1,0:T(8,128)(2,1)S(1)}, u32[]{:S(2)}, u32[]{:S(2)}) collective-permute-start(bf16[64,1024]{1,0:T(8,128)(2,1)S(1)} %collective-permute-done.8.refs_0_), channel_id=1, source_target_pairs={{0,2},{1,9},{2,0},{3,11},{4,6},{5,13},{6,4},{7,15},{8,10},{9,1},{1... | collective-permute-start | bytes 393224 | tf_op jit(solution)/shard_map/ppermute | solution.py:295
  26.4 6.8 %collective-permute-start.11 = (bf16[64,1024]{1,0:T(8,128)(2,1)S(1)}, bf16[64,1024]{1,0:T(8,128)(2,1)S(1)}, u32[]{:S(2)}, u32[]{:S(2)}) collective-permute-start(bf16[64,1024]{1,0:T(8,128)(2,1)S(1)} %collective-permute-done.9.refs_1_), channel_id=1, source_target_pairs={{0,2},{1,9},{2,0},{3,11},{4,6},{5,13},{6,4},{7,15},{8,10},{9,1},{1... | collective-permute-start | bytes 393224 | tf_op jit(solution)/shard_map/ppermute | solution.py:295
  28.4 6.2 %collective-permute-start.7 = (bf16[64,1024]{1,0:T(8,128)(2,1)S(1)}, bf16[64,1024]{1,0:T(8,128)(2,1)S(1)}, u32[]{:S(2)}, u32[]{:S(2)}) collective-permute-start(bf16[64,1024]{1,0:T(8,128)(2,1)S(1)} %collective-permute-done.5.refs_1_), channel_id=1, source_target_pairs={{0,2},{1,9},{2,0},{3,11},{4,6},{5,13},{6,4},{7,15},{8,10},{9,1},{1... | collective-permute-start | bytes 393224 | tf_op jit(solution)/shard_map/ppermute | solution.py:295
  30.7 5.4 %collective-permute-start.14 = (bf16[64,1024]{1,0:T(8,128)(2,1)S(1)}, bf16[64,1024]{1,0:T(8,128)(2,1)S(1)}, u32[]{:S(2)}, u32[]{:S(2)}) collective-permute-start(bf16[64,1024]{1,0:T(8,128)(2,1)S(1)} %hold.3.refs_0_), channel_id=1, source_target_pairs={{0,2},{1,9},{2,0},{3,11},{4,6},{5,13},{6,4},{7,15},{8,10},{9,1},{1... | collective-permute-start | bytes 393224 | tf_op jit(solution)/shard_map/ppermute | solution.py:295
  32.1 5.3 %collective-permute-start.15 = (bf16[64,1024]{1,0:T(8,128)(2,1)S(1)}, bf16[64,1024]{1,0:T(8,128)(2,1)S(1)}, u32[]{:S(2)}, u32[]{:S(2)}) collective-permute-start(bf16[64,1024]{1,0:T(8,128)(2,1)S(1)} %collective-permute-done.13.refs_1_), channel_id=1, source_target_pairs={{0,2},{1,9},{2,0},{3,11},{4,6},{5,13},{6,4},{7,15},{8,10},{9,1},{1... | collective-permute-start | bytes 393224 | tf_op jit(solution)/shard_map/ppermute | solution.py:295
  32.7 4.9 %collective-permute-start.16 = (bf16[256,1024]{1,0:T(8,128)(2,1)S(1)}, bf16[256,1024]{1,0:T(8,128)(2,1)S(1)}, u32[]{:S(2)}, u32[]{:S(2)}) collective-permute-start(bf16[256,1024]{1,0:T(8,128)(2,1)S(1)} %pack.4.refs_0_), channel_id=1, source_target_pairs={{0,1},{1,0},{2,3},{3,2},{4,5},{5,4},{6,7},{7,6},{8,9},{9,8},{10,11... | collective-permute-start | bytes 1572872 | tf_op jit(solution)/shard_map/ppermute | solution.py:295
  33.3 4.3 %collective-permute-start.18 = (bf16[256,1024]{1,0:T(8,128)(2,1)S(1)}, bf16[256,1024]{1,0:T(8,128)(2,1)S(1)}, u32[]{:S(2)}, u32[]{:S(2)}) collective-permute-start(bf16[256,1024]{1,0:T(8,128)(2,1)S(1)} %pack.6.refs_2_), channel_id=1, source_target_pairs={{0,1},{1,0},{2,3},{3,2},{4,5},{5,4},{6,7},{7,6},{8,9},{9,8},{10,11... | collective-permute-start | bytes 1572872 | tf_op jit(solution)/shard_map/ppermute | solution.py:295
  34.7 2.9 %collective-permute-start.17 = (bf16[256,1024]{1,0:T(8,128)(2,1)S(1)}, bf16[256,1024]{1,0:T(8,128)(2,1)S(1)}, u32[]{:S(2)}, u32[]{:S(2)}) collective-permute-start(bf16[256,1024]{1,0:T(8,128)(2,1)S(1)} %pack.5.refs_1_), channel_id=1, source_target_pairs={{0,1},{1,0},{2,3},{3,2},{4,5},{5,4},{6,7},{7,6},{8,9},{9,8},{10,11... | collective-permute-start | bytes 1572872 | tf_op jit(solution)/shard_map/ppermute | solution.py:295
  37.5 2.0 %collective-permute-start.19 = (bf16[256,1024]{1,0:T(8,128)(2,1)S(1)}, bf16[256,1024]{1,0:T(8,128)(2,1)S(1)}, u32[]{:S(2)}, u32[]{:S(2)}) collective-permute-start(bf16[256,1024]{1,0:T(8,128)(2,1)S(1)} %pack.7.refs_3_), channel_id=1, source_target_pairs={{0,1},{1,0},{2,3},{3,2},{4,5},{5,4},{6,7},{7,6},{8,9},{9,8},{10,11... | collective-permute-start | bytes 1572872 | tf_op jit(solution)/shard_map/ppermute | solution.py:295

commit v6 on v5

--- a/solution.py
+++ b/solution.py
@@ -308,7 +308,7 @@
     packs, places, early = [], {}, []
     for step, piece in pieces.items():
         if step == turns[-1]:
-            piece = hold(piece, early[:2])
+            piece = hold(piece, early[1:2])
         held = {0: piece}
         for bit in bits:
             for slot in list(held):

time: 51.6 us -> 51.2 us (level)
  waiting for transfers between devices: 11.6 us -> 7.95 us
  starting transfers between devices: 20.2 us -> 23.5 us
    ppermute x20, waiting for transfers between devices: 11.6 us -> 7.95 us  [send(): return lax.ppermute(value, AXES, pairs)]
    ppermute x20, starting transfers between devices: 20.2 us -> 23.5 us  [send(): return lax.ppermute(value, AXES, pairs)]
  transfers between devices with their start and end apart: 20 -> 20, of which waited for: 11 -> 9; matrix products, arithmetic and copies ran while one was open for 0% -> 0% of each run, Pallas kernels for 0% -> 0%
where the time goes in v6:
time: 51.2 us; the launch traced here: 51 us
  starting transfers between devices  23.5 us (46%)
  Pallas kernels  17.9 us (35%)
  waiting for transfers between devices  7.95 us (16%)
  local copies, waits for them, and re-layouts  0.95 us (2%)
  between operations  0.77 us (2%)
    ppermute x20, starting transfers between devices, send(): return lax.ppermute(value, AXES, pairs)  23.5 us
    pallas_call x1, Pallas kernels, multiply(): pl.pallas_call(functools.partial(product_body, count, windows, places), o...  12 us
    ppermute x20, waiting for transfers between devices, send(): return lax.ppermute(value, AXES, pairs)  7.95 us
    pallas_call x1, Pallas kernels, make_spectra(): pl.pallas_call(spectra_body, out_shape=jax.ShapeDtypeStruct((slices, ROWS...  5.66 us
  transfers between devices with their start and end apart: 20, of which 9 were waited for; matrix products, arithmetic and copies ran while one was open for 0% of the time, Pallas kernels for 0%

profile of v6, /device:TPU:0, one launch (start us, length us, event | category | flops | bytes accessed | tf_op | source)
XLA Modules:
  0.0 51.0 jit_solution(3194036365538712363)
XLA Ops:
  0.7 5.7 %spectra.1.value = bf16[4,32,1024]{2,1,0:T(8,128)(2,1)} custom-call(f32[101]{0:T(128)} %fir_taps.1, s32[16]{0:T(128)} %bins.1, s32[1]{0:T(128)S(6)} %copy.5.offsets, bf16[1408,4096]{1,0:T(8,128)(2,1)} %record.1), custom_call_target="tpu_custom_call" | custom-call | tf_op jit(solution)/shard_map/spectra/pallas_call | solution.py:118
  6.3 0.5 %collective-permute-start = (bf16[4,32,1024]{2,1,0:T(8,128)(2,1)}, bf16[4,32,1024]{2,1,0:T(8,128)(2,1)S(1)}, u32[]{:S(2)}, u32[]{:S(2)}) collective-permute-start(bf16[4,32,1024]{2,1,0:T(8,128)(2,1)} %spectra.1.value), channel_id=1, source_target_pairs={{0,1},{1,0},{2,3},{3,2},{4,5},{5,4},{6,7},{7,6},{8,9},{9,8},{10,11... | collective-permute-start | bytes 786440 | tf_op jit(solution)/shard_map/ppermute | solution.py:295
  6.8 0.9 %copy-done = bf16[4,32,1024]{2,1,0:T(8,128)(2,1)S(1)} copy-done((bf16[4,32,1024]{2,1,0:T(8,128)(2,1)S(1)}, bf16[4,32,1024]{2,1,0:T(8,128)(2,1)}, u32[]{:S(2)}) %copy-start) | copy-done | bytes 262168
  7.8 0.4 collective-permute-done.other
  8.2 0.1 pair_windows.1
  8.3 3.9 %collective-permute-start.4 = (bf16[64,1024]{1,0:T(8,128)(2,1)S(1)}, bf16[64,1024]{1,0:T(8,128)(2,1)S(1)}, u32[]{:S(2)}, u32[]{:S(2)}) collective-permute-start(bf16[64,1024]{1,0:T(8,128)(2,1)S(1)} %get-tuple-element.10), channel_id=1, source_target_pairs={{0,24},{1,7},{2,26},{3,5},{4,28},{5,3},{6,30},{7,1},{8,16},{9,15},... | collective-permute-start | bytes 393224 | tf_op jit(solution)/shard_map/ppermute | solution.py:295
  12.2 0.5 collective-permute-start.8
  12.7 0.1 collective-permute-start.12
  12.8 3.0 %collective-permute-start.1 = (bf16[64,1024]{1,0:T(8,128)(2,1)S(1)}, bf16[64,1024]{1,0:T(8,128)(2,1)S(1)}, u32[]{:S(2)}, u32[]{:S(2)}) collective-permute-start(bf16[64,1024]{1,0:T(8,128)(2,1)S(1)} %get-tuple-element.9.refs_0_), channel_id=1, source_target_pairs={{0,4},{1,17},{2,6},{3,19},{4,0},{5,21},{6,2},{7,23},{8,12},{9,25},... | collective-permute-start | bytes 393224 | tf_op jit(solution)/shard_map/ppermute | solution.py:295
  15.8 1.6 %collective-permute-start.6 = (bf16[64,1024]{1,0:T(8,128)(2,1)S(1)}, bf16[64,1024]{1,0:T(8,128)(2,1)S(1)}, u32[]{:S(2)}, u32[]{:S(2)}) collective-permute-start(bf16[64,1024]{1,0:T(8,128)(2,1)S(1)} %collective-permute-done.4.refs_0_), channel_id=1, source_target_pairs={{0,2},{1,9},{2,0},{3,11},{4,6},{5,13},{6,4},{7,15},{8,10},{9,1},{1... | collective-permute-start | bytes 393224 | tf_op jit(solution)/shard_map/ppermute | solution.py:295
  17.4 0.5 collective-permute-start.2
  17.8 0.4 collective-permute-done.8.refs_0_
  18.2 2.8 %collective-permute-start.9 = (bf16[64,1024]{1,0:T(8,128)(2,1)S(1)}, bf16[64,1024]{1,0:T(8,128)(2,1)S(1)}, u32[]{:S(2)}, u32[]{:S(2)}) collective-permute-start(bf16[64,1024]{1,0:T(8,128)(2,1)S(1)} %collective-permute-done.8.refs_0_), channel_id=1, source_target_pairs={{0,4},{1,17},{2,6},{3,19},{4,0},{5,21},{6,2},{7,23},{8,12},{9,25},... | collective-permute-start | bytes 393224 | tf_op jit(solution)/shard_map/ppermute | solution.py:295
  21.0 0.1 collective-permute-start.5
  21.2 0.6 %collective-permute-done.1.refs_1_ = bf16[64,1024]{1,0:T(8,128)(2,1)S(1)} collective-permute-done((bf16[64,1024]{1,0:T(8,128)(2,1)S(1)}, bf16[64,1024]{1,0:T(8,128)(2,1)S(1)}, u32[]{:S(2)}, u32[]{:S(2)}) %collective-permute-start.1) | collective-permute-done | bytes 131104 | tf_op jit(solution)/shard_map/ppermute | solution.py:295
  21.7 1.1 %collective-permute-start.3 = (bf16[64,1024]{1,0:T(8,128)(2,1)S(1)}, bf16[64,1024]{1,0:T(8,128)(2,1)S(1)}, u32[]{:S(2)}, u32[]{:S(2)}) collective-permute-start(bf16[64,1024]{1,0:T(8,128)(2,1)S(1)} %collective-permute-done.1.refs_1_), channel_id=1, source_target_pairs={{0,2},{1,9},{2,0},{3,11},{4,6},{5,13},{6,4},{7,15},{8,10},{9,1},{1... | collective-permute-start | bytes 393224 | tf_op jit(solution)/shard_map/ppermute | solution.py:295
  22.9 2.6 %collective-permute-start.13 = (bf16[64,1024]{1,0:T(8,128)(2,1)S(1)}, bf16[64,1024]{1,0:T(8,128)(2,1)S(1)}, u32[]{:S(2)}, u32[]{:S(2)}) collective-permute-start(bf16[64,1024]{1,0:T(8,128)(2,1)S(1)} %hold.3.refs_0_), channel_id=1, source_target_pairs={{0,4},{1,17},{2,6},{3,19},{4,0},{5,21},{6,2},{7,23},{8,12},{9,25},... | collective-permute-start | bytes 393224 | tf_op jit(solution)/shard_map/ppermute | solution.py:295
  25.5 0.6 %collective-permute-start.10 = (bf16[64,1024]{1,0:T(8,128)(2,1)S(1)}, bf16[64,1024]{1,0:T(8,128)(2,1)S(1)}, u32[]{:S(2)}, u32[]{:S(2)}) collective-permute-start(bf16[64,1024]{1,0:T(8,128)(2,1)S(1)} %collective-permute-done.8.refs_0_), channel_id=1, source_target_pairs={{0,2},{1,9},{2,0},{3,11},{4,6},{5,13},{6,4},{7,15},{8,10},{9,1},{1... | collective-permute-start | bytes 393224 | tf_op jit(solution)/shard_map/ppermute | solution.py:295
  26.1 1.7 %collective-permute-start.11 = (bf16[64,1024]{1,0:T(8,128)(2,1)S(1)}, bf16[64,1024]{1,0:T(8,128)(2,1)S(1)}, u32[]{:S(2)}, u32[]{:S(2)}) collective-permute-start(bf16[64,1024]{1,0:T(8,128)(2,1)S(1)} %collective-permute-done.9.refs_1_), channel_id=1, source_target_pairs={{0,2},{1,9},{2,0},{3,11},{4,6},{5,13},{6,4},{7,15},{8,10},{9,1},{1... | collective-permute-start | bytes 393224 | tf_op jit(solution)/shard_map/ppermute | solution.py:295
  27.8 0.6 %collective-permute-done.5.refs_1_ = bf16[64,1024]{1,0:T(8,128)(2,1)S(1)} collective-permute-done((bf16[64,1024]{1,0:T(8,128)(2,1)S(1)}, bf16[64,1024]{1,0:T(8,128)(2,1)S(1)}, u32[]{:S(2)}, u32[]{:S(2)}) %collective-permute-start.5) | collective-permute-done | bytes 131104 | tf_op jit(solution)/shard_map/ppermute | solution.py:295
  28.4 2.3 %collective-permute-start.7 = (bf16[64,1024]{1,0:T(8,128)(2,1)S(1)}, bf16[64,1024]{1,0:T(8,128)(2,1)S(1)}, u32[]{:S(2)}, u32[]{:S(2)}) collective-permute-start(bf16[64,1024]{1,0:T(8,128)(2,1)S(1)} %collective-permute-done.5.refs_1_), channel_id=1, source_target_pairs={{0,2},{1,9},{2,0},{3,11},{4,6},{5,13},{6,4},{7,15},{8,10},{9,1},{1... | collective-permute-start | bytes 393224 | tf_op jit(solution)/shard_map/ppermute | solution.py:295
  30.7 0.6 %collective-permute-done.13.refs_1_ = bf16[64,1024]{1,0:T(8,128)(2,1)S(1)} collective-permute-done((bf16[64,1024]{1,0:T(8,128)(2,1)S(1)}, bf16[64,1024]{1,0:T(8,128)(2,1)S(1)}, u32[]{:S(2)}, u32[]{:S(2)}) %collective-permute-start.13) | collective-permute-done | bytes 131104 | tf_op jit(solution)/shard_map/ppermute | solution.py:295
  31.3 1.4 %collective-permute-start.15 = (bf16[64,1024]{1,0:T(8,128)(2,1)S(1)}, bf16[64,1024]{1,0:T(8,128)(2,1)S(1)}, u32[]{:S(2)}, u32[]{:S(2)}) collective-permute-start(bf16[64,1024]{1,0:T(8,128)(2,1)S(1)} %collective-permute-done.13.refs_1_), channel_id=1, source_target_pairs={{0,2},{1,9},{2,0},{3,11},{4,6},{5,13},{6,4},{7,15},{8,10},{9,1},{1... | collective-permute-start | bytes 393224 | tf_op jit(solution)/shard_map/ppermute | solution.py:295
  32.7 0.1 collective-permute-start.16
  32.9 0.5 %collective-permute-start.18 = (bf16[256,1024]{1,0:T(8,128)(2,1)S(1)}, bf16[256,1024]{1,0:T(8,128)(2,1)S(1)}, u32[]{:S(2)}, u32[]{:S(2)}) collective-permute-start(bf16[256,1024]{1,0:T(8,128)(2,1)S(1)} %pack.6.refs_2_), channel_id=1, source_target_pairs={{0,1},{1,0},{2,3},{3,2},{4,5},{5,4},{6,7},{7,6},{8,9},{9,8},{10,11... | collective-permute-start | bytes 1572872 | tf_op jit(solution)/shard_map/ppermute | solution.py:295
  33.4 0.6 %collective-permute-done.7.refs_3_ = bf16[64,1024]{1,0:T(8,128)(2,1)S(1)} collective-permute-done((bf16[64,1024]{1,0:T(8,128)(2,1)S(1)}, bf16[64,1024]{1,0:T(8,128)(2,1)S(1)}, u32[]{:S(2)}, u32[]{:S(2)}) %collective-permute-start.7) | collective-permute-done | bytes 131104 | tf_op jit(solution)/shard_map/ppermute | solution.py:295
  34.0 0.1 collective-permute-start.17
  34.1 1.5 %collective-permute-done.14.refs_2_ = bf16[64,1024]{1,0:T(8,128)(2,1)S(1)} collective-permute-done((bf16[64,1024]{1,0:T(8,128)(2,1)S(1)}, bf16[64,1024]{1,0:T(8,128)(2,1)S(1)}, u32[]{:S(2)}, u32[]{:S(2)}) %collective-permute-start.14) | collective-permute-done | bytes 131104 | tf_op jit(solution)/shard_map/ppermute | solution.py:295
  35.6 1.4 %collective-permute-done.15.refs_3_ = bf16[64,1024]{1,0:T(8,128)(2,1)S(1)} collective-permute-done((bf16[64,1024]{1,0:T(8,128)(2,1)S(1)}, bf16[64,1024]{1,0:T(8,128)(2,1)S(1)}, u32[]{:S(2)}, u32[]{:S(2)}) %collective-permute-start.15) | collective-permute-done | bytes 131104 | tf_op jit(solution)/shard_map/ppermute | solution.py:295
  37.1 0.1 collective-permute-start.19
  37.2 1.9 %collective-permute-done.19.refs_7_ = bf16[256,1024]{1,0:T(8,128)(2,1)S(1)} collective-permute-done((bf16[256,1024]{1,0:T(8,128)(2,1)S(1)}, bf16[256,1024]{1,0:T(8,128)(2,1)S(1)}, u32[]{:S(2)}, u32[]{:S(2)}) %collective-permute-start.19) | collective-permute-done | bytes 524320 | tf_op jit(solution)/shard_map/ppermute | solution.py:295
  39.0 12.0 %products.1 = bf16[16,2,1024,512]{3,2,1,0:T(8,128)(2,1)} custom-call(bf16[256,1024]{1,0:T(8,128)(2,1)S(1)} %pack.4.refs_0_, bf16[256,1024]{1,0:T(8,128)(2,1)S(1)} %pack.5.refs_1_, bf16[256,1024]{1,0:T(8,128)(2,1)S(1)} %pack.6.refs_2_, bf16[256,1024]{1,0:T(8,128)(2,1)S(1)} %pack.7.refs_3_, bf16[256,1024]{1,0:T(8,128)(2,1)S(1)} %collective-permute-done.16.refs_4_, ...), custom_call_target="tpu_custom_call" | custom-call | flops 8589934592 | bytes 33554432 | tf_op jit(solution)/shard_map/products/pallas_call | solution.py:261
  (19 shorter events, 0.2 us)
Async XLA Ops:
  6.3 1.9 %collective-permute-start = (bf16[4,32,1024]{2,1,0:T(8,128)(2,1)}, bf16[4,32,1024]{2,1,0:T(8,128)(2,1)S(1)}, u32[]{:S(2)}, u32[]{:S(2)}) collective-permute-start(bf16[4,32,1024]{2,1,0:T(8,128)(2,1)} %spectra.1.value), channel_id=1, source_target_pairs={{0,1},{1,0},{2,3},{3,2},{4,5},{5,4},{6,7},{7,6},{8,9},{9,8},{10,11... | collective-permute-start | bytes 786440 | tf_op jit(solution)/shard_map/ppermute | solution.py:295
  6.8 0.9 %copy-start = (bf16[4,32,1024]{2,1,0:T(8,128)(2,1)S(1)}, bf16[4,32,1024]{2,1,0:T(8,128)(2,1)}, u32[]{:S(2)}) copy-start(bf16[4,32,1024]{2,1,0:T(8,128)(2,1)} %spectra.1.value) | copy-start | bytes 786436
  8.3 7.5 %collective-permute-start.4 = (bf16[64,1024]{1,0:T(8,128)(2,1)S(1)}, bf16[64,1024]{1,0:T(8,128)(2,1)S(1)}, u32[]{:S(2)}, u32[]{:S(2)}) collective-permute-start(bf16[64,1024]{1,0:T(8,128)(2,1)S(1)} %get-tuple-element.10), channel_id=1, source_target_pairs={{0,24},{1,7},{2,26},{3,5},{4,28},{5,3},{6,30},{7,1},{8,16},{9,15},... | collective-permute-start | bytes 393224 | tf_op jit(solution)/shard_map/ppermute | solution.py:295
  12.2 6.1 %collective-permute-start.8 = (bf16[64,1024]{1,0:T(8,128)(2,1)S(1)}, bf16[64,1024]{1,0:T(8,128)(2,1)S(1)}, u32[]{:S(2)}, u32[]{:S(2)}) collective-permute-start(bf16[64,1024]{1,0:T(8,128)(2,1)S(1)} %get-tuple-element.11), channel_id=1, source_target_pairs={{0,16},{1,5},{2,18},{3,7},{4,20},{5,1},{6,22},{7,3},{8,24},{9,13},... | collective-permute-start | bytes 393224 | tf_op jit(solution)/shard_map/ppermute | solution.py:295
  12.7 8.4 %collective-permute-start.12 = (bf16[64,1024]{1,0:T(8,128)(2,1)S(1)}, bf16[64,1024]{1,0:T(8,128)(2,1)S(1)}, u32[]{:S(2)}, u32[]{:S(2)}) collective-permute-start(bf16[64,1024]{1,0:T(8,128)(2,1)S(1)} %get-tuple-element.12), channel_id=1, source_target_pairs={{0,8},{1,3},{2,10},{3,1},{4,12},{5,7},{6,14},{7,5},{8,0},{9,11},{1... | collective-permute-start | bytes 393224 | tf_op jit(solution)/shard_map/ppermute | solution.py:295
  12.8 8.9 %collective-permute-start.1 = (bf16[64,1024]{1,0:T(8,128)(2,1)S(1)}, bf16[64,1024]{1,0:T(8,128)(2,1)S(1)}, u32[]{:S(2)}, u32[]{:S(2)}) collective-permute-start(bf16[64,1024]{1,0:T(8,128)(2,1)S(1)} %get-tuple-element.9.refs_0_), channel_id=1, source_target_pairs={{0,4},{1,17},{2,6},{3,19},{4,0},{5,21},{6,2},{7,23},{8,12},{9,25},... | collective-permute-start | bytes 393224 | tf_op jit(solution)/shard_map/ppermute | solution.py:295
  15.8 7.0 %collective-permute-start.6 = (bf16[64,1024]{1,0:T(8,128)(2,1)S(1)}, bf16[64,1024]{1,0:T(8,128)(2,1)S(1)}, u32[]{:S(2)}, u32[]{:S(2)}) collective-permute-start(bf16[64,1024]{1,0:T(8,128)(2,1)S(1)} %collective-permute-done.4.refs_0_), channel_id=1, source_target_pairs={{0,2},{1,9},{2,0},{3,11},{4,6},{5,13},{6,4},{7,15},{8,10},{9,1},{1... | collective-permute-start | bytes 393224 | tf_op jit(solution)/shard_map/ppermute | solution.py:295
  17.4 8.1 %collective-permute-start.2 = (bf16[64,1024]{1,0:T(8,128)(2,1)S(1)}, bf16[64,1024]{1,0:T(8,128)(2,1)S(1)}, u32[]{:S(2)}, u32[]{:S(2)}) collective-permute-start(bf16[64,1024]{1,0:T(8,128)(2,1)S(1)} %get-tuple-element.9.refs_0_), channel_id=1, source_target_pairs={{0,2},{1,9},{2,0},{3,11},{4,6},{5,13},{6,4},{7,15},{8,10},{9,1},{1... | collective-permute-start | bytes 393224 | tf_op jit(solution)/shard_map/ppermute | solution.py:295
  18.2 7.9 %collective-permute-start.9 = (bf16[64,1024]{1,0:T(8,128)(2,1)S(1)}, bf16[64,1024]{1,0:T(8,128)(2,1)S(1)}, u32[]{:S(2)}, u32[]{:S(2)}) collective-permute-start(bf16[64,1024]{1,0:T(8,128)(2,1)S(1)} %collective-permute-done.8.refs_0_), channel_id=1, source_target_pairs={{0,4},{1,17},{2,6},{3,19},{4,0},{5,21},{6,2},{7,23},{8,12},{9,25},... | collective-permute-start | bytes 393224 | tf_op jit(solution)/shard_map/ppermute | solution.py:295
  21.0 7.3 %collective-permute-start.5 = (bf16[64,1024]{1,0:T(8,128)(2,1)S(1)}, bf16[64,1024]{1,0:T(8,128)(2,1)S(1)}, u32[]{:S(2)}, u32[]{:S(2)}) collective-permute-start(bf16[64,1024]{1,0:T(8,128)(2,1)S(1)} %collective-permute-done.4.refs_0_), channel_id=1, source_target_pairs={{0,4},{1,17},{2,6},{3,19},{4,0},{5,21},{6,2},{7,23},{8,12},{9,25},... | collective-permute-start | bytes 393224 | tf_op jit(solution)/shard_map/ppermute | solution.py:295
  21.7 8.9 %collective-permute-start.3 = (bf16[64,1024]{1,0:T(8,128)(2,1)S(1)}, bf16[64,1024]{1,0:T(8,128)(2,1)S(1)}, u32[]{:S(2)}, u32[]{:S(2)}) collective-permute-start(bf16[64,1024]{1,0:T(8,128)(2,1)S(1)} %collective-permute-done.1.refs_1_), channel_id=1, source_target_pairs={{0,2},{1,9},{2,0},{3,11},{4,6},{5,13},{6,4},{7,15},{8,10},{9,1},{1... | collective-permute-start | bytes 393224 | tf_op jit(solution)/shard_map/ppermute | solution.py:295
  22.9 8.4 %collective-permute-start.13 = (bf16[64,1024]{1,0:T(8,128)(2,1)S(1)}, bf16[64,1024]{1,0:T(8,128)(2,1)S(1)}, u32[]{:S(2)}, u32[]{:S(2)}) collective-permute-start(bf16[64,1024]{1,0:T(8,128)(2,1)S(1)} %hold.3.refs_0_), channel_id=1, source_target_pairs={{0,4},{1,17},{2,6},{3,19},{4,0},{5,21},{6,2},{7,23},{8,12},{9,25},... | collective-permute-start | bytes 393224 | tf_op jit(solution)/shard_map/ppermute | solution.py:295
  25.5 7.3 %collective-permute-start.10 = (bf16[64,1024]{1,0:T(8,128)(2,1)S(1)}, bf16[64,1024]{1,0:T(8,128)(2,1)S(1)}, u32[]{:S(2)}, u32[]{:S(2)}) collective-permute-start(bf16[64,1024]{1,0:T(8,128)(2,1)S(1)} %collective-permute-done.8.refs_0_), channel_id=1, source_target_pairs={{0,2},{1,9},{2,0},{3,11},{4,6},{5,13},{6,4},{7,15},{8,10},{9,1},{1... | collective-permute-start | bytes 393224 | tf_op jit(solution)/shard_map/ppermute | solution.py:295
  26.1 6.7 %collective-permute-start.11 = (bf16[64,1024]{1,0:T(8,128)(2,1)S(1)}, bf16[64,1024]{1,0:T(8,128)(2,1)S(1)}, u32[]{:S(2)}, u32[]{:S(2)}) collective-permute-start(bf16[64,1024]{1,0:T(8,128)(2,1)S(1)} %collective-permute-done.9.refs_1_), channel_id=1, source_target_pairs={{0,2},{1,9},{2,0},{3,11},{4,6},{5,13},{6,4},{7,15},{8,10},{9,1},{1... | collective-permute-start | bytes 393224 | tf_op jit(solution)/shard_map/ppermute | solution.py:295
  28.4 5.6 %collective-permute-start.7 = (bf16[64,1024]{1,0:T(8,128)(2,1)S(1)}, bf16[64,1024]{1,0:T(8,128)(2,1)S(1)}, u32[]{:S(2)}, u32[]{:S(2)}) collective-permute-start(bf16[64,1024]{1,0:T(8,128)(2,1)S(1)} %collective-permute-done.5.refs_1_), channel_id=1, source_target_pairs={{0,2},{1,9},{2,0},{3,11},{4,6},{5,13},{6,4},{7,15},{8,10},{9,1},{1... | collective-permute-start | bytes 393224 | tf_op jit(solution)/shard_map/ppermute | solution.py:295
  30.7 5.0 %collective-permute-start.14 = (bf16[64,1024]{1,0:T(8,128)(2,1)S(1)}, bf16[64,1024]{1,0:T(8,128)(2,1)S(1)}, u32[]{:S(2)}, u32[]{:S(2)}) collective-permute-start(bf16[64,1024]{1,0:T(8,128)(2,1)S(1)} %hold.3.refs_0_), channel_id=1, source_target_pairs={{0,2},{1,9},{2,0},{3,11},{4,6},{5,13},{6,4},{7,15},{8,10},{9,1},{1... | collective-permute-start | bytes 393224 | tf_op jit(solution)/shard_map/ppermute | solution.py:295
  31.3 5.7 %collective-permute-start.15 = (bf16[64,1024]{1,0:T(8,128)(2,1)S(1)}, bf16[64,1024]{1,0:T(8,128)(2,1)S(1)}, u32[]{:S(2)}, u32[]{:S(2)}) collective-permute-start(bf16[64,1024]{1,0:T(8,128)(2,1)S(1)} %collective-permute-done.13.refs_1_), channel_id=1, source_target_pairs={{0,2},{1,9},{2,0},{3,11},{4,6},{5,13},{6,4},{7,15},{8,10},{9,1},{1... | collective-permute-start | bytes 393224 | tf_op jit(solution)/shard_map/ppermute | solution.py:295
  32.7 4.4 %collective-permute-start.16 = (bf16[256,1024]{1,0:T(8,128)(2,1)S(1)}, bf16[256,1024]{1,0:T(8,128)(2,1)S(1)}, u32[]{:S(2)}, u32[]{:S(2)}) collective-permute-start(bf16[256,1024]{1,0:T(8,128)(2,1)S(1)} %pack.4.refs_0_), channel_id=1, source_target_pairs={{0,1},{1,0},{2,3},{3,2},{4,5},{5,4},{6,7},{7,6},{8,9},{9,8},{10,11... | collective-permute-start | bytes 1572872 | tf_op jit(solution)/shard_map/ppermute | solution.py:295
  32.9 4.3 %collective-permute-start.18 = (bf16[256,1024]{1,0:T(8,128)(2,1)S(1)}, bf16[256,1024]{1,0:T(8,128)(2,1)S(1)}, u32[]{:S(2)}, u32[]{:S(2)}) collective-permute-start(bf16[256,1024]{1,0:T(8,128)(2,1)S(1)} %pack.6.refs_2_), channel_id=1, source_target_pairs={{0,1},{1,0},{2,3},{3,2},{4,5},{5,4},{6,7},{7,6},{8,9},{9,8},{10,11... | collective-permute-start | bytes 1572872 | tf_op jit(solution)/shard_map/ppermute | solution.py:295
  34.0 3.1 %collective-permute-start.17 = (bf16[256,1024]{1,0:T(8,128)(2,1)S(1)}, bf16[256,1024]{1,0:T(8,128)(2,1)S(1)}, u32[]{:S(2)}, u32[]{:S(2)}) collective-permute-start(bf16[256,1024]{1,0:T(8,128)(2,1)S(1)} %pack.5.refs_1_), channel_id=1, source_target_pairs={{0,1},{1,0},{2,3},{3,2},{4,5},{5,4},{6,7},{7,6},{8,9},{9,8},{10,11... | collective-permute-start | bytes 1572872 | tf_op jit(solution)/shard_map/ppermute | solution.py:295
  37.1 2.0 %collective-permute-start.19 = (bf16[256,1024]{1,0:T(8,128)(2,1)S(1)}, bf16[256,1024]{1,0:T(8,128)(2,1)S(1)}, u32[]{:S(2)}, u32[]{:S(2)}) collective-permute-start(bf16[256,1024]{1,0:T(8,128)(2,1)S(1)} %pack.7.refs_3_), channel_id=1, source_target_pairs={{0,1},{1,0},{2,3},{3,2},{4,5},{5,4},{6,7},{7,6},{8,9},{9,8},{10,11... | collective-permute-start | bytes 1572872 | tf_op jit(solution)/shard_map/ppermute | solution.py:295
